TPU v7x, 32 devices: a whole 2x2x4 slice. The times are simulated.
32 devices in a mesh: fsdp: 8 (over z, y), tp: 4 (over x, core).
Axes of the slice: x: 2, y: 2, z: 4, core: 2. Of those that a mesh axis runs over, the one named last changes fastest.
Arguments:
- base_weight: bfloat16 [16384, 26624], P(('fsdp', 'tp')), may hold values from -0.09375 to 0.09375
- left_factor: bfloat16 [16384, 64], P(('fsdp', 'tp')), may hold values from -0.75 to 0.75
- right_factor: bfloat16 [64, 26624], P(None, 'tp'), may hold values from -0.029907227 to 0.029907227
- magnitude: float32 [26624], replicated, may hold values from 6 to 96
Outputs:
- quantized: bfloat16 [16384, 26624], P('fsdp', 'tp')
- block_scales: float32 [128, 208], P('fsdp', 'tp')
All inputs are finite; a program needn't handle non-finite values. Where the computation divides by a largest or mean magnitude, that divisor is 1e-20 or more.
Results may differ from a plain program's by a relative error of at most 0.01.
Values may be sent and summed in bfloat16 or wider, within the bound.
No kernel may reach another device: no remote copies, remote signals or barrier semaphores. Data moves between devices by JAX's collectives and lax.ppermute only.
A program may use at most 320 MiB of HBM per device.

v0:
```python
import functools

import jax
import jax.numpy as jnp
from jax import lax
from jax.experimental import pallas as pl
from jax.experimental.pallas import tpu as pltpu
from jax.sharding import PartitionSpec as P

BLOCK = 128
EPSILON = 1e-06
EARLY = (8, 8, 8, 8, 8, 8)
LATE = (4,)
AHEAD = 2
SCALE = 3
CARRIER = 3
TERMS = 3
SUMS_ROWS = 16
PARAMS = pltpu.CompilerParams(vmem_limit_bytes=52 * 2**20)
MOVE_PARAMS = pltpu.CompilerParams(vmem_limit_bytes=56 * 2**20)


def chunk_blocks(total):
    parts = EARLY + LATE
    bounds = [total * sum(parts[:i]) // sum(parts) for i in range(len(parts) + 1)]
    chunks = [(a, b) for a, b in zip(bounds, bounds[1:]) if b > a]
    return chunks, sum(a < bounds[len(EARLY)] for a, _ in chunks)


def width_of(*counts):
    return max(d for d in (4, 2, 1) if all(count % d == 0 for count in counts))


def after(value, *others):
    return lax.optimization_barrier((value, *others))[0]


def swap(array, d, size, axis="tp"):
    return lax.ppermute(array, axis, [(i, i ^ d) for i in range(size)])


def total_of(array, size, axis):
    d = 1
    while d < size:
        array = array + swap(array, d, size, axis)
        d *= 2
    return array


def move_kernel(moves, number, me_ref, *refs):
    plan = moves(me_ref[0])
    sources, targets = refs[:number], refs[number : -len(plan) - 2]
    holds, came, went = refs[-len(plan) - 2 : -2], refs[-2], refs[-1]
    ins, outs = [], []
    for i, (source, row, col, rows, cols, target, to_row, to_col) in enumerate(plan):
        block = sources[source].at[pl.ds(row, rows), pl.ds(col, cols)]
        place = targets[target].at[pl.ds(to_row, rows), pl.ds(to_col, cols)]
        ins.append(pltpu.make_async_copy(block, holds[i], came.at[i]))
        outs.append(pltpu.make_async_copy(holds[i], place, went.at[i]))
    for copy in ins:
        copy.start()
    for copy, onward in zip(ins, outs):
        copy.wait()
        onward.start()
    for copy in outs:
        copy.wait()


def move(me, arrays, shapes, moves):
    dtype = arrays[0].dtype
    plan = moves(0)
    return pl.pallas_call(
        functools.partial(move_kernel, moves, len(arrays)),
        out_shape=[jax.ShapeDtypeStruct(shape, dtype) for shape in shapes],
        grid_spec=pltpu.PrefetchScalarGridSpec(
            num_scalar_prefetch=1,
            grid=(1,),
            in_specs=[pl.BlockSpec(memory_space=pl.ANY)] * len(arrays),
            out_specs=[pl.BlockSpec(memory_space=pl.ANY)] * len(shapes),
            scratch_shapes=[pltpu.VMEM((rows, cols), dtype) for _, _, _, rows, cols, *_ in plan]
            + [pltpu.SemaphoreType.DMA((len(plan),))] * 2,
        ),
        compiler_params=MOVE_PARAMS,
        cost_estimate=cost(sum(rows * cols for rows, cols in shapes), 1, 0, 2),
    )(me, *arrays)


def parts_of(rows):
    height = rows // 4 if rows % (4 * BLOCK) == 0 else rows
    return [(r, height) for r in range(0, rows, height)]


def column_moves(me, rows, cols, group, first, target):
    col = pl.multiple_of(me * group + first, BLOCK)
    return [(0, r, col, height, cols, target, r, 0) for r, height in parts_of(rows)]


def group_spec(rows, unit, groups, first, d=0):
    return pl.BlockSpec((rows, unit), lambda j, me: (0, (me[0] ^ d) * groups + first + j))


def chunk_spec(rows, unit, first=0):
    return pl.BlockSpec((rows, unit), lambda j, me: (0, first + j))


def left_spec(rank, unit):
    return pl.BlockSpec((rank, unit), lambda j, me: (0, 0))


def whole_spec(array):
    return pl.BlockSpec(array.shape, lambda j, me: (0, 0))


def cost(rows, cols, rank, passes):
    return pl.CostEstimate(
        flops=2 * rows * cols * rank // SCALE, bytes_accessed=2 * passes * rows * cols // SCALE, transcendentals=0
    )


def pack(me, base, tp, distances, first, cols):
    rows, group = base.shape[0], base.shape[1] // tp

    def moves(me):
        return [m for i, d in enumerate(distances) for m in column_moves(me ^ d, rows, cols, group, first, i)]

    return move(me, [base], [(rows, cols)] * len(distances), moves)


def pack_first(me, base, tp, d, left, right, late, cols):
    rows, group = base.shape[0], base.shape[1] // tp
    rank, lane = left.shape
    late_cols = late[1] - late[0]

    def moves(me):
        extras = [
            (1, 0, 0, rank, lane, 0, rows, 0),
            (1, 0, 0, rank, lane, 1, 0, 0),
            (2, 0, late[0], rank, late_cols, 0, rows, lane),
            (2, 0, late[0], rank, late_cols, 1, 0, lane),
        ]
        return column_moves(me ^ d, rows, cols, group, 0, 0) + extras

    return move(me, [base, left, right], [(rows + rank, cols), (rank, lane + late_cols)], moves)


def pack_carrier(me, base, tp, distances, terms, first, cols):
    rows, group = base.shape[0], base.shape[1] // tp

    def moves(me):
        result = []
        for i, d in enumerate(distances):
            result += column_moves(me ^ d, rows, cols, group, first, i)
            result.append((1, d * SUMS_ROWS, 0, SUMS_ROWS, terms.shape[1], i, rows, 0))
        return result

    return move(me, [base, terms], [(rows + SUMS_ROWS, cols)] * len(distances), moves)


def pack_near(me, base, tp):
    rows, group = base.shape[0], base.shape[1] // tp

    def moves(me):
        result = []
        for s in range(2):
            for source, r, col, *rest in column_moves((me // 2) * 2 + s, rows, group, group, 0, 0):
                result.append((source, r, col, *rest[:-2], s * rows + r, 0))
        return result

    return move(me, [base], [(2 * rows, group)], moves)[0]


def near_spec(rows, unit, first):
    return pl.BlockSpec((rows, unit), lambda j, me: ((me[0] % 2) ^ 1, first + j))


def low_rank(extra_ref, start, height, right):
    left = extra_ref[pl.ds(0, right.shape[0]), pl.ds(start, height)]
    return lax.dot_general(left, right, (((0,), (0,)), ((), ())), preferred_element_type=jnp.float32)


def squares_of(piece_ref, extra_ref, right):
    rows, cols = piece_ref.shape
    height = min(rows, BLOCK)
    total = jnp.zeros((8, cols), jnp.float32)
    for r in range(0, rows, height):
        combined = piece_ref[pl.ds(r, height), :].astype(jnp.float32) + low_rank(extra_ref, r, height, right)
        total = total + jnp.sum((combined * combined).reshape(height // 8, 8, cols), axis=0)
    return total


def squares_kernel(tp, me_ref, *refs):
    pieces, extras, right_ref, out_ref = refs[:tp], refs[tp : 2 * tp], refs[-2], refs[-1]
    right = right_ref[...]
    total = sum(squares_of(piece, extra, right) for piece, extra in zip(pieces, extras))
    out_ref[...] = jnp.sum(total, axis=0, keepdims=True)


def sender_squares_kernel(tp, me_ref, *refs):
    pieces, rights, left, sums_ref, terms_ref = refs[:tp], refs[tp : 2 * tp], refs[-3], refs[-2], refs[-1]
    line = lax.broadcasted_iota(jnp.int32, (SUMS_ROWS, sums_ref.shape[1]), 0)
    for d in range(tp):
        sums = jnp.sum(squares_of(pieces[d], left, rights[d][...]), axis=0, keepdims=True)
        sums_ref[pl.ds(d, 1), :] = sums
        block = jnp.zeros(line.shape, jnp.float32)
        for term in range(TERMS):
            part = sums.astype(jnp.bfloat16).astype(jnp.float32)
            block = jnp.where(line == term, part, block)
            sums = sums - part
        terms_ref[pl.ds(d * SUMS_ROWS, SUMS_ROWS), :] = block.astype(jnp.bfloat16)


def column_squares(me, base, near, received, extras, right, unit, first, count):
    rows = base.shape[0]
    rank, cols = right.shape
    tp = len(extras)
    return pl.pallas_call(
        functools.partial(squares_kernel, tp),
        out_shape=jax.ShapeDtypeStruct((1, count * unit), jnp.float32),
        grid_spec=pltpu.PrefetchScalarGridSpec(
            num_scalar_prefetch=1,
            grid=(count,),
            in_specs=[group_spec(rows, unit, cols // unit, first), near_spec(rows, unit, first)]
            + [chunk_spec(rows, unit)] * (tp - 2)
            + [left_spec(rank, max(rows, BLOCK))] * tp
            + [chunk_spec(rank, unit, first)],
            out_specs=chunk_spec(1, unit),
        ),
        compiler_params=PARAMS,
        cost_estimate=cost(tp * rows, count * unit, rank, 1),
    )(me, base, near, *received, *extras, right)


def sender_squares(me, base, extras, rank, unit, first, count, lane):
    rows = base.shape[0]
    tp = len(extras)
    groups = base.shape[1] // (tp * unit)
    return pl.pallas_call(
        functools.partial(sender_squares_kernel, tp),
        out_shape=[
            jax.ShapeDtypeStruct((tp, count * unit), jnp.float32),
            jax.ShapeDtypeStruct((tp * SUMS_ROWS, count * unit), jnp.bfloat16),
        ],
        grid_spec=pltpu.PrefetchScalarGridSpec(
            num_scalar_prefetch=1,
            grid=(count,),
            in_specs=[group_spec(rows, unit, groups, first, d) for d in range(tp)]
            + [chunk_spec(rank, unit, lane // unit)] * tp
            + [left_spec(rank, lane)],
            out_specs=[chunk_spec(tp, unit), chunk_spec(tp * SUMS_ROWS, unit)],
        ),
        compiler_params=PARAMS,
        cost_estimate=cost(tp * rows, count * unit, rank, 1),
    )(me, *[base] * tp, *extras, extras[0])


def export_kernel(tp, first, me_ref, *refs):
    pieces, extras = refs[:tp], refs[tp : 2 * tp]
    right_ref, squares_ref, mag_ref = refs[2 * tp : 2 * tp + 3]
    out_ref, scales_ref = refs[-2:]
    rows, cols = pieces[0].shape
    step = pl.program_id(0)
    if len(refs) > 2 * tp + 5:
        @pl.when(step == 0)
        def _():
            scales_ref[...] = refs[2 * tp + 4][...]

    factor = mag_ref[...] / jnp.sqrt(squares_ref[...] + EPSILON)
    right = right_ref[...]
    height = min(rows, BLOCK)
    for d in range(tp):
        start = (me_ref[0] ^ d) * rows
        for r in range(0, rows, height):
            combined = pieces[d][pl.ds(r, height), :].astype(jnp.float32) + low_rank(extras[d], r, height, right)
            span = pl.ds(pl.multiple_of(start + r, height), height)
            out_ref[span, :] = (combined * factor).astype(jnp.bfloat16)

    lane = lax.broadcasted_iota(jnp.int32, (1, scales_ref.shape[1]), 1)
    per_step = cols // BLOCK
    for i in range(tp * rows // BLOCK):
        span = pl.ds(i * BLOCK, BLOCK)
        line = scales_ref[pl.ds(i, 1), :]
        for j in range(per_step):
            tile = out_ref[span, pl.ds(j * BLOCK, BLOCK)].astype(jnp.float32)
            largest = jnp.max(jnp.max(jnp.abs(tile), axis=0, keepdims=True), axis=1, keepdims=True)
            out_ref[span, pl.ds(j * BLOCK, BLOCK)] = (tile * (1.0 / (largest + EPSILON))).astype(jnp.bfloat16)
            line = jnp.where(lane == (first + step) * per_step + j, largest, line)
        scales_ref[pl.ds(i, 1), :] = line


def export_chunk(me, base, near, received, extras, right, squares, mag, unit, first, count, previous):
    rows = base.shape[0]
    rank, cols = right.shape
    tp = len(extras)
    groups = cols // unit
    result = (
        jax.ShapeDtypeStruct((tp * rows, cols), jnp.bfloat16),
        jax.ShapeDtypeStruct((tp * rows // BLOCK, cols // BLOCK), jnp.float32),
    )
    in_specs = (
        [group_spec(rows, unit, groups, first), near_spec(rows, unit, first)]
        + [chunk_spec(rows, unit)] * (tp - 2)
        + [left_spec(rank, max(rows, BLOCK))] * tp
        + [chunk_spec(rank, unit, first), chunk_spec(1, unit), group_spec(1, unit, groups, first)]
    )
    args = [base, near, *received, *extras, right, squares, mag]
    aliases = {}
    if previous is not None:
        in_specs += [pl.BlockSpec(memory_space=pl.ANY), whole_spec(previous[1])]
        args += list(previous)
        aliases = {len(args) - 1: 0}
    return pl.pallas_call(
        functools.partial(export_kernel, tp, first),
        out_shape=result,
        grid_spec=pltpu.PrefetchScalarGridSpec(
            num_scalar_prefetch=1,
            grid=(count,),
            in_specs=in_specs,
            out_specs=(chunk_spec(tp * rows, unit, first), whole_spec(result[1])),
        ),
        input_output_aliases=aliases,
        compiler_params=PARAMS,
        cost_estimate=cost(tp * rows, count * unit, rank, 2),
    )(me, *args)


def body(tp, fsdp, base, left, right, magnitude):
    rows, rank = left.shape
    cols = right.shape[1]
    blocks = cols // BLOCK
    chunks, early = chunk_blocks(blocks)
    mag = magnitude.reshape(1, -1)
    me = lax.axis_index("tp").astype(jnp.int32).reshape(1)
    lane = -(-rows // BLOCK) * BLOCK
    left = jnp.pad(left.T, ((0, 0), (0, lane - rows)))
    late = (chunks[early][0], chunks[-1][1])
    far = range(2, tp)
    received = {}

    def span(k):
        a, b = chunks[k]
        return a * BLOCK, (b - a) * BLOCK

    def units(k):
        a, b = chunks[k]
        width = width_of(a, b, blocks)
        return width * BLOCK, a // width, (b - a) // width

    def send(k, pieces):
        received[k] = [swap(piece, d, tp) for d, piece in zip(far, pieces)]

    pieces = []
    for d in far:
        if d % 2 == 0:
            piece, own = pack_first(me, base, tp, d, left, right, (late[0] * BLOCK, late[1] * BLOCK), span(0)[1])
        else:
            piece = pack(after(me, own), base, tp, (d,), *span(0))[0]
        pieces.append(piece)
    send(0, pieces)
    pieces = pack(after(me, *pieces), base, tp, far, *span(1))
    send(1, pieces)
    near = lax.all_to_all(
        pack_near(after(me, *pieces), base, tp), "tp", 0, 0, tiled=True,
        axis_index_groups=[[i, i + 1] for i in range(0, tp, 2)],
    )

    even = [own] + [received[0][d - 2][rows:, : own.shape[1]] for d in far[::2]]
    odd = swap(jnp.concatenate(even), 1, tp)
    extras = []
    for i in range(tp // 2):
        extras += [even[i], odd[i * rank : (i + 1) * rank]]

    result = None
    token = ()
    totals = {}
    for k in range(len(chunks)):
        following = k + AHEAD
        if following < len(chunks):
            turn = after(me, *received[k], *token)
            if following == CARRIER:
                width = width_of(late[0], late[1] - late[0], blocks, lane // BLOCK)
                sums, terms = sender_squares(
                    turn, base, extras, rank, width * BLOCK, late[0] // width, (late[1] - late[0]) // width, lane
                )
                late_sums = sums[:1] + swap(sums[1:2], 1, tp)
                send(following, pack_carrier(turn, base, tp, far, terms, *span(following)))
            else:
                send(following, pack(turn, base, tp, far, *span(following)))
        if k < early:
            local = column_squares(after(me, *token), base, near, received[k], extras, right, *units(k))
            if k == CARRIER:
                for piece in received[k]:
                    parts = after(piece, *token)[rows : rows + TERMS, : late_sums.shape[1]].astype(jnp.float32)
                    late_sums = late_sums + jnp.sum(parts, axis=0, keepdims=True)
                local = jnp.concatenate([local, late_sums], axis=1)
            total = lax.psum(local, "fsdp") if k < early - 1 else total_of(local, fsdp, "fsdp")
            totals[k] = total[:, : span(k)[1]]
            if k == CARRIER:
                for i in range(early, len(chunks)):
                    start = span(k)[1] + span(i)[0] - late[0] * BLOCK
                    totals[i] = total[:, start : start + span(i)[1]]
        result = export_chunk(me, base, near, received[k], extras, right, totals[k], mag, *units(k), result)
        token = (result[1],)
    return result


def solution(mesh):
    in_specs = (P(("fsdp", "tp"), None), P(("fsdp", "tp"), None), P(None, "tp"), P())
    out_specs = (P("fsdp", "tp"), P("fsdp", "tp"))
    return jax.shard_map(
        functools.partial(body, mesh.shape["tp"], mesh.shape["fsdp"]), mesh=mesh, in_specs=in_specs, out_specs=out_specs, check_vma=False
    )
```

profile of v0, /device:TPU:0, one launch (start us, length us, event | category | flops | bytes accessed | tf_op | source)
XLA Modules:
  0.0 306.3 jit_solution(13736192161123310986)
XLA Ops:
  2.8 3.0 collective-permute-start
  7.9 2.4 shard_map.61
  12.2 20.6 %collective-permute-done.refs_2_ = bf16[576,1024]{1,0:T(8,128)(2,1)S(1)} collective-permute-done((bf16[576,1024]{1,0:T(8,128)(2,1)}, bf16[576,1024]{1,0:T(8,128)(2,1)S(1)}, u32[]{:S(2)}, u32[]{:S(2)}) %collective-permute-start) | collective-permute-done | bytes 1179680 | tf_op jit(solution)/shard_map/ppermute | solution.py:39
  32.9 22.0 %collective-permute-done.1.refs_3_ = bf16[512,1024]{1,0:T(8,128)(2,1)S(1)} collective-permute-done((bf16[512,1024]{1,0:T(8,128)(2,1)}, bf16[512,1024]{1,0:T(8,128)(2,1)S(1)}, u32[]{:S(2)}, u32[]{:S(2)}) %collective-permute-start.1) | collective-permute-done | bytes 1048608 | tf_op jit(solution)/shard_map/ppermute | solution.py:39
  54.9 2.8 shard_map.63
  59.7 10.2 %shard_map.62 = bf16[1024,6656]{1,0:T(8,128)(2,1)} custom-call(s32[1]{0:T(128)} %bitcast.me_ref, bf16[512,26624]{1,0:T(8,128)(2,1)} %refs_0_.45), custom_call_target="tpu_custom_call" | custom-call | bytes 9087658 | tf_op jit(solution)/shard_map/pallas_call | solution.py:72
  69.9 8.9 %all-to-all-start = ((bf16[2,512,6656]{2,1,0:T(8,128)(2,1)}), bf16[2,512,6656]{2,1,0:T(8,128)(2,1)}, u32[]{:S(2)}, u32[]{:S(2)}) async-start(bf16[2,512,6656]{2,1,0:T(8,128)(2,1)} %bitcast.14), calls=%async_computation | async-start | bytes 27262976 | tf_op jit(solution)/shard_map/all_to_all | solution.py:361
  78.8 11.2 %all-to-all-done = bf16[2,512,6656]{2,1,0:T(8,128)(2,1)} async-done(((bf16[2,512,6656]{2,1,0:T(8,128)(2,1)}), bf16[2,512,6656]{2,1,0:T(8,128)(2,1)}, u32[]{:S(2)}, u32[]{:S(2)}) %all-to-all-start) | async-done | bytes 13631520 | tf_op jit(solution)/shard_map/all_to_all | solution.py:361
  90.0 3.2 %shard_map.64 = f32[1,1024]{1,0:T(1,128)S(1)} custom-call(s32[1]{0:T(128)} %bitcast.me_ref, bf16[512,26624]{1,0:T(8,128)(2,1)} %refs_0_.45, bf16[1024,6656]{1,0:T(8,128)(2,1)} %bitcast.3.refs_1_, bf16[576,1024]{1,0:T(8,128)(2,1)} %copy-done.4, bf16[512,1024]{1,0:T(8,128)(2,1)} %copy-done.6, bf16[64,1024]{1,0:T(8,128)(2,1)S(1)} %copy-done.1, ...), custom_call_target="tpu_custom_call" | custom-call | flops 89478488 | bytes 1398101 | tf_op jit(solution)/shard_map/pallas_call | solution.py:216
  93.2 21.9 %psum.35.refs_9_ = f32[1,1024]{1,0:T(1,128)S(1)} all-reduce(f32[1,1024]{1,0:T(1,128)S(1)} %shard_map.64), channel_id=1, replica_groups=mesh['fsdp'=8,'tp'=4] {'fsdp'}, use_global_device_ids=true, to_apply=%region_0.1 | all-reduce | flops 1024 | bytes 8192 | tf_op jit(solution)/shard_map/psum | solution.py:395
  115.0 5.8 %shard_map.65 = (bf16[2048,6656]{1,0:T(8,128)(2,1)}, f32[16,52]{1,0:T(8,128)S(1)}) custom-call(s32[1]{0:T(128)} %bitcast.me_ref, bf16[512,26624]{1,0:T(8,128)(2,1)} %refs_0_.45, bf16[1024,6656]{1,0:T(8,128)(2,1)} %bitcast.3.refs_1_, bf16[576,1024]{1,0:T(8,128)(2,1)} %copy-done.4, bf16[512,1024]{1,0:T(8,128)(2,1)} %copy-done.6, ...), custom_call_target="tpu_custom_call" | custom-call | flops 89478488 | bytes 2796202 | tf_op jit(solution)/shard_map/pallas_call | solution.py:311
  123.8 2.5 shard_map.70
  127.9 3.1 %shard_map.66 = f32[1,1024]{1,0:T(1,128)S(1)} custom-call(s32[1]{0:T(128)} %bitcast.me_ref, bf16[512,26624]{1,0:T(8,128)(2,1)} %refs_0_.45, bf16[1024,6656]{1,0:T(8,128)(2,1)} %bitcast.3.refs_1_, bf16[512,1024]{1,0:T(8,128)(2,1)} %collective-permute-done.4.refs_2_, bf16[512,1024]{1,0:T(8,128)(2,1)} %collective-permute-done.5.refs_3_, ...), custom_call_target="tpu_custom_call" | custom-call | flops 89478488 | bytes 1398101 | tf_op jit(solution)/shard_map/pallas_call | solution.py:216
  131.0 17.1 %psum.36.refs_9_ = f32[1,1024]{1,0:T(1,128)S(1)} all-reduce(f32[1,1024]{1,0:T(1,128)S(1)} %shard_map.66), channel_id=1, replica_groups=mesh['fsdp'=8,'tp'=4] {'fsdp'}, use_global_device_ids=true, to_apply=%region_1.2 | all-reduce | flops 1024 | bytes 8192 | tf_op jit(solution)/shard_map/psum | solution.py:395
  148.2 5.9 %shard_map.67 = (bf16[2048,6656]{1,0:T(8,128)(2,1)}, f32[16,52]{1,0:T(8,128)S(1)}) custom-call(s32[1]{0:T(128)} %bitcast.me_ref, bf16[512,26624]{1,0:T(8,128)(2,1)} %refs_0_.45, bf16[1024,6656]{1,0:T(8,128)(2,1)} %bitcast.3.refs_1_, bf16[512,1024]{1,0:T(8,128)(2,1)} %collective-permute-done.4.refs_2_, ...), custom_call_target="tpu_custom_call", output_to_operand_aliasing={{0}: (12, {})} | custom-call | flops 89478488 | bytes 2796202 | tf_op jit(solution)/shard_map/pallas_call | solution.py:311
  158.7 3.1 %shard_map.71 = f32[1,1024]{1,0:T(1,128)S(1)} custom-call(s32[1]{0:T(128)} %bitcast.me_ref, bf16[512,26624]{1,0:T(8,128)(2,1)} %refs_0_.45, bf16[1024,6656]{1,0:T(8,128)(2,1)} %bitcast.3.refs_1_, bf16[512,1024]{1,0:T(8,128)(2,1)} %collective-permute-done.2.refs_2_, bf16[512,1024]{1,0:T(8,128)(2,1)} %collective-permute-done.3.refs_3_, ...), custom_call_target="tpu_custom_call" | custom-call | flops 89478488 | bytes 1398101 | tf_op jit(solution)/shard_map/pallas_call | solution.py:216
  161.8 19.1 %psum.37.refs_9_ = f32[1,1024]{1,0:T(1,128)S(1)} all-reduce(f32[1,1024]{1,0:T(1,128)S(1)} %shard_map.71), channel_id=1, replica_groups=mesh['fsdp'=8,'tp'=4] {'fsdp'}, use_global_device_ids=true, to_apply=%region_2.3 | all-reduce | flops 1024 | bytes 8192 | tf_op jit(solution)/shard_map/psum | solution.py:395
  180.9 5.9 %shard_map.72 = (bf16[2048,6656]{1,0:T(8,128)(2,1)}, f32[16,52]{1,0:T(8,128)S(1)}) custom-call(s32[1]{0:T(128)} %bitcast.me_ref, bf16[512,26624]{1,0:T(8,128)(2,1)} %refs_0_.45, bf16[1024,6656]{1,0:T(8,128)(2,1)} %bitcast.3.refs_1_, bf16[512,1024]{1,0:T(8,128)(2,1)} %collective-permute-done.2.refs_2_, ...), custom_call_target="tpu_custom_call", output_to_operand_aliasing={{0}: (12, {})} | custom-call | flops 89478488 | bytes 2796202 | tf_op jit(solution)/shard_map/pallas_call | solution.py:311
  186.8 4.4 %collective-permute-done.10.refs_3_ = bf16[528,1024]{1,0:T(8,128)(2,1)} collective-permute-done((bf16[528,1024]{1,0:T(8,128)(2,1)}, bf16[528,1024]{1,0:T(8,128)(2,1)}, u32[]{:S(2)}, u32[]{:S(2)}) %collective-permute-start.10) | collective-permute-done | bytes 1081376 | tf_op jit(solution)/shard_map/ppermute | solution.py:39
  191.2 2.4 shard_map.76
  196.4 3.2 %shard_map.73 = f32[1,1024]{1,0:T(1,128)S(1)} custom-call(s32[1]{0:T(128)} %bitcast.me_ref, bf16[512,26624]{1,0:T(8,128)(2,1)} %refs_0_.45, bf16[1024,6656]{1,0:T(8,128)(2,1)} %bitcast.3.refs_1_, bf16[528,1024]{1,0:T(8,128)(2,1)} %copy-done.5, bf16[528,1024]{1,0:T(8,128)(2,1)} %collective-permute-done.10.refs_3_, bf16[64,1024]{1,0:T(8,128)(2,1)S(1)} %copy-done.1, ...), custom_call_target="tpu_custom_call" | custom-call | flops 89478488 | bytes 1398101 | tf_op jit(solution)/shard_map/pallas_call | solution.py:216
  199.6 22.2 %psum.38 = f32[1,1536]{1,0:T(1,128)S(1)} all-reduce(f32[1,1536]{1,0:T(1,128)S(1)} %pad_maximum_fusion.1), channel_id=1, replica_groups=mesh['fsdp'=8,'tp'=4] {'fsdp'}, use_global_device_ids=true, to_apply=%region_5.6 | all-reduce | flops 1536 | bytes 12288 | tf_op jit(solution)/shard_map/psum | solution.py:395
  221.9 5.9 %shard_map.74 = (bf16[2048,6656]{1,0:T(8,128)(2,1)}, f32[16,52]{1,0:T(8,128)S(1)}) custom-call(s32[1]{0:T(128)} %bitcast.me_ref, bf16[512,26624]{1,0:T(8,128)(2,1)} %refs_0_.45, bf16[1024,6656]{1,0:T(8,128)(2,1)} %bitcast.3.refs_1_, bf16[528,1024]{1,0:T(8,128)(2,1)} %copy-done.5, ...), custom_call_target="tpu_custom_call", output_to_operand_aliasing={{0}: (12, {})} | custom-call | flops 89478488 | bytes 2796202 | tf_op jit(solution)/shard_map/pallas_call | solution.py:311
  227.7 8.4 %collective-permute-done.8.refs_3_ = bf16[512,1024]{1,0:T(8,128)(2,1)} collective-permute-done((bf16[512,1024]{1,0:T(8,128)(2,1)}, bf16[512,1024]{1,0:T(8,128)(2,1)}, u32[]{:S(2)}, u32[]{:S(2)}) %collective-permute-start.8) | collective-permute-done | bytes 1048608 | tf_op jit(solution)/shard_map/ppermute | solution.py:39
  240.3 3.1 %shard_map.77 = f32[1,1024]{1,0:T(1,128)S(1)} custom-call(s32[1]{0:T(128)} %bitcast.me_ref, bf16[512,26624]{1,0:T(8,128)(2,1)} %refs_0_.45, bf16[1024,6656]{1,0:T(8,128)(2,1)} %bitcast.3.refs_1_, bf16[512,1024]{1,0:T(8,128)(2,1)} %collective-permute-done.7.refs_2_, bf16[512,1024]{1,0:T(8,128)(2,1)} %collective-permute-done.8.refs_3_, ...), custom_call_target="tpu_custom_call" | custom-call | flops 89478488 | bytes 1398101 | tf_op jit(solution)/shard_map/pallas_call | solution.py:216
  243.4 21.8 %psum.39.refs_9_ = f32[1,1024]{1,0:T(1,128)S(1)} all-reduce(f32[1,1024]{1,0:T(1,128)S(1)} %shard_map.77), channel_id=1, replica_groups=mesh['fsdp'=8,'tp'=4] {'fsdp'}, use_global_device_ids=true, to_apply=%region_6.7 | all-reduce | flops 1024 | bytes 8192 | tf_op jit(solution)/shard_map/psum | solution.py:395
  265.2 5.8 %shard_map.78 = (bf16[2048,6656]{1,0:T(8,128)(2,1)}, f32[16,52]{1,0:T(8,128)S(1)}) custom-call(s32[1]{0:T(128)} %bitcast.me_ref, bf16[512,26624]{1,0:T(8,128)(2,1)} %refs_0_.45, bf16[1024,6656]{1,0:T(8,128)(2,1)} %bitcast.3.refs_1_, bf16[512,1024]{1,0:T(8,128)(2,1)} %collective-permute-done.7.refs_2_, ...), custom_call_target="tpu_custom_call", output_to_operand_aliasing={{0}: (12, {})} | custom-call | flops 89478488 | bytes 2796202 | tf_op jit(solution)/shard_map/pallas_call | solution.py:311
  271.1 10.0 %collective-permute-done.15.refs_3_ = bf16[512,1024]{1,0:T(8,128)(2,1)} collective-permute-done((bf16[512,1024]{1,0:T(8,128)(2,1)}, bf16[512,1024]{1,0:T(8,128)(2,1)}, u32[]{:S(2)}, u32[]{:S(2)}) %collective-permute-start.15) | collective-permute-done | bytes 1048608 | tf_op jit(solution)/shard_map/ppermute | solution.py:39
  281.0 3.1 %shard_map.79 = f32[1,1024]{1,0:T(1,128)S(1)} custom-call(s32[1]{0:T(128)} %bitcast.me_ref, bf16[512,26624]{1,0:T(8,128)(2,1)} %refs_0_.45, bf16[1024,6656]{1,0:T(8,128)(2,1)} %bitcast.3.refs_1_, bf16[512,1024]{1,0:T(8,128)(2,1)} %collective-permute-done.14.refs_2_, bf16[512,1024]{1,0:T(8,128)(2,1)} %collective-permute-done.15.refs_3_, ...), custom_call_target="tpu_custom_call" | custom-call | flops 89478488 | bytes 1398101 | tf_op jit(solution)/shard_map/pallas_call | solution.py:216
  291.5 2.6 collective-permute-start.18
  296.0 5.9 %shard_map.80 = (bf16[2048,6656]{1,0:T(8,128)(2,1)}, f32[16,52]{1,0:T(8,128)S(1)}) custom-call(s32[1]{0:T(128)} %bitcast.me_ref, bf16[512,26624]{1,0:T(8,128)(2,1)} %refs_0_.45, bf16[1024,6656]{1,0:T(8,128)(2,1)} %bitcast.3.refs_1_, bf16[512,1024]{1,0:T(8,128)(2,1)} %collective-permute-done.14.refs_2_, ...), custom_call_target="tpu_custom_call", output_to_operand_aliasing={{0}: (12, {})} | custom-call | flops 89478488 | bytes 2796202 | tf_op jit(solution)/shard_map/pallas_call | solution.py:311
  302.4 4.0 %shard_map.81 = (bf16[2048,6656]{1,0:T(8,128)(2,1)}, f32[16,52]{1,0:T(8,128)}) custom-call(s32[1]{0:T(128)} %bitcast.me_ref, bf16[512,26624]{1,0:T(8,128)(2,1)} %refs_0_.45, bf16[1024,6656]{1,0:T(8,128)(2,1)} %bitcast.3.refs_1_, bf16[512,512]{1,0:T(8,128)(2,1)S(1)} %collective-permute-done.12.refs_2_, ...), custom_call_target="tpu_custom_call", output_to_operand_aliasing={{0}: (12, {})} | custom-call | flops 44739240 | bytes 1398101 | tf_op jit(solution)/shard_map/pallas_call | solution.py:311
  (63 shorter events, 34.0 us)
Async XLA Ops:
  2.8 30.0 %collective-permute-start = (bf16[576,1024]{1,0:T(8,128)(2,1)}, bf16[576,1024]{1,0:T(8,128)(2,1)S(1)}, u32[]{:S(2)}, u32[]{:S(2)}) collective-permute-start(bf16[576,1024]{1,0:T(8,128)(2,1)} %get-tuple-element.45), channel_id=1, source_target_pairs={{0,2},{1,3},{2,0},{3,1},{4,6},{5,7},{6,4},{7,5},{8,10},{9,11},{10,... | collective-permute-start | bytes 3538952 | tf_op jit(solution)/shard_map/ppermute | solution.py:39
  7.8 25.0 %copy-start.1 = (bf16[64,1024]{1,0:T(8,128)(2,1)S(1)}, bf16[64,1024]{1,0:T(8,128)(2,1)}, u32[]{:S(2)}) copy-start(bf16[64,1024]{1,0:T(8,128)(2,1)} %get-tuple-element.46.refs_4_.refs_8_) | copy-start | bytes 393220
  7.8 47.1 %collective-permute-start.1 = (bf16[512,1024]{1,0:T(8,128)(2,1)}, bf16[512,1024]{1,0:T(8,128)(2,1)S(1)}, u32[]{:S(2)}, u32[]{:S(2)}) collective-permute-start(bf16[512,1024]{1,0:T(8,128)(2,1)} %shard_map.60), channel_id=1, source_target_pairs={{0,3},{1,2},{2,1},{3,0},{4,7},{5,6},{6,5},{7,4},{8,11},{9,10},{10,... | collective-permute-start | bytes 3145736 | tf_op jit(solution)/shard_map/ppermute | solution.py:39
  10.3 110.6 %collective-permute-start.4 = (bf16[512,1024]{1,0:T(8,128)(2,1)}, bf16[512,1024]{1,0:T(8,128)(2,1)}, u32[]{:S(2)}, u32[]{:S(2)}) collective-permute-start(bf16[512,1024]{1,0:T(8,128)(2,1)} %get-tuple-element.49), channel_id=1, source_target_pairs={{0,2},{1,3},{2,0},{3,1},{4,6},{5,7},{6,4},{7,5},{8,10},{9,11},{10,... | collective-permute-start | bytes 3145736 | tf_op jit(solution)/shard_map/ppermute | solution.py:39
  11.6 109.3 %collective-permute-start.5 = (bf16[512,1024]{1,0:T(8,128)(2,1)}, bf16[512,1024]{1,0:T(8,128)(2,1)}, u32[]{:S(2)}, u32[]{:S(2)}) collective-permute-start(bf16[512,1024]{1,0:T(8,128)(2,1)} %get-tuple-element.50), channel_id=1, source_target_pairs={{0,3},{1,2},{2,1},{3,0},{4,7},{5,6},{6,5},{7,4},{8,11},{9,10},{10,... | collective-permute-start | bytes 3145736 | tf_op jit(solution)/shard_map/ppermute | solution.py:39
  32.8 24.9 %copy-start.4 = (bf16[576,1024]{1,0:T(8,128)(2,1)}, bf16[576,1024]{1,0:T(8,128)(2,1)S(1)}, u32[]{:S(2)}) copy-start(bf16[576,1024]{1,0:T(8,128)(2,1)S(1)} %collective-permute-done.refs_2_) | copy-start | bytes 3538948
  32.8 45.9 %collective-permute-start.6 = (bf16[128,1024]{1,0:T(8,128)(2,1)S(1)}, bf16[128,1024]{1,0:T(8,128)(2,1)S(1)}, u32[]{:S(2)}, u32[]{:S(2)}) collective-permute-start(bf16[128,1024]{1,0:T(8,128)(2,1)S(1)} %pad_maximum_fusion), channel_id=1, source_target_pairs={{0,1},{1,0},{2,3},{3,2},{4,5},{5,4},{6,7},{7,6},{8,9},{9,8},{10,11... | collective-permute-start | bytes 786440 | tf_op jit(solution)/shard_map/ppermute | solution.py:39
  54.9 2.8 copy-start.6
  57.7 96.3 %collective-permute-start.2 = (bf16[512,1024]{1,0:T(8,128)(2,1)}, bf16[512,1024]{1,0:T(8,128)(2,1)}, u32[]{:S(2)}, u32[]{:S(2)}) collective-permute-start(bf16[512,1024]{1,0:T(8,128)(2,1)} %get-tuple-element.53), channel_id=1, source_target_pairs={{0,2},{1,3},{2,0},{3,1},{4,6},{5,7},{6,4},{7,5},{8,10},{9,11},{10,... | collective-permute-start | bytes 3145736 | tf_op jit(solution)/shard_map/ppermute | solution.py:39
  57.9 96.1 %collective-permute-start.3 = (bf16[512,1024]{1,0:T(8,128)(2,1)}, bf16[512,1024]{1,0:T(8,128)(2,1)}, u32[]{:S(2)}, u32[]{:S(2)}) collective-permute-start(bf16[512,1024]{1,0:T(8,128)(2,1)} %get-tuple-element.54), channel_id=1, source_target_pairs={{0,3},{1,2},{2,1},{3,0},{4,7},{5,6},{6,5},{7,4},{8,11},{9,10},{10,... | collective-permute-start | bytes 3145736 | tf_op jit(solution)/shard_map/ppermute | solution.py:39
  69.8 20.1 %copy-start = (bf16[64,6656]{1,0:T(8,128)(2,1)S(1)}, bf16[64,6656]{1,0:T(8,128)(2,1)}, u32[]{:S(2)}) copy-start(bf16[64,6656]{1,0:T(8,128)(2,1)} %refs_8_.25) | copy-start | bytes 2555908
  69.9 20.1 %all-to-all-start = ((bf16[2,512,6656]{2,1,0:T(8,128)(2,1)}), bf16[2,512,6656]{2,1,0:T(8,128)(2,1)}, u32[]{:S(2)}, u32[]{:S(2)}) async-start(bf16[2,512,6656]{2,1,0:T(8,128)(2,1)} %bitcast.14), calls=%async_computation | async-start | bytes 27262976 | tf_op jit(solution)/shard_map/all_to_all | solution.py:361
  90.0 25.1 %copy-start.2 = (f32[26624]{0:T(1024)S(1)}, f32[26624]{0:T(1024)}, u32[]{:S(2)}) copy-start(f32[26624]{0:T(1024)} %param.7) | copy-start | bytes 319492
  123.2 0.6 copy-start.3
  126.3 60.5 %collective-permute-start.9 = (bf16[528,1024]{1,0:T(8,128)(2,1)}, bf16[528,1024]{1,0:T(8,128)(2,1)S(1)}, u32[]{:S(2)}, u32[]{:S(2)}) collective-permute-start(bf16[528,1024]{1,0:T(8,128)(2,1)} %get-tuple-element.64), channel_id=1, source_target_pairs={{0,2},{1,3},{2,0},{3,1},{4,6},{5,7},{6,4},{7,5},{8,10},{9,11},{10,... | collective-permute-start | bytes 3244040 | tf_op jit(solution)/shard_map/ppermute | solution.py:39
  127.9 63.3 %collective-permute-start.10 = (bf16[528,1024]{1,0:T(8,128)(2,1)}, bf16[528,1024]{1,0:T(8,128)(2,1)}, u32[]{:S(2)}, u32[]{:S(2)}) collective-permute-start(bf16[528,1024]{1,0:T(8,128)(2,1)} %get-tuple-element.65), channel_id=1, source_target_pairs={{0,3},{1,2},{2,1},{3,0},{4,7},{5,6},{6,5},{7,4},{8,11},{9,10},{10,... | collective-permute-start | bytes 3244040 | tf_op jit(solution)/shard_map/ppermute | solution.py:39
  156.4 71.3 %collective-permute-start.7 = (bf16[512,1024]{1,0:T(8,128)(2,1)}, bf16[512,1024]{1,0:T(8,128)(2,1)}, u32[]{:S(2)}, u32[]{:S(2)}) collective-permute-start(bf16[512,1024]{1,0:T(8,128)(2,1)} %get-tuple-element.60), channel_id=1, source_target_pairs={{0,2},{1,3},{2,0},{3,1},{4,6},{5,7},{6,4},{7,5},{8,10},{9,11},{10,... | collective-permute-start | bytes 3145736 | tf_op jit(solution)/shard_map/ppermute | solution.py:39
  157.0 79.1 %collective-permute-start.8 = (bf16[512,1024]{1,0:T(8,128)(2,1)}, bf16[512,1024]{1,0:T(8,128)(2,1)}, u32[]{:S(2)}, u32[]{:S(2)}) collective-permute-start(bf16[512,1024]{1,0:T(8,128)(2,1)} %get-tuple-element.61), channel_id=1, source_target_pairs={{0,3},{1,2},{2,1},{3,0},{4,7},{5,6},{6,5},{7,4},{8,11},{9,10},{10,... | collective-permute-start | bytes 3145736 | tf_op jit(solution)/shard_map/ppermute | solution.py:39
  157.1 42.5 %collective-permute-start.11 = (f32[1,512]{1,0:T(1,128)S(1)}, f32[1,512]{1,0:T(1,128)S(1)}, u32[]{:S(2)}, u32[]{:S(2)}) collective-permute-start(f32[1,512]{1,0:T(1,128)S(1)} %slice.31), channel_id=1, source_target_pairs={{0,1},{1,0},{2,3},{3,2},{4,5},{5,4},{6,7},{7,6},{8,9},{9,8},{10,11... | collective-permute-start | bytes 6152 | tf_op jit(solution)/shard_map/ppermute | solution.py:39
  186.8 8.8 %copy-start.5 = (bf16[528,1024]{1,0:T(8,128)(2,1)}, bf16[528,1024]{1,0:T(8,128)(2,1)S(1)}, u32[]{:S(2)}) copy-start(bf16[528,1024]{1,0:T(8,128)(2,1)S(1)} %collective-permute-done.9.refs_2_) | copy-start | bytes 3244036
  193.6 77.5 %collective-permute-start.14 = (bf16[512,1024]{1,0:T(8,128)(2,1)}, bf16[512,1024]{1,0:T(8,128)(2,1)}, u32[]{:S(2)}, u32[]{:S(2)}) collective-permute-start(bf16[512,1024]{1,0:T(8,128)(2,1)} %get-tuple-element.79), channel_id=1, source_target_pairs={{0,2},{1,3},{2,0},{3,1},{4,6},{5,7},{6,4},{7,5},{8,10},{9,11},{10,... | collective-permute-start | bytes 3145736 | tf_op jit(solution)/shard_map/ppermute | solution.py:39
  193.8 87.2 %collective-permute-start.15 = (bf16[512,1024]{1,0:T(8,128)(2,1)}, bf16[512,1024]{1,0:T(8,128)(2,1)}, u32[]{:S(2)}, u32[]{:S(2)}) collective-permute-start(bf16[512,1024]{1,0:T(8,128)(2,1)} %get-tuple-element.80), channel_id=1, source_target_pairs={{0,3},{1,2},{2,1},{3,0},{4,7},{5,6},{6,5},{7,4},{8,11},{9,10},{10,... | collective-permute-start | bytes 3145736 | tf_op jit(solution)/shard_map/ppermute | solution.py:39
  238.2 63.6 %collective-permute-start.12 = (bf16[512,512]{1,0:T(8,128)(2,1)}, bf16[512,512]{1,0:T(8,128)(2,1)S(1)}, u32[]{:S(2)}, u32[]{:S(2)}) collective-permute-start(bf16[512,512]{1,0:T(8,128)(2,1)} %get-tuple-element.76), channel_id=1, source_target_pairs={{0,2},{1,3},{2,0},{3,1},{4,6},{5,7},{6,4},{7,5},{8,10},{9,11},{10,... | collective-permute-start | bytes 1572872 | tf_op jit(solution)/shard_map/ppermute | solution.py:39
  238.5 63.9 %collective-permute-start.13 = (bf16[512,512]{1,0:T(8,128)(2,1)}, bf16[512,512]{1,0:T(8,128)(2,1)S(1)}, u32[]{:S(2)}, u32[]{:S(2)}) collective-permute-start(bf16[512,512]{1,0:T(8,128)(2,1)} %get-tuple-element.77), channel_id=1, source_target_pairs={{0,3},{1,2},{2,1},{3,0},{4,7},{5,6},{6,5},{7,4},{8,11},{9,10},{10,... | collective-permute-start | bytes 1572872 | tf_op jit(solution)/shard_map/ppermute | solution.py:39
  284.2 3.7 %collective-permute-start.16 = (f32[1,1024]{1,0:T(1,128)S(1)}, f32[1,1024]{1,0:T(1,128)S(1)}, u32[]{:S(2)}, u32[]{:S(2)}) collective-permute-start(f32[1,1024]{1,0:T(1,128)S(1)} %shard_map.79), channel_id=1, source_target_pairs={{0,4},{4,0},{8,12},{12,8},{16,20},{20,16},{24,28},{28,24},{1,5},{5... | collective-permute-start | bytes 12296 | tf_op jit(solution)/shard_map/ppermute | solution.py:39
  287.9 3.6 %collective-permute-start.17 = (f32[1,1024]{1,0:T(1,128)S(1)}, f32[1,1024]{1,0:T(1,128)S(1)}, u32[]{:S(2)}, u32[]{:S(2)}) collective-permute-start(f32[1,1024]{1,0:T(1,128)S(1)} %add.31), channel_id=1, source_target_pairs={{0,8},{4,12},{8,0},{12,4},{16,24},{20,28},{24,16},{28,20},{1,9},{5... | collective-permute-start | bytes 12296 | tf_op jit(solution)/shard_map/ppermute | solution.py:39
  291.5 4.5 %collective-permute-start.18 = (f32[1,1024]{1,0:T(1,128)S(1)}, f32[1,1024]{1,0:T(1,128)S(1)}, u32[]{:S(2)}, u32[]{:S(2)}) collective-permute-start(f32[1,1024]{1,0:T(1,128)S(1)} %add.32), channel_id=1, source_target_pairs={{0,16},{4,20},{8,24},{12,28},{16,0},{20,4},{24,8},{28,12},{1,17},{... | collective-permute-start | bytes 12296 | tf_op jit(solution)/shard_map/ppermute | solution.py:39
where the time goes:
time: 307 us; the launch traced here: 306 us
  blocking collectives  102 us (33%)
  Pallas kernels  89.2 us (29%)
  waiting for transfers between devices  83.1 us (27%)
  starting transfers between devices  29.5 us (10%)
    psum x5, blocking collectives, body(): lax.psum(local, 'fsdp')  102 us
    ppermute x19, waiting for transfers between devices, swap(): return lax.ppermute(array, axis, [(i, i ^ d) for i in range(size)])  71.9 us
    pallas_call x7, Pallas kernels, export_chunk(): pl.pallas_call(functools.partial(export_kernel, tp, first), out_shape=res...  39.1 us
    pallas_call x9, Pallas kernels, move(): pl.pallas_call(functools.partial(move_kernel, moves, len(arrays)), out_sh...  28.9 us
    ppermute x19, starting transfers between devices, swap(): return lax.ppermute(array, axis, [(i, i ^ d) for i in range(size)])  20.6 us
    pallas_call x6, Pallas kernels, column_squares(): pl.pallas_call(functools.partial(squares_kernel, tp), out_shape=jax.Shape...  18.9 us
    all_to_all x1, waiting for transfers between devices, body(): lax.all_to_all(pack_near(after(me, *pieces), base, tp), 'tp', 0, 0, tiled...  11.2 us
    all_to_all x1, starting transfers between devices, body(): lax.all_to_all(pack_near(after(me, *pieces), base, tp), 'tp', 0, 0, tiled...  8.89 us
  transfers between devices with their start and end apart: 20, of which 10 were waited for; matrix products, arithmetic and copies ran while one was open for 0% of the time, Pallas kernels for 27%

commit v1 on v0

--- a/solution.py
+++ b/solution.py
@@ -42,8 +42,9 @@
 def total_of(array, size, axis):
     d = 1
     while d < size:
-        array = array + swap(array, d, size, axis)
-        d *= 2
+        others = (d,) if 2 * d == size else (d, 2 * d, 3 * d)
+        array = array + sum(swap(array, other, size, axis) for other in others)
+        d *= 1 + len(others)
     return array
 
 
@@ -86,7 +87,7 @@
 
 
 def parts_of(rows):
-    height = rows // 4 if rows % (4 * BLOCK) == 0 else rows
+    height = rows // 8 if rows % BLOCK == 0 else rows
     return [(r, height) for r in range(0, rows, height)]
 
 
@@ -150,10 +151,11 @@
         result = []
         for i, d in enumerate(distances):
             result += column_moves(me ^ d, rows, cols, group, first, i)
-            result.append((1, d * SUMS_ROWS, 0, SUMS_ROWS, terms.shape[1], i, rows, 0))
+            if d % 2 == 0:
+                result.append((1, d // 2 * SUMS_ROWS, 0, SUMS_ROWS, terms.shape[1], i, rows, 0))
         return result
 
-    return move(me, [base, terms], [(rows + SUMS_ROWS, cols)] * len(distances), moves)
+    return move(me, [base, terms], [(rows + (d + 1) % 2 * SUMS_ROWS, cols) for d in distances], moves)
 
 
 def pack_near(me, base, tp):
@@ -196,17 +198,31 @@
 
 
 def sender_squares_kernel(tp, me_ref, *refs):
-    pieces, rights, left, sums_ref, terms_ref = refs[:tp], refs[tp : 2 * tp], refs[-3], refs[-2], refs[-1]
+    pieces, rights, left, sums_ref = refs[:tp], refs[tp : 2 * tp], refs[-2], refs[-1]
+    for d in range(tp):
+        sums_ref[pl.ds(d, 1), :] = jnp.sum(squares_of(pieces[d], left, rights[d][...]), axis=0, keepdims=True)
+
+
+def terms_kernel(sums_ref, terms_ref):
     line = lax.broadcasted_iota(jnp.int32, (SUMS_ROWS, sums_ref.shape[1]), 0)
-    for d in range(tp):
-        sums = jnp.sum(squares_of(pieces[d], left, rights[d][...]), axis=0, keepdims=True)
-        sums_ref[pl.ds(d, 1), :] = sums
+    for i in range(sums_ref.shape[0]):
+        sums = sums_ref[pl.ds(i, 1), :]
         block = jnp.zeros(line.shape, jnp.float32)
         for term in range(TERMS):
             part = sums.astype(jnp.bfloat16).astype(jnp.float32)
             block = jnp.where(line == term, part, block)
             sums = sums - part
-        terms_ref[pl.ds(d * SUMS_ROWS, SUMS_ROWS), :] = block.astype(jnp.bfloat16)
+        terms_ref[pl.ds(i * SUMS_ROWS, SUMS_ROWS), :] = block.astype(jnp.bfloat16)
+
+
+def terms_of(sums):
+    rows, cols = sums.shape
+    return pl.pallas_call(
+        terms_kernel,
+        out_shape=jax.ShapeDtypeStruct((rows * SUMS_ROWS, cols), jnp.bfloat16),
+        compiler_params=PARAMS,
+        cost_estimate=cost(rows, cols, 0, 2),
+    )(sums)
 
 
 def column_squares(me, base, near, received, extras, right, unit, first, count):
@@ -236,58 +252,66 @@
     groups = base.shape[1] // (tp * unit)
     return pl.pallas_call(
         functools.partial(sender_squares_kernel, tp),
-        out_shape=[
-            jax.ShapeDtypeStruct((tp, count * unit), jnp.float32),
-            jax.ShapeDtypeStruct((tp * SUMS_ROWS, count * unit), jnp.bfloat16),
-        ],
+        out_shape=jax.ShapeDtypeStruct((tp, count * unit), jnp.float32),
         grid_spec=pltpu.PrefetchScalarGridSpec(
             num_scalar_prefetch=1,
             grid=(count,),
             in_specs=[group_spec(rows, unit, groups, first, d) for d in range(tp)]
             + [chunk_spec(rank, unit, lane // unit)] * tp
             + [left_spec(rank, lane)],
-            out_specs=[chunk_spec(tp, unit), chunk_spec(tp * SUMS_ROWS, unit)],
+            out_specs=chunk_spec(tp, unit),
         ),
         compiler_params=PARAMS,
         cost_estimate=cost(tp * rows, count * unit, rank, 1),
     )(me, *[base] * tp, *extras, extras[0])
 
 
-def export_kernel(tp, first, me_ref, *refs):
-    pieces, extras = refs[:tp], refs[tp : 2 * tp]
-    right_ref, squares_ref, mag_ref = refs[2 * tp : 2 * tp + 3]
+def export_kernel(tp, ds, first, me_ref, *refs):
+    number = len(ds)
+    pieces, extras = refs[:number], refs[number : 2 * number]
+    right_ref, squares_ref, mag_ref = refs[2 * number : 2 * number + 3]
     out_ref, scales_ref = refs[-2:]
     rows, cols = pieces[0].shape
     step = pl.program_id(0)
-    if len(refs) > 2 * tp + 5:
+    if len(refs) > 2 * number + 5:
         @pl.when(step == 0)
         def _():
-            scales_ref[...] = refs[2 * tp + 4][...]
+            scales_ref[...] = refs[2 * number + 4][...]
 
     factor = mag_ref[...] / jnp.sqrt(squares_ref[...] + EPSILON)
     right = right_ref[...]
-    height = min(rows, BLOCK)
-    for d in range(tp):
-        start = (me_ref[0] ^ d) * rows
-        for r in range(0, rows, height):
-            combined = pieces[d][pl.ds(r, height), :].astype(jnp.float32) + low_rank(extras[d], r, height, right)
-            span = pl.ds(pl.multiple_of(start + r, height), height)
-            out_ref[span, :] = (combined * factor).astype(jnp.bfloat16)
-
     lane = lax.broadcasted_iota(jnp.int32, (1, scales_ref.shape[1]), 1)
     per_step = cols // BLOCK
-    for i in range(tp * rows // BLOCK):
-        span = pl.ds(i * BLOCK, BLOCK)
-        line = scales_ref[pl.ds(i, 1), :]
+
+    def merge(i, r, height):
+        combined = pieces[i][pl.ds(r, height), :].astype(jnp.float32) + low_rank(extras[i], r, height, right)
+        return (combined * factor).astype(jnp.bfloat16)
+
+    def finish(merged, span, block):
+        line = scales_ref[pl.ds(block, 1), :]
         for j in range(per_step):
-            tile = out_ref[span, pl.ds(j * BLOCK, BLOCK)].astype(jnp.float32)
+            tile = merged[:, j * BLOCK : (j + 1) * BLOCK].astype(jnp.float32)
             largest = jnp.max(jnp.max(jnp.abs(tile), axis=0, keepdims=True), axis=1, keepdims=True)
             out_ref[span, pl.ds(j * BLOCK, BLOCK)] = (tile * (1.0 / (largest + EPSILON))).astype(jnp.bfloat16)
             line = jnp.where(lane == (first + step) * per_step + j, largest, line)
-        scales_ref[pl.ds(i, 1), :] = line
-
-
-def export_chunk(me, base, near, received, extras, right, squares, mag, unit, first, count, previous):
+        scales_ref[pl.ds(block, 1), :] = line
+
+    if rows % BLOCK == 0:
+        for i, d in enumerate(ds):
+            place = me_ref[0] ^ d
+            start = place * rows if out_ref.shape[0] > rows else 0
+            for r in range(0, rows, BLOCK):
+                span = pl.ds(pl.multiple_of(start + r, BLOCK), BLOCK)
+                finish(merge(i, r, BLOCK), span, place * (rows // BLOCK) + r // BLOCK)
+    else:
+        for i, d in enumerate(ds):
+            out_ref[pl.ds(pl.multiple_of((me_ref[0] ^ d) * rows, rows), rows), :] = merge(i, 0, rows)
+        for block in range(tp * rows // BLOCK):
+            span = pl.ds(block * BLOCK, BLOCK)
+            finish(out_ref[span, :], span, block)
+
+
+def export_chunk(me, base, near, received, extras, right, squares, mag, ds, unit, first, count, previous):
     rows = base.shape[0]
     rank, cols = right.shape
     tp = len(extras)
@@ -296,30 +320,36 @@
         jax.ShapeDtypeStruct((tp * rows, cols), jnp.bfloat16),
         jax.ShapeDtypeStruct((tp * rows // BLOCK, cols // BLOCK), jnp.float32),
     )
+    pieces = [base, near, *received]
+    piece_specs = [group_spec(rows, unit, groups, first), near_spec(rows, unit, first)]
+    piece_specs += [chunk_spec(rows, unit)] * (tp - 2)
     in_specs = (
-        [group_spec(rows, unit, groups, first), near_spec(rows, unit, first)]
-        + [chunk_spec(rows, unit)] * (tp - 2)
-        + [left_spec(rank, max(rows, BLOCK))] * tp
+        [piece_specs[d] for d in ds]
+        + [left_spec(rank, max(rows, BLOCK))] * len(ds)
         + [chunk_spec(rank, unit, first), chunk_spec(1, unit), group_spec(1, unit, groups, first)]
     )
-    args = [base, near, *received, *extras, right, squares, mag]
+    args = [pieces[d] for d in ds] + [extras[d] for d in ds] + [right, squares, mag]
     aliases = {}
     if previous is not None:
         in_specs += [pl.BlockSpec(memory_space=pl.ANY), whole_spec(previous[1])]
         args += list(previous)
         aliases = {len(args) - 1: 0}
+    if len(ds) == 1:
+        out_spec = pl.BlockSpec((rows, unit), lambda j, me: (me[0] ^ ds[0], first + j))
+    else:
+        out_spec = chunk_spec(tp * rows, unit, first)
     return pl.pallas_call(
-        functools.partial(export_kernel, tp, first),
+        functools.partial(export_kernel, tp, ds, first),
         out_shape=result,
         grid_spec=pltpu.PrefetchScalarGridSpec(
             num_scalar_prefetch=1,
             grid=(count,),
             in_specs=in_specs,
-            out_specs=(chunk_spec(tp * rows, unit, first), whole_spec(result[1])),
+            out_specs=(out_spec, whole_spec(result[1])),
         ),
         input_output_aliases=aliases,
         compiler_params=PARAMS,
-        cost_estimate=cost(tp * rows, count * unit, rank, 2),
+        cost_estimate=cost(len(ds) * rows, count * unit, rank, 2),
     )(me, *args)
 
 
@@ -378,17 +408,18 @@
             turn = after(me, *received[k], *token)
             if following == CARRIER:
                 width = width_of(late[0], late[1] - late[0], blocks, lane // BLOCK)
-                sums, terms = sender_squares(
+                sums = sender_squares(
                     turn, base, extras, rank, width * BLOCK, late[0] // width, (late[1] - late[0]) // width, lane
                 )
-                late_sums = sums[:1] + swap(sums[1:2], 1, tp)
-                send(following, pack_carrier(turn, base, tp, far, terms, *span(following)))
+                sums = sums[0::2] + swap(sums[1::2], 1, tp)
+                late_sums = sums[:1]
+                send(following, pack_carrier(turn, base, tp, far, terms_of(sums), *span(following)))
             else:
                 send(following, pack(turn, base, tp, far, *span(following)))
         if k < early:
             local = column_squares(after(me, *token), base, near, received[k], extras, right, *units(k))
             if k == CARRIER:
-                for piece in received[k]:
+                for piece in received[k][::2]:
                     parts = after(piece, *token)[rows : rows + TERMS, : late_sums.shape[1]].astype(jnp.float32)
                     late_sums = late_sums + jnp.sum(parts, axis=0, keepdims=True)
                 local = jnp.concatenate([local, late_sums], axis=1)
@@ -398,7 +429,9 @@
                 for i in range(early, len(chunks)):
                     start = span(k)[1] + span(i)[0] - late[0] * BLOCK
                     totals[i] = total[:, start : start + span(i)[1]]
-        result = export_chunk(me, base, near, received[k], extras, right, totals[k], mag, *units(k), result)
+        split = k == len(chunks) - 1 and rows % BLOCK == 0 and tp > 2
+        for ds in (tuple(range(tp - 1)), (tp - 1,)) if split else (tuple(range(tp)),):
+            result = export_chunk(me, base, near, received[k], extras, right, totals[k], mag, ds, *units(k), result)
         token = (result[1],)
     return result
 

time: 307 us -> 307 us (level)
  waiting for transfers between devices: 83.1 us -> 70.8 us
  blocking collectives: 102 us -> 110 us
    psum x5, blocking collectives: 102 us -> 110 us  [body(): lax.psum(local, 'fsdp')]
    all_to_all x1, waiting for transfers between devices: 11.2 us -> 3.49 us  [body(): lax.all_to_all(pack_near(after(me, *pieces), base, tp), 'tp', 0, 0, tiled...]
    ppermute x19 -> x20, waiting for transfers between devices: 71.9 us -> 67.3 us  [swap(): return lax.ppermute(array, axis, [(i, i ^ d) for i in range(size)])]
    pallas_call x8 -> x10, Pallas kernels: 41.4 us -> 42.9 us  [the longest x8 40.5 us: export_chunk(): pl.pallas_call(functools.partial(export_kernel, tp, ds, first), out_shape...]
    ppermute x19 -> x20, starting transfers between devices: 20.6 us -> 21.8 us  [swap(): return lax.ppermute(array, axis, [(i, i ^ d) for i in range(size)])]
  transfers between devices with their start and end apart: 20 -> 21, of which waited for: 10 -> 13; matrix products, arithmetic and copies ran while one was open for 0% -> 0% of each run, Pallas kernels for 27% -> 29%
where the time goes in v1:
time: 307 us; the launch traced here: 306 us
  blocking collectives  110 us (36%)
  Pallas kernels  91.8 us (30%)
  waiting for transfers between devices  70.8 us (23%)
  starting transfers between devices  30.7 us (10%)
    psum x5, blocking collectives, body(): lax.psum(local, 'fsdp')  110 us
    ppermute x20, waiting for transfers between devices, swap(): return lax.ppermute(array, axis, [(i, i ^ d) for i in range(size)])  67.3 us
    pallas_call x8, Pallas kernels, export_chunk(): pl.pallas_call(functools.partial(export_kernel, tp, ds, first), out_shape...  40.5 us
    pallas_call x9, Pallas kernels, move(): pl.pallas_call(functools.partial(move_kernel, moves, len(arrays)), out_sh...  30.1 us
    ppermute x20, starting transfers between devices, swap(): return lax.ppermute(array, axis, [(i, i ^ d) for i in range(size)])  21.8 us
    pallas_call x6, Pallas kernels, column_squares(): pl.pallas_call(functools.partial(squares_kernel, tp), out_shape=jax.Shape...  18.8 us
    all_to_all x1, starting transfers between devices, body(): lax.all_to_all(pack_near(after(me, *pieces), base, tp), 'tp', 0, 0, tiled...  8.9 us
  transfers between devices with their start and end apart: 21, of which 13 were waited for; matrix products, arithmetic and copies ran while one was open for 0% of the time, Pallas kernels for 29%

profile of v1, /device:TPU:0, one launch (start us, length us, event | category | flops | bytes accessed | tf_op | source)
XLA Modules:
  0.0 305.8 jit_solution(3215063749793441974)
XLA Ops:
  2.9 3.0 collective-permute-start
  12.6 20.3 %collective-permute-done.refs_2_ = bf16[576,1024]{1,0:T(8,128)(2,1)S(1)} collective-permute-done((bf16[576,1024]{1,0:T(8,128)(2,1)}, bf16[576,1024]{1,0:T(8,128)(2,1)S(1)}, u32[]{:S(2)}, u32[]{:S(2)}) %collective-permute-start) | collective-permute-done | bytes 1179680 | tf_op jit(solution)/shard_map/ppermute | solution.py:39
  33.0 10.1 %shard_map.63 = bf16[1024,6656]{1,0:T(8,128)(2,1)} custom-call(s32[1]{0:T(128)} %bitcast.me_ref, bf16[512,26624]{1,0:T(8,128)(2,1)} %refs_0_.45), custom_call_target="tpu_custom_call" | custom-call | bytes 9087658 | tf_op jit(solution)/shard_map/pallas_call | solution.py:73
  43.1 8.9 %all-to-all-start = ((bf16[2,512,6656]{2,1,0:T(8,128)(2,1)}), bf16[2,512,6656]{2,1,0:T(8,128)(2,1)}, u32[]{:S(2)}, u32[]{:S(2)}) async-start(bf16[2,512,6656]{2,1,0:T(8,128)(2,1)} %bitcast.14), calls=%async_computation | async-start | bytes 27262976 | tf_op jit(solution)/shard_map/all_to_all | solution.py:391
  52.0 3.0 collective-permute-done.1.refs_3_
  55.0 2.6 shard_map.61
  59.8 3.5 %all-to-all-done = bf16[2,512,6656]{2,1,0:T(8,128)(2,1)} async-done(((bf16[2,512,6656]{2,1,0:T(8,128)(2,1)}), bf16[2,512,6656]{2,1,0:T(8,128)(2,1)}, u32[]{:S(2)}, u32[]{:S(2)}) %all-to-all-start) | async-done | bytes 13631520 | tf_op jit(solution)/shard_map/all_to_all | solution.py:391
  63.3 3.1 %shard_map.64 = f32[1,1024]{1,0:T(1,128)S(1)} custom-call(s32[1]{0:T(128)} %bitcast.me_ref, bf16[512,26624]{1,0:T(8,128)(2,1)} %refs_0_.45, bf16[1024,6656]{1,0:T(8,128)(2,1)} %bitcast.3.refs_1_, bf16[576,1024]{1,0:T(8,128)(2,1)} %copy-done.4, bf16[512,1024]{1,0:T(8,128)(2,1)} %collective-permute-done.1.refs_3_, bf16[64,1024]{1,0:T(8,128)(2,1)S(1)} %copy-done.1, ...), custom_call_target="tpu_custom_call" | custom-call | flops 89478488 | bytes 1398101 | tf_op jit(solution)/shard_map/pallas_call | solution.py:232
  66.4 22.3 %psum.35.refs_9_ = f32[1,1024]{1,0:T(1,128)S(1)} all-reduce(f32[1,1024]{1,0:T(1,128)S(1)} %shard_map.64), channel_id=1, replica_groups=mesh['fsdp'=8,'tp'=4] {'fsdp'}, use_global_device_ids=true, to_apply=%region_0.1 | all-reduce | flops 1024 | bytes 8192 | tf_op jit(solution)/shard_map/psum | solution.py:426
  88.6 5.8 %shard_map.65 = (bf16[2048,6656]{1,0:T(8,128)(2,1)}, f32[16,52]{1,0:T(8,128)S(1)}) custom-call(s32[1]{0:T(128)} %bitcast.me_ref, bf16[512,26624]{1,0:T(8,128)(2,1)} %refs_0_.45, bf16[1024,6656]{1,0:T(8,128)(2,1)} %bitcast.3.refs_1_, bf16[576,1024]{1,0:T(8,128)(2,1)} %copy-done.4, bf16[512,1024]{1,0:T(8,128)(2,1)} %collective-permute-done.1.refs_3_, ...), custom_call_target="tpu_custom_call" | custom-call | flops 89478488 | bytes 2796202 | tf_op jit(solution)/shard_map/pallas_call | solution.py:341
  94.5 5.5 %collective-permute-done.5.refs_3_ = bf16[512,1024]{1,0:T(8,128)(2,1)} collective-permute-done((bf16[512,1024]{1,0:T(8,128)(2,1)}, bf16[512,1024]{1,0:T(8,128)(2,1)}, u32[]{:S(2)}, u32[]{:S(2)}) %collective-permute-start.5) | collective-permute-done | bytes 1048608 | tf_op jit(solution)/shard_map/ppermute | solution.py:39
  108.9 3.1 %shard_map.66 = f32[1,1024]{1,0:T(1,128)S(1)} custom-call(s32[1]{0:T(128)} %bitcast.me_ref, bf16[512,26624]{1,0:T(8,128)(2,1)} %refs_0_.45, bf16[1024,6656]{1,0:T(8,128)(2,1)} %bitcast.3.refs_1_, bf16[512,1024]{1,0:T(8,128)(2,1)} %collective-permute-done.4.refs_2_, bf16[512,1024]{1,0:T(8,128)(2,1)} %collective-permute-done.5.refs_3_, ...), custom_call_target="tpu_custom_call" | custom-call | flops 89478488 | bytes 1398101 | tf_op jit(solution)/shard_map/pallas_call | solution.py:232
  112.0 21.8 %psum.36.refs_9_ = f32[1,1024]{1,0:T(1,128)S(1)} all-reduce(f32[1,1024]{1,0:T(1,128)S(1)} %shard_map.66), channel_id=1, replica_groups=mesh['fsdp'=8,'tp'=4] {'fsdp'}, use_global_device_ids=true, to_apply=%region_1.2 | all-reduce | flops 1024 | bytes 8192 | tf_op jit(solution)/shard_map/psum | solution.py:426
  133.9 5.9 %shard_map.67 = (bf16[2048,6656]{1,0:T(8,128)(2,1)}, f32[16,52]{1,0:T(8,128)S(1)}) custom-call(s32[1]{0:T(128)} %bitcast.me_ref, bf16[512,26624]{1,0:T(8,128)(2,1)} %refs_0_.45, bf16[1024,6656]{1,0:T(8,128)(2,1)} %bitcast.3.refs_1_, bf16[512,1024]{1,0:T(8,128)(2,1)} %collective-permute-done.4.refs_2_, ...), custom_call_target="tpu_custom_call", output_to_operand_aliasing={{0}: (12, {})} | custom-call | flops 89478488 | bytes 2796202 | tf_op jit(solution)/shard_map/pallas_call | solution.py:341
  139.8 5.1 %collective-permute-done.3.refs_3_ = bf16[512,1024]{1,0:T(8,128)(2,1)} collective-permute-done((bf16[512,1024]{1,0:T(8,128)(2,1)}, bf16[512,1024]{1,0:T(8,128)(2,1)}, u32[]{:S(2)}, u32[]{:S(2)}) %collective-permute-start.3) | collective-permute-done | bytes 1048608 | tf_op jit(solution)/shard_map/ppermute | solution.py:39
  149.6 3.1 %shard_map.72 = f32[1,1024]{1,0:T(1,128)S(1)} custom-call(s32[1]{0:T(128)} %bitcast.me_ref, bf16[512,26624]{1,0:T(8,128)(2,1)} %refs_0_.45, bf16[1024,6656]{1,0:T(8,128)(2,1)} %bitcast.3.refs_1_, bf16[512,1024]{1,0:T(8,128)(2,1)} %collective-permute-done.2.refs_2_, bf16[512,1024]{1,0:T(8,128)(2,1)} %collective-permute-done.3.refs_3_, ...), custom_call_target="tpu_custom_call" | custom-call | flops 89478488 | bytes 1398101 | tf_op jit(solution)/shard_map/pallas_call | solution.py:232
  152.8 21.9 %psum.37.refs_9_ = f32[1,1024]{1,0:T(1,128)S(1)} all-reduce(f32[1,1024]{1,0:T(1,128)S(1)} %shard_map.72), channel_id=1, replica_groups=mesh['fsdp'=8,'tp'=4] {'fsdp'}, use_global_device_ids=true, to_apply=%region_2.3 | all-reduce | flops 1024 | bytes 8192 | tf_op jit(solution)/shard_map/psum | solution.py:426
  174.6 5.9 %shard_map.73 = (bf16[2048,6656]{1,0:T(8,128)(2,1)}, f32[16,52]{1,0:T(8,128)S(1)}) custom-call(s32[1]{0:T(128)} %bitcast.me_ref, bf16[512,26624]{1,0:T(8,128)(2,1)} %refs_0_.45, bf16[1024,6656]{1,0:T(8,128)(2,1)} %bitcast.3.refs_1_, bf16[512,1024]{1,0:T(8,128)(2,1)} %collective-permute-done.2.refs_2_, ...), custom_call_target="tpu_custom_call", output_to_operand_aliasing={{0}: (12, {})} | custom-call | flops 89478488 | bytes 2796202 | tf_op jit(solution)/shard_map/pallas_call | solution.py:341
  180.6 10.0 %collective-permute-done.11.refs_3_ = bf16[512,1024]{1,0:T(8,128)(2,1)} collective-permute-done((bf16[512,1024]{1,0:T(8,128)(2,1)}, bf16[512,1024]{1,0:T(8,128)(2,1)}, u32[]{:S(2)}, u32[]{:S(2)}) %collective-permute-start.11) | collective-permute-done | bytes 1048608 | tf_op jit(solution)/shard_map/ppermute | solution.py:39
  190.6 3.0 shard_map.77
  195.6 3.1 %shard_map.74 = f32[1,1024]{1,0:T(1,128)S(1)} custom-call(s32[1]{0:T(128)} %bitcast.me_ref, bf16[512,26624]{1,0:T(8,128)(2,1)} %refs_0_.45, bf16[1024,6656]{1,0:T(8,128)(2,1)} %bitcast.3.refs_1_, bf16[528,1024]{1,0:T(8,128)(2,1)} %copy-done.5, bf16[512,1024]{1,0:T(8,128)(2,1)} %collective-permute-done.11.refs_3_, bf16[64,1024]{1,0:T(8,128)(2,1)S(1)} %copy-done.1, ...), custom_call_target="tpu_custom_call" | custom-call | flops 89478488 | bytes 1398101 | tf_op jit(solution)/shard_map/pallas_call | solution.py:232
  199.5 22.3 %psum.38 = f32[1,1536]{1,0:T(1,128)S(1)} all-reduce(f32[1,1536]{1,0:T(1,128)S(1)} %pad_maximum_fusion.1), channel_id=1, replica_groups=mesh['fsdp'=8,'tp'=4] {'fsdp'}, use_global_device_ids=true, to_apply=%region_4.5 | all-reduce | flops 1536 | bytes 12288 | tf_op jit(solution)/shard_map/psum | solution.py:426
  221.8 5.9 %shard_map.75 = (bf16[2048,6656]{1,0:T(8,128)(2,1)}, f32[16,52]{1,0:T(8,128)S(1)}) custom-call(s32[1]{0:T(128)} %bitcast.me_ref, bf16[512,26624]{1,0:T(8,128)(2,1)} %refs_0_.45, bf16[1024,6656]{1,0:T(8,128)(2,1)} %bitcast.3.refs_1_, bf16[528,1024]{1,0:T(8,128)(2,1)} %copy-done.5, ...), custom_call_target="tpu_custom_call", output_to_operand_aliasing={{0}: (12, {})} | custom-call | flops 89478488 | bytes 2796202 | tf_op jit(solution)/shard_map/pallas_call | solution.py:341
  227.7 7.8 %collective-permute-done.8.refs_3_ = bf16[512,1024]{1,0:T(8,128)(2,1)} collective-permute-done((bf16[512,1024]{1,0:T(8,128)(2,1)}, bf16[512,1024]{1,0:T(8,128)(2,1)}, u32[]{:S(2)}, u32[]{:S(2)}) %collective-permute-start.8) | collective-permute-done | bytes 1048608 | tf_op jit(solution)/shard_map/ppermute | solution.py:39
  239.7 3.2 %shard_map.78 = f32[1,1024]{1,0:T(1,128)S(1)} custom-call(s32[1]{0:T(128)} %bitcast.me_ref, bf16[512,26624]{1,0:T(8,128)(2,1)} %refs_0_.45, bf16[1024,6656]{1,0:T(8,128)(2,1)} %bitcast.3.refs_1_, bf16[512,1024]{1,0:T(8,128)(2,1)} %collective-permute-done.7.refs_2_, bf16[512,1024]{1,0:T(8,128)(2,1)} %collective-permute-done.8.refs_3_, ...), custom_call_target="tpu_custom_call" | custom-call | flops 89478488 | bytes 1398101 | tf_op jit(solution)/shard_map/pallas_call | solution.py:232
  242.9 21.9 %psum.39.refs_9_ = f32[1,1024]{1,0:T(1,128)S(1)} all-reduce(f32[1,1024]{1,0:T(1,128)S(1)} %shard_map.78), channel_id=1, replica_groups=mesh['fsdp'=8,'tp'=4] {'fsdp'}, use_global_device_ids=true, to_apply=%region_5.6 | all-reduce | flops 1024 | bytes 8192 | tf_op jit(solution)/shard_map/psum | solution.py:426
  264.8 6.0 %shard_map.79 = (bf16[2048,6656]{1,0:T(8,128)(2,1)}, f32[16,52]{1,0:T(8,128)S(1)}) custom-call(s32[1]{0:T(128)} %bitcast.me_ref, bf16[512,26624]{1,0:T(8,128)(2,1)} %refs_0_.45, bf16[1024,6656]{1,0:T(8,128)(2,1)} %bitcast.3.refs_1_, bf16[512,1024]{1,0:T(8,128)(2,1)} %collective-permute-done.7.refs_2_, ...), custom_call_target="tpu_custom_call", output_to_operand_aliasing={{0}: (12, {})} | custom-call | flops 89478488 | bytes 2796202 | tf_op jit(solution)/shard_map/pallas_call | solution.py:341
  270.7 9.7 %collective-permute-done.15.refs_3_ = bf16[512,1024]{1,0:T(8,128)(2,1)} collective-permute-done((bf16[512,1024]{1,0:T(8,128)(2,1)}, bf16[512,1024]{1,0:T(8,128)(2,1)}, u32[]{:S(2)}, u32[]{:S(2)}) %collective-permute-start.15) | collective-permute-done | bytes 1048608 | tf_op jit(solution)/shard_map/ppermute | solution.py:39
  280.5 3.1 %shard_map.80 = f32[1,1024]{1,0:T(1,128)S(1)} custom-call(s32[1]{0:T(128)} %bitcast.me_ref, bf16[512,26624]{1,0:T(8,128)(2,1)} %refs_0_.45, bf16[1024,6656]{1,0:T(8,128)(2,1)} %bitcast.3.refs_1_, bf16[512,1024]{1,0:T(8,128)(2,1)} %collective-permute-done.14.refs_2_, bf16[512,1024]{1,0:T(8,128)(2,1)} %collective-permute-done.15.refs_3_, ...), custom_call_target="tpu_custom_call" | custom-call | flops 89478488 | bytes 1398101 | tf_op jit(solution)/shard_map/pallas_call | solution.py:232
  290.3 2.7 collective-permute-start.19
  294.8 5.9 %shard_map.81 = (bf16[2048,6656]{1,0:T(8,128)(2,1)}, f32[16,52]{1,0:T(8,128)S(1)}) custom-call(s32[1]{0:T(128)} %bitcast.me_ref, bf16[512,26624]{1,0:T(8,128)(2,1)} %refs_0_.45, bf16[1024,6656]{1,0:T(8,128)(2,1)} %bitcast.3.refs_1_, bf16[512,1024]{1,0:T(8,128)(2,1)} %collective-permute-done.14.refs_2_, ...), custom_call_target="tpu_custom_call", output_to_operand_aliasing={{0}: (12, {})} | custom-call | flops 89478488 | bytes 2796202 | tf_op jit(solution)/shard_map/pallas_call | solution.py:341
  300.8 3.7 %shard_map.82 = (bf16[2048,6656]{1,0:T(8,128)(2,1)}, f32[16,52]{1,0:T(8,128)S(1)}) custom-call(s32[1]{0:T(128)} %bitcast.me_ref, bf16[512,26624]{1,0:T(8,128)(2,1)} %refs_0_.45, bf16[1024,6656]{1,0:T(8,128)(2,1)} %bitcast.3.refs_1_, bf16[512,512]{1,0:T(8,128)(2,1)S(1)} %collective-permute-done.13.refs_2_, ...), custom_call_target="tpu_custom_call", output_to_operand_aliasing={{0}: (10, {})} | custom-call | flops 33554432 | bytes 1048576 | tf_op jit(solution)/shard_map/pallas_call | solution.py:341
  (65 shorter events, 41.6 us)
Async XLA Ops:
  2.9 30.0 %collective-permute-start = (bf16[576,1024]{1,0:T(8,128)(2,1)}, bf16[576,1024]{1,0:T(8,128)(2,1)S(1)}, u32[]{:S(2)}, u32[]{:S(2)}) collective-permute-start(bf16[576,1024]{1,0:T(8,128)(2,1)} %get-tuple-element.44), channel_id=1, source_target_pairs={{0,2},{1,3},{2,0},{3,1},{4,6},{5,7},{6,4},{7,5},{8,10},{9,11},{10,... | collective-permute-start | bytes 3538952 | tf_op jit(solution)/shard_map/ppermute | solution.py:39
  5.9 27.0 %copy-start.1 = (bf16[64,1024]{1,0:T(8,128)(2,1)S(1)}, bf16[64,1024]{1,0:T(8,128)(2,1)}, u32[]{:S(2)}) copy-start(bf16[64,1024]{1,0:T(8,128)(2,1)} %get-tuple-element.45.refs_4_.refs_8_.refs_3_) | copy-start | bytes 393220
  8.0 47.0 %collective-permute-start.1 = (bf16[512,1024]{1,0:T(8,128)(2,1)}, bf16[512,1024]{1,0:T(8,128)(2,1)}, u32[]{:S(2)}, u32[]{:S(2)}) collective-permute-start(bf16[512,1024]{1,0:T(8,128)(2,1)} %shard_map.60), channel_id=1, source_target_pairs={{0,3},{1,2},{2,1},{3,0},{4,7},{5,6},{6,5},{7,4},{8,11},{9,10},{10,... | collective-permute-start | bytes 3145736 | tf_op jit(solution)/shard_map/ppermute | solution.py:39
  10.7 83.8 %collective-permute-start.4 = (bf16[512,1024]{1,0:T(8,128)(2,1)}, bf16[512,1024]{1,0:T(8,128)(2,1)}, u32[]{:S(2)}, u32[]{:S(2)}) collective-permute-start(bf16[512,1024]{1,0:T(8,128)(2,1)} %get-tuple-element.51), channel_id=1, source_target_pairs={{0,2},{1,3},{2,0},{3,1},{4,6},{5,7},{6,4},{7,5},{8,10},{9,11},{10,... | collective-permute-start | bytes 3145736 | tf_op jit(solution)/shard_map/ppermute | solution.py:39
  12.0 88.0 %collective-permute-start.5 = (bf16[512,1024]{1,0:T(8,128)(2,1)}, bf16[512,1024]{1,0:T(8,128)(2,1)}, u32[]{:S(2)}, u32[]{:S(2)}) collective-permute-start(bf16[512,1024]{1,0:T(8,128)(2,1)} %get-tuple-element.52), channel_id=1, source_target_pairs={{0,3},{1,2},{2,1},{3,0},{4,7},{5,6},{6,5},{7,4},{8,11},{9,10},{10,... | collective-permute-start | bytes 3145736 | tf_op jit(solution)/shard_map/ppermute | solution.py:39
  32.9 10.2 %copy-start.4 = (bf16[576,1024]{1,0:T(8,128)(2,1)}, bf16[576,1024]{1,0:T(8,128)(2,1)S(1)}, u32[]{:S(2)}) copy-start(bf16[576,1024]{1,0:T(8,128)(2,1)S(1)} %collective-permute-done.refs_2_) | copy-start | bytes 3538948
  32.9 26.8 %collective-permute-start.6 = (bf16[128,1024]{1,0:T(8,128)(2,1)S(1)}, bf16[128,1024]{1,0:T(8,128)(2,1)S(1)}, u32[]{:S(2)}, u32[]{:S(2)}) collective-permute-start(bf16[128,1024]{1,0:T(8,128)(2,1)S(1)} %pad_maximum_fusion), channel_id=1, source_target_pairs={{0,1},{1,0},{2,3},{3,2},{4,5},{5,4},{6,7},{7,6},{8,9},{9,8},{10,11... | collective-permute-start | bytes 786440 | tf_op jit(solution)/shard_map/ppermute | solution.py:39
  43.1 20.2 %copy-start = (bf16[64,6656]{1,0:T(8,128)(2,1)S(1)}, bf16[64,6656]{1,0:T(8,128)(2,1)}, u32[]{:S(2)}) copy-start(bf16[64,6656]{1,0:T(8,128)(2,1)} %refs_2_.5) | copy-start | bytes 2555908
  43.1 20.1 %all-to-all-start = ((bf16[2,512,6656]{2,1,0:T(8,128)(2,1)}), bf16[2,512,6656]{2,1,0:T(8,128)(2,1)}, u32[]{:S(2)}, u32[]{:S(2)}) async-start(bf16[2,512,6656]{2,1,0:T(8,128)(2,1)} %bitcast.14), calls=%async_computation | async-start | bytes 27262976 | tf_op jit(solution)/shard_map/all_to_all | solution.py:391
  57.7 31.0 %copy-start.2 = (f32[26624]{0:T(1024)S(1)}, f32[26624]{0:T(1024)}, u32[]{:S(2)}) copy-start(f32[26624]{0:T(1024)} %param.7) | copy-start | bytes 319492
  57.7 82.1 %collective-permute-start.2 = (bf16[512,1024]{1,0:T(8,128)(2,1)}, bf16[512,1024]{1,0:T(8,128)(2,1)}, u32[]{:S(2)}, u32[]{:S(2)}) collective-permute-start(bf16[512,1024]{1,0:T(8,128)(2,1)} %get-tuple-element.48), channel_id=1, source_target_pairs={{0,2},{1,3},{2,0},{3,1},{4,6},{5,7},{6,4},{7,5},{8,10},{9,11},{10,... | collective-permute-start | bytes 3145736 | tf_op jit(solution)/shard_map/ppermute | solution.py:39
  57.9 87.0 %collective-permute-start.3 = (bf16[512,1024]{1,0:T(8,128)(2,1)}, bf16[512,1024]{1,0:T(8,128)(2,1)}, u32[]{:S(2)}, u32[]{:S(2)}) collective-permute-start(bf16[512,1024]{1,0:T(8,128)(2,1)} %get-tuple-element.49), channel_id=1, source_target_pairs={{0,3},{1,2},{2,1},{3,0},{4,7},{5,6},{6,5},{7,4},{8,11},{9,10},{10,... | collective-permute-start | bytes 3145736 | tf_op jit(solution)/shard_map/ppermute | solution.py:39
  102.3 1.2 collective-permute-start.9
  103.6 0.6 copy-start.3
  106.8 83.8 %collective-permute-start.10 = (bf16[528,1024]{1,0:T(8,128)(2,1)}, bf16[528,1024]{1,0:T(8,128)(2,1)S(1)}, u32[]{:S(2)}, u32[]{:S(2)}) collective-permute-start(bf16[528,1024]{1,0:T(8,128)(2,1)} %get-tuple-element.62), channel_id=1, source_target_pairs={{0,2},{1,3},{2,0},{3,1},{4,6},{5,7},{6,4},{7,5},{8,10},{9,11},{10,... | collective-permute-start | bytes 3244040 | tf_op jit(solution)/shard_map/ppermute | solution.py:39
  108.8 81.7 %collective-permute-start.11 = (bf16[512,1024]{1,0:T(8,128)(2,1)}, bf16[512,1024]{1,0:T(8,128)(2,1)}, u32[]{:S(2)}, u32[]{:S(2)}) collective-permute-start(bf16[512,1024]{1,0:T(8,128)(2,1)} %get-tuple-element.63), channel_id=1, source_target_pairs={{0,3},{1,2},{2,1},{3,0},{4,7},{5,6},{6,5},{7,4},{8,11},{9,10},{10,... | collective-permute-start | bytes 3145736 | tf_op jit(solution)/shard_map/ppermute | solution.py:39
  147.6 80.2 %collective-permute-start.7 = (bf16[512,1024]{1,0:T(8,128)(2,1)}, bf16[512,1024]{1,0:T(8,128)(2,1)}, u32[]{:S(2)}, u32[]{:S(2)}) collective-permute-start(bf16[512,1024]{1,0:T(8,128)(2,1)} %get-tuple-element.59), channel_id=1, source_target_pairs={{0,2},{1,3},{2,0},{3,1},{4,6},{5,7},{6,4},{7,5},{8,10},{9,11},{10,... | collective-permute-start | bytes 3145736 | tf_op jit(solution)/shard_map/ppermute | solution.py:39
  147.8 87.7 %collective-permute-start.8 = (bf16[512,1024]{1,0:T(8,128)(2,1)}, bf16[512,1024]{1,0:T(8,128)(2,1)}, u32[]{:S(2)}, u32[]{:S(2)}) collective-permute-start(bf16[512,1024]{1,0:T(8,128)(2,1)} %get-tuple-element.60), channel_id=1, source_target_pairs={{0,3},{1,2},{2,1},{3,0},{4,7},{5,6},{6,5},{7,4},{8,11},{9,10},{10,... | collective-permute-start | bytes 3145736 | tf_op jit(solution)/shard_map/ppermute | solution.py:39
  190.6 5.0 %copy-start.5 = (bf16[528,1024]{1,0:T(8,128)(2,1)}, bf16[528,1024]{1,0:T(8,128)(2,1)S(1)}, u32[]{:S(2)}) copy-start(bf16[528,1024]{1,0:T(8,128)(2,1)S(1)} %collective-permute-done.10.refs_2_) | copy-start | bytes 3244036
  193.6 77.2 %collective-permute-start.14 = (bf16[512,1024]{1,0:T(8,128)(2,1)}, bf16[512,1024]{1,0:T(8,128)(2,1)}, u32[]{:S(2)}, u32[]{:S(2)}) collective-permute-start(bf16[512,1024]{1,0:T(8,128)(2,1)} %get-tuple-element.75), channel_id=1, source_target_pairs={{0,2},{1,3},{2,0},{3,1},{4,6},{5,7},{6,4},{7,5},{8,10},{9,11},{10,... | collective-permute-start | bytes 3145736 | tf_op jit(solution)/shard_map/ppermute | solution.py:39
  193.8 86.6 %collective-permute-start.15 = (bf16[512,1024]{1,0:T(8,128)(2,1)}, bf16[512,1024]{1,0:T(8,128)(2,1)}, u32[]{:S(2)}, u32[]{:S(2)}) collective-permute-start(bf16[512,1024]{1,0:T(8,128)(2,1)} %get-tuple-element.76), channel_id=1, source_target_pairs={{0,3},{1,2},{2,1},{3,0},{4,7},{5,6},{6,5},{7,4},{8,11},{9,10},{10,... | collective-permute-start | bytes 3145736 | tf_op jit(solution)/shard_map/ppermute | solution.py:39
  237.7 63.1 %collective-permute-start.13 = (bf16[512,512]{1,0:T(8,128)(2,1)}, bf16[512,512]{1,0:T(8,128)(2,1)S(1)}, u32[]{:S(2)}, u32[]{:S(2)}) collective-permute-start(bf16[512,512]{1,0:T(8,128)(2,1)} %get-tuple-element.73), channel_id=1, source_target_pairs={{0,2},{1,3},{2,0},{3,1},{4,6},{5,7},{6,4},{7,5},{8,10},{9,11},{10,... | collective-permute-start | bytes 1572872 | tf_op jit(solution)/shard_map/ppermute | solution.py:39
  237.9 66.5 %collective-permute-start.12 = (bf16[512,512]{1,0:T(8,128)(2,1)}, bf16[512,512]{1,0:T(8,128)(2,1)S(1)}, u32[]{:S(2)}, u32[]{:S(2)}) collective-permute-start(bf16[512,512]{1,0:T(8,128)(2,1)} %get-tuple-element.72), channel_id=1, source_target_pairs={{0,3},{1,2},{2,1},{3,0},{4,7},{5,6},{6,5},{7,4},{8,11},{9,10},{10,... | collective-permute-start | bytes 1572872 | tf_op jit(solution)/shard_map/ppermute | solution.py:39
  283.6 4.6 %collective-permute-start.18 = (f32[1,1024]{1,0:T(1,128)S(1)}, f32[1,1024]{1,0:T(1,128)S(1)}, u32[]{:S(2)}, u32[]{:S(2)}) collective-permute-start(f32[1,1024]{1,0:T(1,128)S(1)} %shard_map.80), channel_id=1, source_target_pairs={{0,12},{4,8},{8,4},{12,0},{16,28},{20,24},{24,20},{28,16},{1,13},{... | collective-permute-start | bytes 12296 | tf_op jit(solution)/shard_map/ppermute | solution.py:39
  286.2 3.6 %collective-permute-start.17 = (f32[1,1024]{1,0:T(1,128)S(1)}, f32[1,1024]{1,0:T(1,128)S(1)}, u32[]{:S(2)}, u32[]{:S(2)}) collective-permute-start(f32[1,1024]{1,0:T(1,128)S(1)} %shard_map.80), channel_id=1, source_target_pairs={{0,8},{4,12},{8,0},{12,4},{16,24},{20,28},{24,16},{28,20},{1,9},{5... | collective-permute-start | bytes 12296 | tf_op jit(solution)/shard_map/ppermute | solution.py:39
  286.6 3.6 %collective-permute-start.16 = (f32[1,1024]{1,0:T(1,128)S(1)}, f32[1,1024]{1,0:T(1,128)S(1)}, u32[]{:S(2)}, u32[]{:S(2)}) collective-permute-start(f32[1,1024]{1,0:T(1,128)S(1)} %shard_map.80), channel_id=1, source_target_pairs={{0,4},{4,0},{8,12},{12,8},{16,20},{20,16},{24,28},{28,24},{1,5},{5... | collective-permute-start | bytes 12296 | tf_op jit(solution)/shard_map/ppermute | solution.py:39
  290.3 4.6 %collective-permute-start.19 = (f32[1,1024]{1,0:T(1,128)S(1)}, f32[1,1024]{1,0:T(1,128)S(1)}, u32[]{:S(2)}, u32[]{:S(2)}) collective-permute-start(f32[1,1024]{1,0:T(1,128)S(1)} %add_add_fusion), channel_id=1, source_target_pairs={{0,16},{4,20},{8,24},{12,28},{16,0},{20,4},{24,8},{28,12},{1,17},{... | collective-permute-start | bytes 12296 | tf_op jit(solution)/shard_map/ppermute | solution.py:39

commit v2 on v1

--- a/solution.py
+++ b/solution.py
@@ -190,11 +190,12 @@
     return total
 
 
-def squares_kernel(tp, me_ref, *refs):
-    pieces, extras, right_ref, out_ref = refs[:tp], refs[tp : 2 * tp], refs[-2], refs[-1]
+def squares_kernel(number, me_ref, *refs):
+    pieces, extras, right_ref, out_ref = refs[:number], refs[number : 2 * number], refs[2 * number], refs[-1]
     right = right_ref[...]
     total = sum(squares_of(piece, extra, right) for piece, extra in zip(pieces, extras))
-    out_ref[...] = jnp.sum(total, axis=0, keepdims=True)
+    total = jnp.sum(total, axis=0, keepdims=True)
+    out_ref[...] = total + refs[-2][...] if len(refs) > 2 * number + 2 else total
 
 
 def sender_squares_kernel(tp, me_ref, *refs):
@@ -225,25 +226,33 @@
     )(sums)
 
 
-def column_squares(me, base, near, received, extras, right, unit, first, count):
+def piece_specs(tp, rows, unit, groups, first):
+    specs = [group_spec(rows, unit, groups, first), near_spec(rows, unit, first)]
+    return specs + [chunk_spec(rows, unit)] * (tp - 2)
+
+
+def column_squares(me, base, near, received, extras, right, ds, unit, first, count, previous=None):
     rows = base.shape[0]
     rank, cols = right.shape
-    tp = len(extras)
+    pieces = [base, near, *received]
+    specs = piece_specs(len(extras), rows, unit, cols // unit, first)
+    in_specs = [specs[d] for d in ds] + [left_spec(rank, max(rows, BLOCK))] * len(ds) + [chunk_spec(rank, unit, first)]
+    args = [pieces[d] for d in ds] + [extras[d] for d in ds] + [right]
+    if previous is not None:
+        in_specs.append(chunk_spec(1, unit))
+        args.append(previous)
     return pl.pallas_call(
-        functools.partial(squares_kernel, tp),
+        functools.partial(squares_kernel, len(ds)),
         out_shape=jax.ShapeDtypeStruct((1, count * unit), jnp.float32),
         grid_spec=pltpu.PrefetchScalarGridSpec(
             num_scalar_prefetch=1,
             grid=(count,),
-            in_specs=[group_spec(rows, unit, cols // unit, first), near_spec(rows, unit, first)]
-            + [chunk_spec(rows, unit)] * (tp - 2)
-            + [left_spec(rank, max(rows, BLOCK))] * tp
-            + [chunk_spec(rank, unit, first)],
+            in_specs=in_specs,
             out_specs=chunk_spec(1, unit),
         ),
         compiler_params=PARAMS,
-        cost_estimate=cost(tp * rows, count * unit, rank, 1),
-    )(me, base, near, *received, *extras, right)
+        cost_estimate=cost(len(ds) * rows, count * unit, rank, 1),
+    )(me, *args)
 
 
 def sender_squares(me, base, extras, rank, unit, first, count, lane):
@@ -321,10 +330,9 @@
         jax.ShapeDtypeStruct((tp * rows // BLOCK, cols // BLOCK), jnp.float32),
     )
     pieces = [base, near, *received]
-    piece_specs = [group_spec(rows, unit, groups, first), near_spec(rows, unit, first)]
-    piece_specs += [chunk_spec(rows, unit)] * (tp - 2)
+    specs = piece_specs(tp, rows, unit, groups, first)
     in_specs = (
-        [piece_specs[d] for d in ds]
+        [specs[d] for d in ds]
         + [left_spec(rank, max(rows, BLOCK))] * len(ds)
         + [chunk_spec(rank, unit, first), chunk_spec(1, unit), group_spec(1, unit, groups, first)]
     )
@@ -399,9 +407,16 @@
     for i in range(tp // 2):
         extras += [even[i], odd[i * rank : (i + 1) * rank]]
 
+    apart = rows % BLOCK == 0 and len(chunks) == early + 1
+    every = tuple(range(tp))
     result = None
     token = ()
     totals = {}
+
+    def export(k, ds):
+        nonlocal result
+        result = export_chunk(me, base, near, received.get(k, ()), extras, right, totals[k], mag, ds, *units(k), result)
+
     for k in range(len(chunks)):
         following = k + AHEAD
         if following < len(chunks):
@@ -417,7 +432,13 @@
             else:
                 send(following, pack(turn, base, tp, far, *span(following)))
         if k < early:
-            local = column_squares(after(me, *token), base, near, received[k], extras, right, *units(k))
+            if apart and k == early - 1:
+                export(early, every[:2])
+                token = (result[1],)
+            turn = after(me, *token)
+            local = None
+            for ds in (every[:-1], every[-1:]) if apart and k == early - 1 else (every,):
+                local = column_squares(turn, base, near, received[k], extras, right, ds, *units(k), local)
             if k == CARRIER:
                 for piece in received[k][::2]:
                     parts = after(piece, *token)[rows : rows + TERMS, : late_sums.shape[1]].astype(jnp.float32)
@@ -429,9 +450,11 @@
                 for i in range(early, len(chunks)):
                     start = span(k)[1] + span(i)[0] - late[0] * BLOCK
                     totals[i] = total[:, start : start + span(i)[1]]
-        split = k == len(chunks) - 1 and rows % BLOCK == 0 and tp > 2
-        for ds in (tuple(range(tp - 1)), (tp - 1,)) if split else (tuple(range(tp)),):
-            result = export_chunk(me, base, near, received[k], extras, right, totals[k], mag, ds, *units(k), result)
+        if apart and k == early:
+            for d in far:
+                export(k, (d,))
+        else:
+            export(k, every)
         token = (result[1],)
     return result
 

time: 307 us -> 304 us (level)
  waiting for transfers between devices: 70.8 us -> 64.6 us
    ppermute x20, waiting for transfers between devices: 67.3 us -> 61.6 us  [swap(): return lax.ppermute(array, axis, [(i, i ^ d) for i in range(size)])]
    pallas_call x6 -> x7, Pallas kernels: 18.8 us -> 20.1 us  [column_squares(): pl.pallas_call(functools.partial(squares_kernel, len(ds)), out_shape=jax....]
    pallas_call x8 -> x9, Pallas kernels: 40.5 us -> 41.4 us  [export_chunk(): pl.pallas_call(functools.partial(export_kernel, tp, ds, first), out_shape...]
  transfers between devices with their start and end apart: 21 -> 21, of which waited for: 13 -> 14; matrix products, arithmetic and copies ran while one was open for 0% -> 1% of each run, Pallas kernels for 29% -> 30%
where the time goes in v2:
time: 304 us; the launch traced here: 303 us
  blocking collectives  110 us (36%)
  Pallas kernels  93.7 us (31%)
  waiting for transfers between devices  64.6 us (21%)
  starting transfers between devices  30.6 us (10%)
    psum x5, blocking collectives, body(): lax.psum(local, 'fsdp')  110 us
    ppermute x20, waiting for transfers between devices, swap(): return lax.ppermute(array, axis, [(i, i ^ d) for i in range(size)])  61.6 us
    pallas_call x9, Pallas kernels, export_chunk(): pl.pallas_call(functools.partial(export_kernel, tp, ds, first), out_shape...  41.4 us
    pallas_call x9, Pallas kernels, move(): pl.pallas_call(functools.partial(move_kernel, moves, len(arrays)), out_sh...  29.8 us
    ppermute x20, starting transfers between devices, swap(): return lax.ppermute(array, axis, [(i, i ^ d) for i in range(size)])  21.7 us
    pallas_call x7, Pallas kernels, column_squares(): pl.pallas_call(functools.partial(squares_kernel, len(ds)), out_shape=jax....  20.1 us
    all_to_all x1, starting transfers between devices, body(): lax.all_to_all(pack_near(after(me, *pieces), base, tp), 'tp', 0, 0, tiled...  8.88 us
  transfers between devices with their start and end apart: 21, of which 14 were waited for; matrix products, arithmetic and copies ran while one was open for 1% of the time, Pallas kernels for 30%

profile of v2, /device:TPU:0, one launch (start us, length us, event | category | flops | bytes accessed | tf_op | source)
XLA Modules:
  0.0 303.1 jit_solution(9275123467760511487)
XLA Ops:
  2.9 3.0 collective-permute-start
  12.6 20.3 %collective-permute-done.refs_2_ = bf16[576,1024]{1,0:T(8,128)(2,1)S(1)} collective-permute-done((bf16[576,1024]{1,0:T(8,128)(2,1)}, bf16[576,1024]{1,0:T(8,128)(2,1)S(1)}, u32[]{:S(2)}, u32[]{:S(2)}) %collective-permute-start) | collective-permute-done | bytes 1179680 | tf_op jit(solution)/shard_map/ppermute | solution.py:39
  33.7 9.8 %shard_map.63 = bf16[1024,6656]{1,0:T(8,128)(2,1)} custom-call(s32[1]{0:T(128)} %bitcast.me_ref, bf16[512,26624]{1,0:T(8,128)(2,1)} %refs_0_.45), custom_call_target="tpu_custom_call" | custom-call | bytes 9087658 | tf_op jit(solution)/shard_map/pallas_call | solution.py:73
  43.5 8.9 %all-to-all-start = ((bf16[2,512,6656]{2,1,0:T(8,128)(2,1)}), bf16[2,512,6656]{2,1,0:T(8,128)(2,1)}, u32[]{:S(2)}, u32[]{:S(2)}) async-start(bf16[2,512,6656]{2,1,0:T(8,128)(2,1)} %bitcast.15), calls=%async_computation | async-start | bytes 27262976 | tf_op jit(solution)/shard_map/all_to_all | solution.py:399
  52.4 2.6 collective-permute-done.1.refs_3_
  60.7 3.0 all-to-all-done
  63.7 3.1 %shard_map.64 = f32[1,1024]{1,0:T(1,128)S(1)} custom-call(s32[1]{0:T(128)} %bitcast.me_ref, bf16[512,26624]{1,0:T(8,128)(2,1)} %refs_0_.45, bf16[1024,6656]{1,0:T(8,128)(2,1)} %bitcast.3.refs_1_, bf16[576,1024]{1,0:T(8,128)(2,1)} %copy-done.4, bf16[512,1024]{1,0:T(8,128)(2,1)} %collective-permute-done.1.refs_3_, bf16[64,1024]{1,0:T(8,128)(2,1)S(1)} %copy-done.1, ...), custom_call_target="tpu_custom_call" | custom-call | flops 89478488 | bytes 1398101 | tf_op jit(solution)/shard_map/pallas_call | solution.py:244
  66.8 22.3 %psum.35.refs_9_ = f32[1,1024]{1,0:T(1,128)S(1)} all-reduce(f32[1,1024]{1,0:T(1,128)S(1)} %shard_map.64), channel_id=1, replica_groups=mesh['fsdp'=8,'tp'=4] {'fsdp'}, use_global_device_ids=true, to_apply=%region_0.1 | all-reduce | flops 1024 | bytes 8192 | tf_op jit(solution)/shard_map/psum | solution.py:447
  89.1 5.8 %shard_map.65 = (bf16[2048,6656]{1,0:T(8,128)(2,1)}, f32[16,52]{1,0:T(8,128)S(1)}) custom-call(s32[1]{0:T(128)} %bitcast.me_ref, bf16[512,26624]{1,0:T(8,128)(2,1)} %refs_0_.45, bf16[1024,6656]{1,0:T(8,128)(2,1)} %bitcast.3.refs_1_, bf16[576,1024]{1,0:T(8,128)(2,1)} %copy-done.4, bf16[512,1024]{1,0:T(8,128)(2,1)} %collective-permute-done.1.refs_3_, ...), custom_call_target="tpu_custom_call" | custom-call | flops 89478488 | bytes 2796202 | tf_op jit(solution)/shard_map/pallas_call | solution.py:349
  94.9 5.1 %collective-permute-done.5.refs_3_ = bf16[512,1024]{1,0:T(8,128)(2,1)} collective-permute-done((bf16[512,1024]{1,0:T(8,128)(2,1)}, bf16[512,1024]{1,0:T(8,128)(2,1)}, u32[]{:S(2)}, u32[]{:S(2)}) %collective-permute-start.5) | collective-permute-done | bytes 1048608 | tf_op jit(solution)/shard_map/ppermute | solution.py:39
  104.2 2.7 shard_map.71
  108.9 3.1 %shard_map.66 = f32[1,1024]{1,0:T(1,128)S(1)} custom-call(s32[1]{0:T(128)} %bitcast.me_ref, bf16[512,26624]{1,0:T(8,128)(2,1)} %refs_0_.45, bf16[1024,6656]{1,0:T(8,128)(2,1)} %bitcast.3.refs_1_, bf16[512,1024]{1,0:T(8,128)(2,1)} %copy-done.6, bf16[512,1024]{1,0:T(8,128)(2,1)} %collective-permute-done.5.refs_3_, bf16[64,1024]{1,0:T(8,128)(2,1)S(1)} %copy-done.1, ...), custom_call_target="tpu_custom_call" | custom-call | flops 89478488 | bytes 1398101 | tf_op jit(solution)/shard_map/pallas_call | solution.py:244
  112.1 21.8 %psum.36.refs_9_ = f32[1,1024]{1,0:T(1,128)S(1)} all-reduce(f32[1,1024]{1,0:T(1,128)S(1)} %shard_map.66), channel_id=1, replica_groups=mesh['fsdp'=8,'tp'=4] {'fsdp'}, use_global_device_ids=true, to_apply=%region_1.2 | all-reduce | flops 1024 | bytes 8192 | tf_op jit(solution)/shard_map/psum | solution.py:447
  133.9 5.9 %shard_map.67 = (bf16[2048,6656]{1,0:T(8,128)(2,1)}, f32[16,52]{1,0:T(8,128)S(1)}) custom-call(s32[1]{0:T(128)} %bitcast.me_ref, bf16[512,26624]{1,0:T(8,128)(2,1)} %refs_0_.45, bf16[1024,6656]{1,0:T(8,128)(2,1)} %bitcast.3.refs_1_, bf16[512,1024]{1,0:T(8,128)(2,1)} %copy-done.6, ...), custom_call_target="tpu_custom_call", output_to_operand_aliasing={{0}: (12, {})} | custom-call | flops 89478488 | bytes 2796202 | tf_op jit(solution)/shard_map/pallas_call | solution.py:349
  139.8 5.1 %collective-permute-done.3.refs_3_ = bf16[512,1024]{1,0:T(8,128)(2,1)} collective-permute-done((bf16[512,1024]{1,0:T(8,128)(2,1)}, bf16[512,1024]{1,0:T(8,128)(2,1)}, u32[]{:S(2)}, u32[]{:S(2)}) %collective-permute-start.3) | collective-permute-done | bytes 1048608 | tf_op jit(solution)/shard_map/ppermute | solution.py:39
  149.6 3.1 %shard_map.72 = f32[1,1024]{1,0:T(1,128)S(1)} custom-call(s32[1]{0:T(128)} %bitcast.me_ref, bf16[512,26624]{1,0:T(8,128)(2,1)} %refs_0_.45, bf16[1024,6656]{1,0:T(8,128)(2,1)} %bitcast.3.refs_1_, bf16[512,1024]{1,0:T(8,128)(2,1)} %collective-permute-done.2.refs_2_, bf16[512,1024]{1,0:T(8,128)(2,1)} %collective-permute-done.3.refs_3_, ...), custom_call_target="tpu_custom_call" | custom-call | flops 89478488 | bytes 1398101 | tf_op jit(solution)/shard_map/pallas_call | solution.py:244
  152.7 21.9 %psum.37.refs_9_ = f32[1,1024]{1,0:T(1,128)S(1)} all-reduce(f32[1,1024]{1,0:T(1,128)S(1)} %shard_map.72), channel_id=1, replica_groups=mesh['fsdp'=8,'tp'=4] {'fsdp'}, use_global_device_ids=true, to_apply=%region_2.3 | all-reduce | flops 1024 | bytes 8192 | tf_op jit(solution)/shard_map/psum | solution.py:447
  174.6 5.9 %shard_map.73 = (bf16[2048,6656]{1,0:T(8,128)(2,1)}, f32[16,52]{1,0:T(8,128)S(1)}) custom-call(s32[1]{0:T(128)} %bitcast.me_ref, bf16[512,26624]{1,0:T(8,128)(2,1)} %refs_0_.45, bf16[1024,6656]{1,0:T(8,128)(2,1)} %bitcast.3.refs_1_, bf16[512,1024]{1,0:T(8,128)(2,1)} %collective-permute-done.2.refs_2_, ...), custom_call_target="tpu_custom_call", output_to_operand_aliasing={{0}: (12, {})} | custom-call | flops 89478488 | bytes 2796202 | tf_op jit(solution)/shard_map/pallas_call | solution.py:349
  180.5 10.0 %collective-permute-done.11.refs_3_ = bf16[512,1024]{1,0:T(8,128)(2,1)} collective-permute-done((bf16[512,1024]{1,0:T(8,128)(2,1)}, bf16[512,1024]{1,0:T(8,128)(2,1)}, u32[]{:S(2)}, u32[]{:S(2)}) %collective-permute-start.11) | collective-permute-done | bytes 1048608 | tf_op jit(solution)/shard_map/ppermute | solution.py:39
  190.6 3.0 shard_map.77
  195.7 3.1 %shard_map.74 = f32[1,1024]{1,0:T(1,128)S(1)} custom-call(s32[1]{0:T(128)} %bitcast.me_ref, bf16[512,26624]{1,0:T(8,128)(2,1)} %refs_0_.45, bf16[1024,6656]{1,0:T(8,128)(2,1)} %bitcast.3.refs_1_, bf16[528,1024]{1,0:T(8,128)(2,1)} %copy-done.5, bf16[512,1024]{1,0:T(8,128)(2,1)} %collective-permute-done.11.refs_3_, bf16[64,1024]{1,0:T(8,128)(2,1)S(1)} %copy-done.1, ...), custom_call_target="tpu_custom_call" | custom-call | flops 89478488 | bytes 1398101 | tf_op jit(solution)/shard_map/pallas_call | solution.py:244
  199.5 22.3 %psum.38 = f32[1,1536]{1,0:T(1,128)S(1)} all-reduce(f32[1,1536]{1,0:T(1,128)S(1)} %pad_maximum_fusion.1), channel_id=1, replica_groups=mesh['fsdp'=8,'tp'=4] {'fsdp'}, use_global_device_ids=true, to_apply=%region_4.5 | all-reduce | flops 1536 | bytes 12288 | tf_op jit(solution)/shard_map/psum | solution.py:447
  221.8 5.9 %shard_map.75 = (bf16[2048,6656]{1,0:T(8,128)(2,1)}, f32[16,52]{1,0:T(8,128)S(1)}) custom-call(s32[1]{0:T(128)} %bitcast.me_ref, bf16[512,26624]{1,0:T(8,128)(2,1)} %refs_0_.45, bf16[1024,6656]{1,0:T(8,128)(2,1)} %bitcast.3.refs_1_, bf16[528,1024]{1,0:T(8,128)(2,1)} %copy-done.5, ...), custom_call_target="tpu_custom_call", output_to_operand_aliasing={{0}: (12, {})} | custom-call | flops 89478488 | bytes 2796202 | tf_op jit(solution)/shard_map/pallas_call | solution.py:349
  227.8 7.7 %collective-permute-done.8.refs_3_ = bf16[512,1024]{1,0:T(8,128)(2,1)} collective-permute-done((bf16[512,1024]{1,0:T(8,128)(2,1)}, bf16[512,1024]{1,0:T(8,128)(2,1)}, u32[]{:S(2)}, u32[]{:S(2)}) %collective-permute-start.8) | collective-permute-done | bytes 1048608 | tf_op jit(solution)/shard_map/ppermute | solution.py:39
  239.8 3.1 %shard_map.78 = f32[1,1024]{1,0:T(1,128)S(1)} custom-call(s32[1]{0:T(128)} %bitcast.me_ref, bf16[512,26624]{1,0:T(8,128)(2,1)} %refs_0_.45, bf16[1024,6656]{1,0:T(8,128)(2,1)} %bitcast.3.refs_1_, bf16[512,1024]{1,0:T(8,128)(2,1)} %collective-permute-done.7.refs_2_, bf16[512,1024]{1,0:T(8,128)(2,1)} %collective-permute-done.8.refs_3_, ...), custom_call_target="tpu_custom_call" | custom-call | flops 89478488 | bytes 1398101 | tf_op jit(solution)/shard_map/pallas_call | solution.py:244
  242.9 21.9 %psum.39.refs_9_ = f32[1,1024]{1,0:T(1,128)S(1)} all-reduce(f32[1,1024]{1,0:T(1,128)S(1)} %shard_map.78), channel_id=1, replica_groups=mesh['fsdp'=8,'tp'=4] {'fsdp'}, use_global_device_ids=true, to_apply=%region_5.6 | all-reduce | flops 1024 | bytes 8192 | tf_op jit(solution)/shard_map/psum | solution.py:447
  264.8 5.9 %shard_map.79 = (bf16[2048,6656]{1,0:T(8,128)(2,1)}, f32[16,52]{1,0:T(8,128)S(1)}) custom-call(s32[1]{0:T(128)} %bitcast.me_ref, bf16[512,26624]{1,0:T(8,128)(2,1)} %refs_0_.45, bf16[1024,6656]{1,0:T(8,128)(2,1)} %bitcast.3.refs_1_, bf16[512,1024]{1,0:T(8,128)(2,1)} %collective-permute-done.7.refs_2_, ...), custom_call_target="tpu_custom_call", output_to_operand_aliasing={{0}: (12, {})} | custom-call | flops 89478488 | bytes 2796202 | tf_op jit(solution)/shard_map/pallas_call | solution.py:349
  270.7 3.3 %shard_map.80 = (bf16[2048,6656]{1,0:T(8,128)(2,1)}, f32[16,52]{1,0:T(8,128)S(1)}) custom-call(s32[1]{0:T(128)} %bitcast.me_ref, bf16[512,26624]{1,0:T(8,128)(2,1)} %refs_0_.45, bf16[1024,6656]{1,0:T(8,128)(2,1)} %bitcast.3.refs_1_, bf16[64,1024]{1,0:T(8,128)(2,1)S(1)} %copy-done.1, ...), custom_call_target="tpu_custom_call", output_to_operand_aliasing={{0}: (8, {})} | custom-call | flops 22369620 | bytes 699050 | tf_op jit(solution)/shard_map/pallas_call | solution.py:349
  274.0 2.7 shard_map.81.refs_3_
  276.7 3.7 %collective-permute-done.15.refs_0_.refs_3_ = bf16[512,1024]{1,0:T(8,128)(2,1)} collective-permute-done((bf16[512,1024]{1,0:T(8,128)(2,1)}, bf16[512,1024]{1,0:T(8,128)(2,1)}, u32[]{:S(2)}, u32[]{:S(2)}) %collective-permute-start.15) | collective-permute-done | bytes 1048608 | tf_op jit(solution)/shard_map/ppermute | solution.py:39
  288.9 2.6 collective-permute-start.19
  293.5 5.9 %shard_map.83 = (bf16[2048,6656]{1,0:T(8,128)(2,1)}, f32[16,52]{1,0:T(8,128)S(1)}) custom-call(s32[1]{0:T(128)} %bitcast.me_ref, bf16[512,26624]{1,0:T(8,128)(2,1)} %refs_0_.45, bf16[1024,6656]{1,0:T(8,128)(2,1)} %bitcast.3.refs_1_, bf16[512,1024]{1,0:T(8,128)(2,1)} %collective-permute-done.14.refs_2_, ...), custom_call_target="tpu_custom_call", output_to_operand_aliasing={{0}: (12, {})} | custom-call | flops 89478488 | bytes 2796202 | tf_op jit(solution)/shard_map/pallas_call | solution.py:349
  (69 shorter events, 47.4 us)
Async XLA Ops:
  2.9 30.0 %collective-permute-start = (bf16[576,1024]{1,0:T(8,128)(2,1)}, bf16[576,1024]{1,0:T(8,128)(2,1)S(1)}, u32[]{:S(2)}, u32[]{:S(2)}) collective-permute-start(bf16[576,1024]{1,0:T(8,128)(2,1)} %get-tuple-element.46), channel_id=1, source_target_pairs={{0,2},{1,3},{2,0},{3,1},{4,6},{5,7},{6,4},{7,5},{8,10},{9,11},{10,... | collective-permute-start | bytes 3538952 | tf_op jit(solution)/shard_map/ppermute | solution.py:39
  5.9 27.0 %copy-start.1 = (bf16[64,1024]{1,0:T(8,128)(2,1)S(1)}, bf16[64,1024]{1,0:T(8,128)(2,1)}, u32[]{:S(2)}) copy-start(bf16[64,1024]{1,0:T(8,128)(2,1)} %get-tuple-element.47.refs_4_.refs_8_.refs_2_.refs_3_) | copy-start | bytes 393220
  8.0 47.0 %collective-permute-start.1 = (bf16[512,1024]{1,0:T(8,128)(2,1)}, bf16[512,1024]{1,0:T(8,128)(2,1)}, u32[]{:S(2)}, u32[]{:S(2)}) collective-permute-start(bf16[512,1024]{1,0:T(8,128)(2,1)} %shard_map.60), channel_id=1, source_target_pairs={{0,3},{1,2},{2,1},{3,0},{4,7},{5,6},{6,5},{7,4},{8,11},{9,10},{10,... | collective-permute-start | bytes 3145736 | tf_op jit(solution)/shard_map/ppermute | solution.py:39
  10.7 84.2 %collective-permute-start.4 = (bf16[512,1024]{1,0:T(8,128)(2,1)}, bf16[512,1024]{1,0:T(8,128)(2,1)S(1)}, u32[]{:S(2)}, u32[]{:S(2)}) collective-permute-start(bf16[512,1024]{1,0:T(8,128)(2,1)} %get-tuple-element.53), channel_id=1, source_target_pairs={{0,2},{1,3},{2,0},{3,1},{4,6},{5,7},{6,4},{7,5},{8,10},{9,11},{10,... | collective-permute-start | bytes 3145736 | tf_op jit(solution)/shard_map/ppermute | solution.py:39
  12.0 88.0 %collective-permute-start.5 = (bf16[512,1024]{1,0:T(8,128)(2,1)}, bf16[512,1024]{1,0:T(8,128)(2,1)}, u32[]{:S(2)}, u32[]{:S(2)}) collective-permute-start(bf16[512,1024]{1,0:T(8,128)(2,1)} %get-tuple-element.54), channel_id=1, source_target_pairs={{0,3},{1,2},{2,1},{3,0},{4,7},{5,6},{6,5},{7,4},{8,11},{9,10},{10,... | collective-permute-start | bytes 3145736 | tf_op jit(solution)/shard_map/ppermute | solution.py:39
  32.9 10.6 %copy-start.4 = (bf16[576,1024]{1,0:T(8,128)(2,1)}, bf16[576,1024]{1,0:T(8,128)(2,1)S(1)}, u32[]{:S(2)}) copy-start(bf16[576,1024]{1,0:T(8,128)(2,1)S(1)} %collective-permute-done.refs_2_) | copy-start | bytes 3538948
  33.7 26.0 %collective-permute-start.6 = (bf16[128,1024]{1,0:T(8,128)(2,1)}, bf16[128,1024]{1,0:T(8,128)(2,1)}, u32[]{:S(2)}, u32[]{:S(2)}) collective-permute-start(bf16[128,1024]{1,0:T(8,128)(2,1)} %pad_maximum_fusion), channel_id=1, source_target_pairs={{0,1},{1,0},{2,3},{3,2},{4,5},{5,4},{6,7},{7,6},{8,9},{9,8},{10,11... | collective-permute-start | bytes 786440 | tf_op jit(solution)/shard_map/ppermute | solution.py:39
  43.5 20.2 %copy-start = (bf16[64,6656]{1,0:T(8,128)(2,1)S(1)}, bf16[64,6656]{1,0:T(8,128)(2,1)}, u32[]{:S(2)}) copy-start(bf16[64,6656]{1,0:T(8,128)(2,1)} %refs_2_.9) | copy-start | bytes 2555908
  43.5 20.2 %all-to-all-start = ((bf16[2,512,6656]{2,1,0:T(8,128)(2,1)}), bf16[2,512,6656]{2,1,0:T(8,128)(2,1)}, u32[]{:S(2)}, u32[]{:S(2)}) async-start(bf16[2,512,6656]{2,1,0:T(8,128)(2,1)} %bitcast.15), calls=%async_computation | async-start | bytes 27262976 | tf_op jit(solution)/shard_map/all_to_all | solution.py:399
  57.7 31.4 %copy-start.2 = (f32[26624]{0:T(1024)S(1)}, f32[26624]{0:T(1024)}, u32[]{:S(2)}) copy-start(f32[26624]{0:T(1024)} %param.7) | copy-start | bytes 319492
  57.7 82.2 %collective-permute-start.2 = (bf16[512,1024]{1,0:T(8,128)(2,1)}, bf16[512,1024]{1,0:T(8,128)(2,1)}, u32[]{:S(2)}, u32[]{:S(2)}) collective-permute-start(bf16[512,1024]{1,0:T(8,128)(2,1)} %get-tuple-element.50), channel_id=1, source_target_pairs={{0,2},{1,3},{2,0},{3,1},{4,6},{5,7},{6,4},{7,5},{8,10},{9,11},{10,... | collective-permute-start | bytes 3145736 | tf_op jit(solution)/shard_map/ppermute | solution.py:39
  57.9 87.0 %collective-permute-start.3 = (bf16[512,1024]{1,0:T(8,128)(2,1)}, bf16[512,1024]{1,0:T(8,128)(2,1)}, u32[]{:S(2)}, u32[]{:S(2)}) collective-permute-start(bf16[512,1024]{1,0:T(8,128)(2,1)} %get-tuple-element.51), channel_id=1, source_target_pairs={{0,3},{1,2},{2,1},{3,0},{4,7},{5,6},{6,5},{7,4},{8,11},{9,10},{10,... | collective-permute-start | bytes 3145736 | tf_op jit(solution)/shard_map/ppermute | solution.py:39
  94.9 7.4 %copy-start.6 = (bf16[512,1024]{1,0:T(8,128)(2,1)}, bf16[512,1024]{1,0:T(8,128)(2,1)S(1)}, u32[]{:S(2)}) copy-start(bf16[512,1024]{1,0:T(8,128)(2,1)S(1)} %collective-permute-done.4.refs_2_) | copy-start | bytes 3145732
  102.3 1.2 collective-permute-start.9
  103.6 0.6 copy-start.3
  106.9 83.7 %collective-permute-start.10 = (bf16[528,1024]{1,0:T(8,128)(2,1)}, bf16[528,1024]{1,0:T(8,128)(2,1)S(1)}, u32[]{:S(2)}, u32[]{:S(2)}) collective-permute-start(bf16[528,1024]{1,0:T(8,128)(2,1)} %get-tuple-element.64), channel_id=1, source_target_pairs={{0,2},{1,3},{2,0},{3,1},{4,6},{5,7},{6,4},{7,5},{8,10},{9,11},{10,... | collective-permute-start | bytes 3244040 | tf_op jit(solution)/shard_map/ppermute | solution.py:39
  108.9 81.7 %collective-permute-start.11 = (bf16[512,1024]{1,0:T(8,128)(2,1)}, bf16[512,1024]{1,0:T(8,128)(2,1)}, u32[]{:S(2)}, u32[]{:S(2)}) collective-permute-start(bf16[512,1024]{1,0:T(8,128)(2,1)} %get-tuple-element.65), channel_id=1, source_target_pairs={{0,3},{1,2},{2,1},{3,0},{4,7},{5,6},{6,5},{7,4},{8,11},{9,10},{10,... | collective-permute-start | bytes 3145736 | tf_op jit(solution)/shard_map/ppermute | solution.py:39
  147.5 80.2 %collective-permute-start.7 = (bf16[512,1024]{1,0:T(8,128)(2,1)}, bf16[512,1024]{1,0:T(8,128)(2,1)}, u32[]{:S(2)}, u32[]{:S(2)}) collective-permute-start(bf16[512,1024]{1,0:T(8,128)(2,1)} %get-tuple-element.61), channel_id=1, source_target_pairs={{0,2},{1,3},{2,0},{3,1},{4,6},{5,7},{6,4},{7,5},{8,10},{9,11},{10,... | collective-permute-start | bytes 3145736 | tf_op jit(solution)/shard_map/ppermute | solution.py:39
  147.8 87.7 %collective-permute-start.8 = (bf16[512,1024]{1,0:T(8,128)(2,1)}, bf16[512,1024]{1,0:T(8,128)(2,1)}, u32[]{:S(2)}, u32[]{:S(2)}) collective-permute-start(bf16[512,1024]{1,0:T(8,128)(2,1)} %get-tuple-element.62), channel_id=1, source_target_pairs={{0,3},{1,2},{2,1},{3,0},{4,7},{5,6},{6,5},{7,4},{8,11},{9,10},{10,... | collective-permute-start | bytes 3145736 | tf_op jit(solution)/shard_map/ppermute | solution.py:39
  190.6 5.1 %copy-start.5 = (bf16[528,1024]{1,0:T(8,128)(2,1)}, bf16[528,1024]{1,0:T(8,128)(2,1)S(1)}, u32[]{:S(2)}) copy-start(bf16[528,1024]{1,0:T(8,128)(2,1)S(1)} %collective-permute-done.10.refs_2_) | copy-start | bytes 3244036
  193.6 80.4 %collective-permute-start.14 = (bf16[512,1024]{1,0:T(8,128)(2,1)}, bf16[512,1024]{1,0:T(8,128)(2,1)}, u32[]{:S(2)}, u32[]{:S(2)}) collective-permute-start(bf16[512,1024]{1,0:T(8,128)(2,1)} %get-tuple-element.77), channel_id=1, source_target_pairs={{0,2},{1,3},{2,0},{3,1},{4,6},{5,7},{6,4},{7,5},{8,10},{9,11},{10,... | collective-permute-start | bytes 3145736 | tf_op jit(solution)/shard_map/ppermute | solution.py:39
  193.9 86.6 %collective-permute-start.15 = (bf16[512,1024]{1,0:T(8,128)(2,1)}, bf16[512,1024]{1,0:T(8,128)(2,1)}, u32[]{:S(2)}, u32[]{:S(2)}) collective-permute-start(bf16[512,1024]{1,0:T(8,128)(2,1)} %get-tuple-element.78), channel_id=1, source_target_pairs={{0,3},{1,2},{2,1},{3,0},{4,7},{5,6},{6,5},{7,4},{8,11},{9,10},{10,... | collective-permute-start | bytes 3145736 | tf_op jit(solution)/shard_map/ppermute | solution.py:39
  237.7 61.7 %collective-permute-start.13 = (bf16[512,512]{1,0:T(8,128)(2,1)}, bf16[512,512]{1,0:T(8,128)(2,1)S(1)}, u32[]{:S(2)}, u32[]{:S(2)}) collective-permute-start(bf16[512,512]{1,0:T(8,128)(2,1)} %get-tuple-element.75), channel_id=1, source_target_pairs={{0,2},{1,3},{2,0},{3,1},{4,6},{5,7},{6,4},{7,5},{8,10},{9,11},{10,... | collective-permute-start | bytes 1572872 | tf_op jit(solution)/shard_map/ppermute | solution.py:39
  238.0 63.8 %collective-permute-start.12 = (bf16[512,512]{1,0:T(8,128)(2,1)}, bf16[512,512]{1,0:T(8,128)(2,1)S(1)}, u32[]{:S(2)}, u32[]{:S(2)}) collective-permute-start(bf16[512,512]{1,0:T(8,128)(2,1)} %get-tuple-element.74), channel_id=1, source_target_pairs={{0,3},{1,2},{2,1},{3,0},{4,7},{5,6},{6,5},{7,4},{8,11},{9,10},{10,... | collective-permute-start | bytes 1572872 | tf_op jit(solution)/shard_map/ppermute | solution.py:39
  282.2 4.6 %collective-permute-start.18 = (f32[1,1024]{1,0:T(1,128)S(1)}, f32[1,1024]{1,0:T(1,128)S(1)}, u32[]{:S(2)}, u32[]{:S(2)}) collective-permute-start(f32[1,1024]{1,0:T(1,128)S(1)} %shard_map.82), channel_id=1, source_target_pairs={{0,12},{4,8},{8,4},{12,0},{16,28},{20,24},{24,20},{28,16},{1,13},{... | collective-permute-start | bytes 12296 | tf_op jit(solution)/shard_map/ppermute | solution.py:39
  284.8 3.6 %collective-permute-start.17 = (f32[1,1024]{1,0:T(1,128)S(1)}, f32[1,1024]{1,0:T(1,128)S(1)}, u32[]{:S(2)}, u32[]{:S(2)}) collective-permute-start(f32[1,1024]{1,0:T(1,128)S(1)} %shard_map.82), channel_id=1, source_target_pairs={{0,8},{4,12},{8,0},{12,4},{16,24},{20,28},{24,16},{28,20},{1,9},{5... | collective-permute-start | bytes 12296 | tf_op jit(solution)/shard_map/ppermute | solution.py:39
  285.3 3.6 %collective-permute-start.16 = (f32[1,1024]{1,0:T(1,128)S(1)}, f32[1,1024]{1,0:T(1,128)S(1)}, u32[]{:S(2)}, u32[]{:S(2)}) collective-permute-start(f32[1,1024]{1,0:T(1,128)S(1)} %shard_map.82), channel_id=1, source_target_pairs={{0,4},{4,0},{8,12},{12,8},{16,20},{20,16},{24,28},{28,24},{1,5},{5... | collective-permute-start | bytes 12296 | tf_op jit(solution)/shard_map/ppermute | solution.py:39
  288.9 4.6 %collective-permute-start.19 = (f32[1,1024]{1,0:T(1,128)S(1)}, f32[1,1024]{1,0:T(1,128)S(1)}, u32[]{:S(2)}, u32[]{:S(2)}) collective-permute-start(f32[1,1024]{1,0:T(1,128)S(1)} %add_add_fusion), channel_id=1, source_target_pairs={{0,16},{4,20},{8,24},{12,28},{16,0},{20,4},{24,8},{28,12},{1,17},{... | collective-permute-start | bytes 12296 | tf_op jit(solution)/shard_map/ppermute | solution.py:39

commit v3 on v2

--- a/solution.py
+++ b/solution.py
@@ -48,37 +48,42 @@
     return array
 
 
-def move_kernel(moves, number, me_ref, *refs):
+def move_kernel(moves, number, direct, me_ref, *refs):
     plan = moves(me_ref[0])
-    sources, targets = refs[:number], refs[number : -len(plan) - 2]
-    holds, came, went = refs[-len(plan) - 2 : -2], refs[-2], refs[-1]
+    holds = () if direct else refs[-len(plan) - 2 : -2]
+    sources, targets = refs[:number], refs[number : len(refs) - len(holds) - 2]
+    came, went = refs[-2:]
     ins, outs = [], []
     for i, (source, row, col, rows, cols, target, to_row, to_col) in enumerate(plan):
         block = sources[source].at[pl.ds(row, rows), pl.ds(col, cols)]
         place = targets[target].at[pl.ds(to_row, rows), pl.ds(to_col, cols)]
-        ins.append(pltpu.make_async_copy(block, holds[i], came.at[i]))
-        outs.append(pltpu.make_async_copy(holds[i], place, went.at[i]))
+        ins.append(pltpu.make_async_copy(block, place if direct else holds[i], came.at[i]))
+        if not direct:
+            outs.append(pltpu.make_async_copy(holds[i], place, went.at[i]))
     for copy in ins:
         copy.start()
-    for copy, onward in zip(ins, outs):
+    for i, copy in enumerate(ins):
         copy.wait()
-        onward.start()
+        if not direct:
+            outs[i].start()
     for copy in outs:
         copy.wait()
 
 
-def move(me, arrays, shapes, moves):
+def move(me, arrays, shapes, moves, direct=False):
     dtype = arrays[0].dtype
     plan = moves(0)
+    kind = pltpu.VMEM if direct else jax.ShapeDtypeStruct
+    space = pltpu.VMEM if direct else pl.ANY
     return pl.pallas_call(
-        functools.partial(move_kernel, moves, len(arrays)),
-        out_shape=[jax.ShapeDtypeStruct(shape, dtype) for shape in shapes],
+        functools.partial(move_kernel, moves, len(arrays), direct),
+        out_shape=[kind(shape, dtype) for shape in shapes],
         grid_spec=pltpu.PrefetchScalarGridSpec(
             num_scalar_prefetch=1,
             grid=(1,),
             in_specs=[pl.BlockSpec(memory_space=pl.ANY)] * len(arrays),
-            out_specs=[pl.BlockSpec(memory_space=pl.ANY)] * len(shapes),
-            scratch_shapes=[pltpu.VMEM((rows, cols), dtype) for _, _, _, rows, cols, *_ in plan]
+            out_specs=[pl.BlockSpec(memory_space=space)] * len(shapes),
+            scratch_shapes=[pltpu.VMEM((rows, cols), dtype) for _, _, _, rows, cols, *_ in (() if direct else plan)]
             + [pltpu.SemaphoreType.DMA((len(plan),))] * 2,
         ),
         compiler_params=MOVE_PARAMS,
@@ -141,7 +146,7 @@
         ]
         return column_moves(me ^ d, rows, cols, group, 0, 0) + extras
 
-    return move(me, [base, left, right], [(rows + rank, cols), (rank, lane + late_cols)], moves)
+    return move(me, [base, left, right], [(rows + rank, cols), (rank, lane + late_cols)], moves, direct=True)
 
 
 def pack_carrier(me, base, tp, distances, terms, first, cols):

time: 304 us -> 303 us (level)
  no operation moved by 1% of the time
where the time goes in v3:
time: 303 us; the launch traced here: 302 us
  blocking collectives  110 us (36%)
  Pallas kernels  93 us (31%)
  waiting for transfers between devices  64.4 us (21%)
  starting transfers between devices  30.6 us (10%)
    psum x5, blocking collectives, body(): lax.psum(local, 'fsdp')  110 us
    ppermute x20, waiting for transfers between devices, swap(): return lax.ppermute(array, axis, [(i, i ^ d) for i in range(size)])  61.5 us
    pallas_call x9, Pallas kernels, export_chunk(): pl.pallas_call(functools.partial(export_kernel, tp, ds, first), out_shape...  41.4 us
    pallas_call x9, Pallas kernels, move(): pl.pallas_call(functools.partial(move_kernel, moves, len(arrays), direct)...  29.1 us
    ppermute x20, starting transfers between devices, swap(): return lax.ppermute(array, axis, [(i, i ^ d) for i in range(size)])  21.7 us
    pallas_call x7, Pallas kernels, column_squares(): pl.pallas_call(functools.partial(squares_kernel, len(ds)), out_shape=jax....  20.1 us
    all_to_all x1, starting transfers between devices, body(): lax.all_to_all(pack_near(after(me, *pieces), base, tp), 'tp', 0, 0, tiled...  8.89 us
  transfers between devices with their start and end apart: 21, of which 14 were waited for; matrix products, arithmetic and copies ran while one was open for 1% of the time, Pallas kernels for 30%

profile of v3, /device:TPU:0, one launch (start us, length us, event | category | flops | bytes accessed | tf_op | source)
XLA Modules:
  0.0 302.2 jit_solution(13621062771980974129)
XLA Ops:
  2.2 3.0 collective-permute-start
  11.9 20.1 %collective-permute-done.refs_2_ = bf16[576,1024]{1,0:T(8,128)(2,1)S(1)} collective-permute-done((bf16[576,1024]{1,0:T(8,128)(2,1)S(1)}, bf16[576,1024]{1,0:T(8,128)(2,1)S(1)}, u32[]{:S(2)}, u32[]{:S(2)}) %collective-permute-start) | collective-permute-done | bytes 1179680 | tf_op jit(solution)/shard_map/ppermute | solution.py:39
  32.8 9.8 %shard_map.63 = bf16[1024,6656]{1,0:T(8,128)(2,1)} custom-call(s32[1]{0:T(128)} %bitcast.me_ref, bf16[512,26624]{1,0:T(8,128)(2,1)} %refs_0_.45), custom_call_target="tpu_custom_call" | custom-call | bytes 9087658 | tf_op jit(solution)/shard_map/pallas_call | solution.py:78
  42.5 8.9 %all-to-all-start = ((bf16[2,512,6656]{2,1,0:T(8,128)(2,1)}), bf16[2,512,6656]{2,1,0:T(8,128)(2,1)}, u32[]{:S(2)}, u32[]{:S(2)}) async-start(bf16[2,512,6656]{2,1,0:T(8,128)(2,1)} %bitcast.15), calls=%async_computation | async-start | bytes 27262976 | tf_op jit(solution)/shard_map/all_to_all | solution.py:404
  51.4 2.7 collective-permute-done.1.refs_3_
  59.8 2.9 all-to-all-done
  62.7 3.1 %shard_map.64 = f32[1,1024]{1,0:T(1,128)S(1)} custom-call(s32[1]{0:T(128)} %bitcast.me_ref, bf16[512,26624]{1,0:T(8,128)(2,1)} %refs_0_.45, bf16[1024,6656]{1,0:T(8,128)(2,1)} %bitcast.3.refs_1_, bf16[576,1024]{1,0:T(8,128)(2,1)} %copy-done.3, bf16[512,1024]{1,0:T(8,128)(2,1)} %collective-permute-done.1.refs_3_, ...), custom_call_target="tpu_custom_call" | custom-call | flops 89478488 | bytes 1398101 | tf_op jit(solution)/shard_map/pallas_call | solution.py:249
  65.9 22.3 %psum.35.refs_9_ = f32[1,1024]{1,0:T(1,128)S(1)} all-reduce(f32[1,1024]{1,0:T(1,128)S(1)} %shard_map.64), channel_id=1, replica_groups=mesh['fsdp'=8,'tp'=4] {'fsdp'}, use_global_device_ids=true, to_apply=%region_0.1 | all-reduce | flops 1024 | bytes 8192 | tf_op jit(solution)/shard_map/psum | solution.py:452
  88.1 5.8 %shard_map.65 = (bf16[2048,6656]{1,0:T(8,128)(2,1)}, f32[16,52]{1,0:T(8,128)S(1)}) custom-call(s32[1]{0:T(128)} %bitcast.me_ref, bf16[512,26624]{1,0:T(8,128)(2,1)} %refs_0_.45, bf16[1024,6656]{1,0:T(8,128)(2,1)} %bitcast.3.refs_1_, bf16[576,1024]{1,0:T(8,128)(2,1)} %copy-done.3, bf16[512,1024]{1,0:T(8,128)(2,1)} %collective-permute-done.1.refs_3_, ...), custom_call_target="tpu_custom_call" | custom-call | flops 89478488 | bytes 2796202 | tf_op jit(solution)/shard_map/pallas_call | solution.py:354
  94.0 5.1 %collective-permute-done.5.refs_3_ = bf16[512,1024]{1,0:T(8,128)(2,1)} collective-permute-done((bf16[512,1024]{1,0:T(8,128)(2,1)}, bf16[512,1024]{1,0:T(8,128)(2,1)}, u32[]{:S(2)}, u32[]{:S(2)}) %collective-permute-start.5) | collective-permute-done | bytes 1048608 | tf_op jit(solution)/shard_map/ppermute | solution.py:39
  103.3 2.7 shard_map.71
  108.0 3.1 %shard_map.66 = f32[1,1024]{1,0:T(1,128)S(1)} custom-call(s32[1]{0:T(128)} %bitcast.me_ref, bf16[512,26624]{1,0:T(8,128)(2,1)} %refs_0_.45, bf16[1024,6656]{1,0:T(8,128)(2,1)} %bitcast.3.refs_1_, bf16[512,1024]{1,0:T(8,128)(2,1)} %copy-done.5, bf16[512,1024]{1,0:T(8,128)(2,1)} %collective-permute-done.5.refs_3_, ...), custom_call_target="tpu_custom_call" | custom-call | flops 89478488 | bytes 1398101 | tf_op jit(solution)/shard_map/pallas_call | solution.py:249
  111.1 21.8 %psum.36.refs_9_ = f32[1,1024]{1,0:T(1,128)S(1)} all-reduce(f32[1,1024]{1,0:T(1,128)S(1)} %shard_map.66), channel_id=1, replica_groups=mesh['fsdp'=8,'tp'=4] {'fsdp'}, use_global_device_ids=true, to_apply=%region_1.2 | all-reduce | flops 1024 | bytes 8192 | tf_op jit(solution)/shard_map/psum | solution.py:452
  133.0 5.9 %shard_map.67 = (bf16[2048,6656]{1,0:T(8,128)(2,1)}, f32[16,52]{1,0:T(8,128)S(1)}) custom-call(s32[1]{0:T(128)} %bitcast.me_ref, bf16[512,26624]{1,0:T(8,128)(2,1)} %refs_0_.45, bf16[1024,6656]{1,0:T(8,128)(2,1)} %bitcast.3.refs_1_, bf16[512,1024]{1,0:T(8,128)(2,1)} %copy-done.5, ...), custom_call_target="tpu_custom_call", output_to_operand_aliasing={{0}: (12, {})} | custom-call | flops 89478488 | bytes 2796202 | tf_op jit(solution)/shard_map/pallas_call | solution.py:354
  138.9 5.1 %collective-permute-done.3.refs_3_ = bf16[512,1024]{1,0:T(8,128)(2,1)} collective-permute-done((bf16[512,1024]{1,0:T(8,128)(2,1)}, bf16[512,1024]{1,0:T(8,128)(2,1)}, u32[]{:S(2)}, u32[]{:S(2)}) %collective-permute-start.3) | collective-permute-done | bytes 1048608 | tf_op jit(solution)/shard_map/ppermute | solution.py:39
  148.7 3.1 %shard_map.72 = f32[1,1024]{1,0:T(1,128)S(1)} custom-call(s32[1]{0:T(128)} %bitcast.me_ref, bf16[512,26624]{1,0:T(8,128)(2,1)} %refs_0_.45, bf16[1024,6656]{1,0:T(8,128)(2,1)} %bitcast.3.refs_1_, bf16[512,1024]{1,0:T(8,128)(2,1)} %collective-permute-done.2.refs_2_, bf16[512,1024]{1,0:T(8,128)(2,1)} %collective-permute-done.3.refs_3_, ...), custom_call_target="tpu_custom_call" | custom-call | flops 89478488 | bytes 1398101 | tf_op jit(solution)/shard_map/pallas_call | solution.py:249
  151.8 21.9 %psum.37.refs_9_ = f32[1,1024]{1,0:T(1,128)S(1)} all-reduce(f32[1,1024]{1,0:T(1,128)S(1)} %shard_map.72), channel_id=1, replica_groups=mesh['fsdp'=8,'tp'=4] {'fsdp'}, use_global_device_ids=true, to_apply=%region_2.3 | all-reduce | flops 1024 | bytes 8192 | tf_op jit(solution)/shard_map/psum | solution.py:452
  173.6 5.9 %shard_map.73 = (bf16[2048,6656]{1,0:T(8,128)(2,1)}, f32[16,52]{1,0:T(8,128)S(1)}) custom-call(s32[1]{0:T(128)} %bitcast.me_ref, bf16[512,26624]{1,0:T(8,128)(2,1)} %refs_0_.45, bf16[1024,6656]{1,0:T(8,128)(2,1)} %bitcast.3.refs_1_, bf16[512,1024]{1,0:T(8,128)(2,1)} %collective-permute-done.2.refs_2_, ...), custom_call_target="tpu_custom_call", output_to_operand_aliasing={{0}: (12, {})} | custom-call | flops 89478488 | bytes 2796202 | tf_op jit(solution)/shard_map/pallas_call | solution.py:354
  179.6 10.1 %collective-permute-done.11.refs_3_ = bf16[512,1024]{1,0:T(8,128)(2,1)} collective-permute-done((bf16[512,1024]{1,0:T(8,128)(2,1)}, bf16[512,1024]{1,0:T(8,128)(2,1)}, u32[]{:S(2)}, u32[]{:S(2)}) %collective-permute-start.11) | collective-permute-done | bytes 1048608 | tf_op jit(solution)/shard_map/ppermute | solution.py:39
  189.7 3.0 %shard_map.77 = (bf16[512,1024]{1,0:T(8,128)(2,1)}, bf16[512,1024]{1,0:T(8,128)(2,1)}) custom-call(s32[1]{0:T(128)} %bitcast.me_ref, bf16[512,26624]{1,0:T(8,128)(2,1)} %refs_0_.45), custom_call_target="tpu_custom_call" | custom-call | bytes 1398101 | tf_op jit(solution)/shard_map/pallas_call | solution.py:78
  194.7 3.1 %shard_map.74 = f32[1,1024]{1,0:T(1,128)S(1)} custom-call(s32[1]{0:T(128)} %bitcast.me_ref, bf16[512,26624]{1,0:T(8,128)(2,1)} %refs_0_.45, bf16[1024,6656]{1,0:T(8,128)(2,1)} %bitcast.3.refs_1_, bf16[528,1024]{1,0:T(8,128)(2,1)} %copy-done.4, bf16[512,1024]{1,0:T(8,128)(2,1)} %collective-permute-done.11.refs_3_, ...), custom_call_target="tpu_custom_call" | custom-call | flops 89478488 | bytes 1398101 | tf_op jit(solution)/shard_map/pallas_call | solution.py:249
  198.6 22.3 %psum.38 = f32[1,1536]{1,0:T(1,128)S(1)} all-reduce(f32[1,1536]{1,0:T(1,128)S(1)} %pad_maximum_fusion.1), channel_id=1, replica_groups=mesh['fsdp'=8,'tp'=4] {'fsdp'}, use_global_device_ids=true, to_apply=%region_4.5 | all-reduce | flops 1536 | bytes 12288 | tf_op jit(solution)/shard_map/psum | solution.py:452
  220.9 6.0 %shard_map.75 = (bf16[2048,6656]{1,0:T(8,128)(2,1)}, f32[16,52]{1,0:T(8,128)S(1)}) custom-call(s32[1]{0:T(128)} %bitcast.me_ref, bf16[512,26624]{1,0:T(8,128)(2,1)} %refs_0_.45, bf16[1024,6656]{1,0:T(8,128)(2,1)} %bitcast.3.refs_1_, bf16[528,1024]{1,0:T(8,128)(2,1)} %copy-done.4, ...), custom_call_target="tpu_custom_call", output_to_operand_aliasing={{0}: (12, {})} | custom-call | flops 89478488 | bytes 2796202 | tf_op jit(solution)/shard_map/pallas_call | solution.py:354
  226.9 7.7 %collective-permute-done.8.refs_3_ = bf16[512,1024]{1,0:T(8,128)(2,1)} collective-permute-done((bf16[512,1024]{1,0:T(8,128)(2,1)}, bf16[512,1024]{1,0:T(8,128)(2,1)}, u32[]{:S(2)}, u32[]{:S(2)}) %collective-permute-start.8) | collective-permute-done | bytes 1048608 | tf_op jit(solution)/shard_map/ppermute | solution.py:39
  238.8 3.1 %shard_map.78 = f32[1,1024]{1,0:T(1,128)S(1)} custom-call(s32[1]{0:T(128)} %bitcast.me_ref, bf16[512,26624]{1,0:T(8,128)(2,1)} %refs_0_.45, bf16[1024,6656]{1,0:T(8,128)(2,1)} %bitcast.3.refs_1_, bf16[512,1024]{1,0:T(8,128)(2,1)} %collective-permute-done.7.refs_2_, bf16[512,1024]{1,0:T(8,128)(2,1)} %collective-permute-done.8.refs_3_, ...), custom_call_target="tpu_custom_call" | custom-call | flops 89478488 | bytes 1398101 | tf_op jit(solution)/shard_map/pallas_call | solution.py:249
  242.0 21.9 %psum.39.refs_9_ = f32[1,1024]{1,0:T(1,128)S(1)} all-reduce(f32[1,1024]{1,0:T(1,128)S(1)} %shard_map.78), channel_id=1, replica_groups=mesh['fsdp'=8,'tp'=4] {'fsdp'}, use_global_device_ids=true, to_apply=%region_5.6 | all-reduce | flops 1024 | bytes 8192 | tf_op jit(solution)/shard_map/psum | solution.py:452
  263.8 5.9 %shard_map.79 = (bf16[2048,6656]{1,0:T(8,128)(2,1)}, f32[16,52]{1,0:T(8,128)S(1)}) custom-call(s32[1]{0:T(128)} %bitcast.me_ref, bf16[512,26624]{1,0:T(8,128)(2,1)} %refs_0_.45, bf16[1024,6656]{1,0:T(8,128)(2,1)} %bitcast.3.refs_1_, bf16[512,1024]{1,0:T(8,128)(2,1)} %collective-permute-done.7.refs_2_, ...), custom_call_target="tpu_custom_call", output_to_operand_aliasing={{0}: (12, {})} | custom-call | flops 89478488 | bytes 2796202 | tf_op jit(solution)/shard_map/pallas_call | solution.py:354
  269.7 3.3 %shard_map.80 = (bf16[2048,6656]{1,0:T(8,128)(2,1)}, f32[16,52]{1,0:T(8,128)S(1)}) custom-call(s32[1]{0:T(128)} %bitcast.me_ref, bf16[512,26624]{1,0:T(8,128)(2,1)} %refs_0_.45, bf16[1024,6656]{1,0:T(8,128)(2,1)} %bitcast.3.refs_1_, bf16[64,1024]{1,0:T(8,128)(2,1)S(1)} %get-tuple-element.47.refs_4_.refs_8_.refs_2_.refs_3_, ...), custom_call_target="tpu_custom_call", output_to_operand_aliasing={{0}: (8, {})} | custom-call | flops 22369620 | bytes 699050 | tf_op jit(solution)/shard_map/pallas_call | solution.py:354
  273.1 2.7 shard_map.81.refs_3_
  275.8 3.8 %collective-permute-done.15.refs_0_.refs_3_ = bf16[512,1024]{1,0:T(8,128)(2,1)} collective-permute-done((bf16[512,1024]{1,0:T(8,128)(2,1)}, bf16[512,1024]{1,0:T(8,128)(2,1)}, u32[]{:S(2)}, u32[]{:S(2)}) %collective-permute-start.15) | collective-permute-done | bytes 1048608 | tf_op jit(solution)/shard_map/ppermute | solution.py:39
  288.0 2.7 collective-permute-start.19
  292.5 5.9 %shard_map.83 = (bf16[2048,6656]{1,0:T(8,128)(2,1)}, f32[16,52]{1,0:T(8,128)S(1)}) custom-call(s32[1]{0:T(128)} %bitcast.me_ref, bf16[512,26624]{1,0:T(8,128)(2,1)} %refs_0_.45, bf16[1024,6656]{1,0:T(8,128)(2,1)} %bitcast.3.refs_1_, bf16[512,1024]{1,0:T(8,128)(2,1)} %collective-permute-done.14.refs_2_, ...), custom_call_target="tpu_custom_call", output_to_operand_aliasing={{0}: (12, {})} | custom-call | flops 89478488 | bytes 2796202 | tf_op jit(solution)/shard_map/pallas_call | solution.py:354
  (67 shorter events, 46.6 us)
Async XLA Ops:
  2.2 29.8 %collective-permute-start = (bf16[576,1024]{1,0:T(8,128)(2,1)S(1)}, bf16[576,1024]{1,0:T(8,128)(2,1)S(1)}, u32[]{:S(2)}, u32[]{:S(2)}) collective-permute-start(bf16[576,1024]{1,0:T(8,128)(2,1)S(1)} %get-tuple-element.46), channel_id=1, source_target_pairs={{0,2},{1,3},{2,0},{3,1},{4,6},{5,7},{6,4},{7,5},{8,10},{9,11},{10,... | collective-permute-start | bytes 3538952 | tf_op jit(solution)/shard_map/ppermute | solution.py:39
  7.3 46.8 %collective-permute-start.1 = (bf16[512,1024]{1,0:T(8,128)(2,1)}, bf16[512,1024]{1,0:T(8,128)(2,1)}, u32[]{:S(2)}, u32[]{:S(2)}) collective-permute-start(bf16[512,1024]{1,0:T(8,128)(2,1)} %shard_map.60), channel_id=1, source_target_pairs={{0,3},{1,2},{2,1},{3,0},{4,7},{5,6},{6,5},{7,4},{8,11},{9,10},{10,... | collective-permute-start | bytes 3145736 | tf_op jit(solution)/shard_map/ppermute | solution.py:39
  10.0 83.9 %collective-permute-start.4 = (bf16[512,1024]{1,0:T(8,128)(2,1)}, bf16[512,1024]{1,0:T(8,128)(2,1)S(1)}, u32[]{:S(2)}, u32[]{:S(2)}) collective-permute-start(bf16[512,1024]{1,0:T(8,128)(2,1)} %get-tuple-element.53), channel_id=1, source_target_pairs={{0,2},{1,3},{2,0},{3,1},{4,6},{5,7},{6,4},{7,5},{8,10},{9,11},{10,... | collective-permute-start | bytes 3145736 | tf_op jit(solution)/shard_map/ppermute | solution.py:39
  11.2 87.8 %collective-permute-start.5 = (bf16[512,1024]{1,0:T(8,128)(2,1)}, bf16[512,1024]{1,0:T(8,128)(2,1)}, u32[]{:S(2)}, u32[]{:S(2)}) collective-permute-start(bf16[512,1024]{1,0:T(8,128)(2,1)} %get-tuple-element.54), channel_id=1, source_target_pairs={{0,3},{1,2},{2,1},{3,0},{4,7},{5,6},{6,5},{7,4},{8,11},{9,10},{10,... | collective-permute-start | bytes 3145736 | tf_op jit(solution)/shard_map/ppermute | solution.py:39
  32.0 10.6 %copy-start.3 = (bf16[576,1024]{1,0:T(8,128)(2,1)}, bf16[576,1024]{1,0:T(8,128)(2,1)S(1)}, u32[]{:S(2)}) copy-start(bf16[576,1024]{1,0:T(8,128)(2,1)S(1)} %collective-permute-done.refs_2_) | copy-start | bytes 3538948
  32.8 26.1 %collective-permute-start.6 = (bf16[128,1024]{1,0:T(8,128)(2,1)}, bf16[128,1024]{1,0:T(8,128)(2,1)}, u32[]{:S(2)}, u32[]{:S(2)}) collective-permute-start(bf16[128,1024]{1,0:T(8,128)(2,1)} %pad_maximum_fusion), channel_id=1, source_target_pairs={{0,1},{1,0},{2,3},{3,2},{4,5},{5,4},{6,7},{7,6},{8,9},{9,8},{10,11... | collective-permute-start | bytes 786440 | tf_op jit(solution)/shard_map/ppermute | solution.py:39
  42.5 20.2 %copy-start = (bf16[64,6656]{1,0:T(8,128)(2,1)S(1)}, bf16[64,6656]{1,0:T(8,128)(2,1)}, u32[]{:S(2)}) copy-start(bf16[64,6656]{1,0:T(8,128)(2,1)} %refs_2_.9) | copy-start | bytes 2555908
  42.5 20.2 %all-to-all-start = ((bf16[2,512,6656]{2,1,0:T(8,128)(2,1)}), bf16[2,512,6656]{2,1,0:T(8,128)(2,1)}, u32[]{:S(2)}, u32[]{:S(2)}) async-start(bf16[2,512,6656]{2,1,0:T(8,128)(2,1)} %bitcast.15), calls=%async_computation | async-start | bytes 27262976 | tf_op jit(solution)/shard_map/all_to_all | solution.py:404
  56.7 31.4 %copy-start.1 = (f32[26624]{0:T(1024)S(1)}, f32[26624]{0:T(1024)}, u32[]{:S(2)}) copy-start(f32[26624]{0:T(1024)} %param.7) | copy-start | bytes 319492
  56.8 82.2 %collective-permute-start.2 = (bf16[512,1024]{1,0:T(8,128)(2,1)}, bf16[512,1024]{1,0:T(8,128)(2,1)}, u32[]{:S(2)}, u32[]{:S(2)}) collective-permute-start(bf16[512,1024]{1,0:T(8,128)(2,1)} %get-tuple-element.50), channel_id=1, source_target_pairs={{0,2},{1,3},{2,0},{3,1},{4,6},{5,7},{6,4},{7,5},{8,10},{9,11},{10,... | collective-permute-start | bytes 3145736 | tf_op jit(solution)/shard_map/ppermute | solution.py:39
  57.0 87.0 %collective-permute-start.3 = (bf16[512,1024]{1,0:T(8,128)(2,1)}, bf16[512,1024]{1,0:T(8,128)(2,1)}, u32[]{:S(2)}, u32[]{:S(2)}) collective-permute-start(bf16[512,1024]{1,0:T(8,128)(2,1)} %get-tuple-element.51), channel_id=1, source_target_pairs={{0,3},{1,2},{2,1},{3,0},{4,7},{5,6},{6,5},{7,4},{8,11},{9,10},{10,... | collective-permute-start | bytes 3145736 | tf_op jit(solution)/shard_map/ppermute | solution.py:39
  94.0 7.4 %copy-start.5 = (bf16[512,1024]{1,0:T(8,128)(2,1)}, bf16[512,1024]{1,0:T(8,128)(2,1)S(1)}, u32[]{:S(2)}) copy-start(bf16[512,1024]{1,0:T(8,128)(2,1)S(1)} %collective-permute-done.4.refs_2_) | copy-start | bytes 3145732
  101.4 1.2 collective-permute-start.9
  102.7 0.6 copy-start.2
  105.9 83.7 %collective-permute-start.10 = (bf16[528,1024]{1,0:T(8,128)(2,1)}, bf16[528,1024]{1,0:T(8,128)(2,1)S(1)}, u32[]{:S(2)}, u32[]{:S(2)}) collective-permute-start(bf16[528,1024]{1,0:T(8,128)(2,1)} %get-tuple-element.64), channel_id=1, source_target_pairs={{0,2},{1,3},{2,0},{3,1},{4,6},{5,7},{6,4},{7,5},{8,10},{9,11},{10,... | collective-permute-start | bytes 3244040 | tf_op jit(solution)/shard_map/ppermute | solution.py:39
  108.0 81.7 %collective-permute-start.11 = (bf16[512,1024]{1,0:T(8,128)(2,1)}, bf16[512,1024]{1,0:T(8,128)(2,1)}, u32[]{:S(2)}, u32[]{:S(2)}) collective-permute-start(bf16[512,1024]{1,0:T(8,128)(2,1)} %get-tuple-element.65), channel_id=1, source_target_pairs={{0,3},{1,2},{2,1},{3,0},{4,7},{5,6},{6,5},{7,4},{8,11},{9,10},{10,... | collective-permute-start | bytes 3145736 | tf_op jit(solution)/shard_map/ppermute | solution.py:39
  146.6 80.3 %collective-permute-start.7 = (bf16[512,1024]{1,0:T(8,128)(2,1)}, bf16[512,1024]{1,0:T(8,128)(2,1)}, u32[]{:S(2)}, u32[]{:S(2)}) collective-permute-start(bf16[512,1024]{1,0:T(8,128)(2,1)} %get-tuple-element.61), channel_id=1, source_target_pairs={{0,2},{1,3},{2,0},{3,1},{4,6},{5,7},{6,4},{7,5},{8,10},{9,11},{10,... | collective-permute-start | bytes 3145736 | tf_op jit(solution)/shard_map/ppermute | solution.py:39
  146.8 87.7 %collective-permute-start.8 = (bf16[512,1024]{1,0:T(8,128)(2,1)}, bf16[512,1024]{1,0:T(8,128)(2,1)}, u32[]{:S(2)}, u32[]{:S(2)}) collective-permute-start(bf16[512,1024]{1,0:T(8,128)(2,1)} %get-tuple-element.62), channel_id=1, source_target_pairs={{0,3},{1,2},{2,1},{3,0},{4,7},{5,6},{6,5},{7,4},{8,11},{9,10},{10,... | collective-permute-start | bytes 3145736 | tf_op jit(solution)/shard_map/ppermute | solution.py:39
  189.7 5.1 %copy-start.4 = (bf16[528,1024]{1,0:T(8,128)(2,1)}, bf16[528,1024]{1,0:T(8,128)(2,1)S(1)}, u32[]{:S(2)}) copy-start(bf16[528,1024]{1,0:T(8,128)(2,1)S(1)} %collective-permute-done.10.refs_2_) | copy-start | bytes 3244036
  192.7 80.4 %collective-permute-start.14 = (bf16[512,1024]{1,0:T(8,128)(2,1)}, bf16[512,1024]{1,0:T(8,128)(2,1)}, u32[]{:S(2)}, u32[]{:S(2)}) collective-permute-start(bf16[512,1024]{1,0:T(8,128)(2,1)} %get-tuple-element.77), channel_id=1, source_target_pairs={{0,2},{1,3},{2,0},{3,1},{4,6},{5,7},{6,4},{7,5},{8,10},{9,11},{10,... | collective-permute-start | bytes 3145736 | tf_op jit(solution)/shard_map/ppermute | solution.py:39
  192.9 86.6 %collective-permute-start.15 = (bf16[512,1024]{1,0:T(8,128)(2,1)}, bf16[512,1024]{1,0:T(8,128)(2,1)}, u32[]{:S(2)}, u32[]{:S(2)}) collective-permute-start(bf16[512,1024]{1,0:T(8,128)(2,1)} %get-tuple-element.78), channel_id=1, source_target_pairs={{0,3},{1,2},{2,1},{3,0},{4,7},{5,6},{6,5},{7,4},{8,11},{9,10},{10,... | collective-permute-start | bytes 3145736 | tf_op jit(solution)/shard_map/ppermute | solution.py:39
  236.8 61.7 %collective-permute-start.13 = (bf16[512,512]{1,0:T(8,128)(2,1)}, bf16[512,512]{1,0:T(8,128)(2,1)S(1)}, u32[]{:S(2)}, u32[]{:S(2)}) collective-permute-start(bf16[512,512]{1,0:T(8,128)(2,1)} %get-tuple-element.75), channel_id=1, source_target_pairs={{0,2},{1,3},{2,0},{3,1},{4,6},{5,7},{6,4},{7,5},{8,10},{9,11},{10,... | collective-permute-start | bytes 1572872 | tf_op jit(solution)/shard_map/ppermute | solution.py:39
  237.0 63.8 %collective-permute-start.12 = (bf16[512,512]{1,0:T(8,128)(2,1)}, bf16[512,512]{1,0:T(8,128)(2,1)S(1)}, u32[]{:S(2)}, u32[]{:S(2)}) collective-permute-start(bf16[512,512]{1,0:T(8,128)(2,1)} %get-tuple-element.74), channel_id=1, source_target_pairs={{0,3},{1,2},{2,1},{3,0},{4,7},{5,6},{6,5},{7,4},{8,11},{9,10},{10,... | collective-permute-start | bytes 1572872 | tf_op jit(solution)/shard_map/ppermute | solution.py:39
  281.3 4.6 %collective-permute-start.18 = (f32[1,1024]{1,0:T(1,128)S(1)}, f32[1,1024]{1,0:T(1,128)S(1)}, u32[]{:S(2)}, u32[]{:S(2)}) collective-permute-start(f32[1,1024]{1,0:T(1,128)S(1)} %shard_map.82), channel_id=1, source_target_pairs={{0,12},{4,8},{8,4},{12,0},{16,28},{20,24},{24,20},{28,16},{1,13},{... | collective-permute-start | bytes 12296 | tf_op jit(solution)/shard_map/ppermute | solution.py:39
  283.9 3.6 %collective-permute-start.17 = (f32[1,1024]{1,0:T(1,128)S(1)}, f32[1,1024]{1,0:T(1,128)S(1)}, u32[]{:S(2)}, u32[]{:S(2)}) collective-permute-start(f32[1,1024]{1,0:T(1,128)S(1)} %shard_map.82), channel_id=1, source_target_pairs={{0,8},{4,12},{8,0},{12,4},{16,24},{20,28},{24,16},{28,20},{1,9},{5... | collective-permute-start | bytes 12296 | tf_op jit(solution)/shard_map/ppermute | solution.py:39
  284.3 3.6 %collective-permute-start.16 = (f32[1,1024]{1,0:T(1,128)S(1)}, f32[1,1024]{1,0:T(1,128)S(1)}, u32[]{:S(2)}, u32[]{:S(2)}) collective-permute-start(f32[1,1024]{1,0:T(1,128)S(1)} %shard_map.82), channel_id=1, source_target_pairs={{0,4},{4,0},{8,12},{12,8},{16,20},{20,16},{24,28},{28,24},{1,5},{5... | collective-permute-start | bytes 12296 | tf_op jit(solution)/shard_map/ppermute | solution.py:39
  288.0 4.6 %collective-permute-start.19 = (f32[1,1024]{1,0:T(1,128)S(1)}, f32[1,1024]{1,0:T(1,128)S(1)}, u32[]{:S(2)}, u32[]{:S(2)}) collective-permute-start(f32[1,1024]{1,0:T(1,128)S(1)} %add_add_fusion), channel_id=1, source_target_pairs={{0,16},{4,20},{8,24},{12,28},{16,0},{20,4},{24,8},{28,12},{1,17},{... | collective-permute-start | bytes 12296 | tf_op jit(solution)/shard_map/ppermute | solution.py:39

commit v4 on v3

--- a/solution.py
+++ b/solution.py
@@ -13,7 +13,7 @@
 LATE = (4,)
 AHEAD = 2
 SCALE = 3
-CARRIER = 3
+CARRIER = 4
 TERMS = 3
 SUMS_ROWS = 16
 PARAMS = pltpu.CompilerParams(vmem_limit_bytes=52 * 2**20)
@@ -49,7 +49,7 @@
 
 
 def move_kernel(moves, number, direct, me_ref, *refs):
-    plan = moves(me_ref[0])
+    plan = moves(me_ref[0], me_ref[1])
     holds = () if direct else refs[-len(plan) - 2 : -2]
     sources, targets = refs[:number], refs[number : len(refs) - len(holds) - 2]
     came, went = refs[-2:]
@@ -72,7 +72,7 @@
 
 def move(me, arrays, shapes, moves, direct=False):
     dtype = arrays[0].dtype
-    plan = moves(0)
+    plan = moves(0, 0)
     kind = pltpu.VMEM if direct else jax.ShapeDtypeStruct
     space = pltpu.VMEM if direct else pl.ANY
     return pl.pallas_call(
@@ -126,7 +126,7 @@
 def pack(me, base, tp, distances, first, cols):
     rows, group = base.shape[0], base.shape[1] // tp
 
-    def moves(me):
+    def moves(me, line):
         return [m for i, d in enumerate(distances) for m in column_moves(me ^ d, rows, cols, group, first, i)]
 
     return move(me, [base], [(rows, cols)] * len(distances), moves)
@@ -136,23 +136,23 @@
     rows, group = base.shape[0], base.shape[1] // tp
     rank, lane = left.shape
     late_cols = late[1] - late[0]
-
-    def moves(me):
-        extras = [
-            (1, 0, 0, rank, lane, 0, rows, 0),
-            (1, 0, 0, rank, lane, 1, 0, 0),
-            (2, 0, late[0], rank, late_cols, 0, rows, lane),
-            (2, 0, late[0], rank, late_cols, 1, 0, lane),
-        ]
-        return column_moves(me ^ d, rows, cols, group, 0, 0) + extras
-
-    return move(me, [base, left, right], [(rows + rank, cols), (rank, lane + late_cols)], moves, direct=True)
+    half, quarter = rank // 2, rank // 4
+
+    def moves(me, line):
+        result = column_moves(me ^ d, rows, cols, group, 0, 0)
+        for i in range(2):
+            result.append((1, i * half, 0, half, lane, 0, rows, i * lane))
+            row = pl.multiple_of(line % 2 * half + i * quarter, quarter)
+            result.append((2, row, late[0], quarter, late_cols, 0, rows + half, i * late_cols))
+        return result
+
+    return move(me, [base, left, right], [(rows + half + quarter, cols)], moves, direct=True)[0]
 
 
 def pack_carrier(me, base, tp, distances, terms, first, cols):
     rows, group = base.shape[0], base.shape[1] // tp
 
-    def moves(me):
+    def moves(me, line):
         result = []
         for i, d in enumerate(distances):
             result += column_moves(me ^ d, rows, cols, group, first, i)
@@ -166,7 +166,7 @@
 def pack_near(me, base, tp):
     rows, group = base.shape[0], base.shape[1] // tp
 
-    def moves(me):
+    def moves(me, line):
         result = []
         for s in range(2):
             for source, r, col, *rest in column_moves((me // 2) * 2 + s, rows, group, group, 0, 0):
@@ -260,10 +260,11 @@
     )(me, *args)
 
 
-def sender_squares(me, base, extras, rank, unit, first, count, lane):
+def sender_squares(me, base, left, rights, unit, first, count):
     rows = base.shape[0]
-    tp = len(extras)
+    tp = len(rights)
     groups = base.shape[1] // (tp * unit)
+    rank = left.shape[0]
     return pl.pallas_call(
         functools.partial(sender_squares_kernel, tp),
         out_shape=jax.ShapeDtypeStruct((tp, count * unit), jnp.float32),
@@ -271,13 +272,13 @@
             num_scalar_prefetch=1,
             grid=(count,),
             in_specs=[group_spec(rows, unit, groups, first, d) for d in range(tp)]
-            + [chunk_spec(rank, unit, lane // unit)] * tp
-            + [left_spec(rank, lane)],
+            + [chunk_spec(rank, unit)] * tp
+            + [whole_spec(left)],
             out_specs=chunk_spec(tp, unit),
         ),
         compiler_params=PARAMS,
         cost_estimate=cost(tp * rows, count * unit, rank, 1),
-    )(me, *[base] * tp, *extras, extras[0])
+    )(me, *[base] * tp, *rights, left)
 
 
 def export_kernel(tp, ds, first, me_ref, *refs):
@@ -372,7 +373,8 @@
     blocks = cols // BLOCK
     chunks, early = chunk_blocks(blocks)
     mag = magnitude.reshape(1, -1)
-    me = lax.axis_index("tp").astype(jnp.int32).reshape(1)
+    line = lax.axis_index("fsdp").astype(jnp.int32)
+    me = jnp.stack([lax.axis_index("tp").astype(jnp.int32), line])
     lane = -(-rows // BLOCK) * BLOCK
     left = jnp.pad(left.T, ((0, 0), (0, lane - rows)))
     late = (chunks[early][0], chunks[-1][1])
@@ -394,9 +396,9 @@
     pieces = []
     for d in far:
         if d % 2 == 0:
-            piece, own = pack_first(me, base, tp, d, left, right, (late[0] * BLOCK, late[1] * BLOCK), span(0)[1])
+            piece = pack_first(me, base, tp, d, left, right, (late[0] * BLOCK, late[1] * BLOCK), span(0)[1])
         else:
-            piece = pack(after(me, own), base, tp, (d,), *span(0))[0]
+            piece = pack(after(me, *pieces), base, tp, (d,), *span(0))[0]
         pieces.append(piece)
     send(0, pieces)
     pieces = pack(after(me, *pieces), base, tp, far, *span(1))
@@ -406,11 +408,24 @@
         axis_index_groups=[[i, i + 1] for i in range(0, tp, 2)],
     )
 
-    even = [own] + [received[0][d - 2][rows:, : own.shape[1]] for d in far[::2]]
-    odd = swap(jnp.concatenate(even), 1, tp)
-    extras = []
-    for i in range(tp // 2):
-        extras += [even[i], odd[i * rank : (i + 1) * rank]]
+    def unfold(block, width):
+        return jnp.concatenate([block[:, :width], block[:, width : 2 * width]])
+
+    def alternate(even):
+        odd = swap(jnp.concatenate(even), 1, tp)
+        return [array for i, own in enumerate(even) for array in (own, odd[i * rank : (i + 1) * rank])]
+
+    arrived = [received[0][d - 2] for d in far[::2]]
+    half, late_cols = rank // 2, (late[1] - late[0]) * BLOCK
+    extras = alternate([left] + [unfold(piece[rows : rows + half], lane) for piece in arrived])
+
+    def late_rights():
+        mine = jnp.concatenate([unfold(piece[rows + half :], late_cols) for piece in arrived], axis=1)
+        other = swap(mine, 1, fsdp, "fsdp")
+        both = jnp.where(line % 2 == 0, jnp.concatenate([mine, other]), jnp.concatenate([other, mine]))
+        even = [right[:, late[0] * BLOCK : late[1] * BLOCK]]
+        even += [both[:, i * late_cols : (i + 1) * late_cols] for i in range(len(arrived))]
+        return alternate(even)
 
     apart = rows % BLOCK == 0 and len(chunks) == early + 1
     every = tuple(range(tp))
@@ -427,9 +442,9 @@
         if following < len(chunks):
             turn = after(me, *received[k], *token)
             if following == CARRIER:
-                width = width_of(late[0], late[1] - late[0], blocks, lane // BLOCK)
+                width = width_of(late[0], late[1] - late[0], blocks)
                 sums = sender_squares(
-                    turn, base, extras, rank, width * BLOCK, late[0] // width, (late[1] - late[0]) // width, lane
+                    turn, base, left, late_rights(), width * BLOCK, late[0] // width, (late[1] - late[0]) // width
                 )
                 sums = sums[0::2] + swap(sums[1::2], 1, tp)
                 late_sums = sums[:1]

time: 303 us -> 307 us (1.013)
  Pallas kernels: 93 us -> 107 us
  waiting for transfers between devices: 64.4 us -> 51.6 us
    ppermute x20 -> x22, waiting for transfers between devices: 61.5 us -> 51.6 us  [swap(): return lax.ppermute(array, axis, [(i, i ^ d) for i in range(size)])]
    pallas_call x9, Pallas kernels: 29.1 us -> 34.7 us  [move(): pl.pallas_call(functools.partial(move_kernel, moves, len(arrays), direct)...]
    pallas_call x9, Pallas kernels: 41.4 us -> 46.2 us  [export_chunk(): pl.pallas_call(functools.partial(export_kernel, tp, ds, first), out_shape...]
    ppermute x20 -> x22, starting transfers between devices: 21.7 us -> 23.6 us  [swap(): return lax.ppermute(array, axis, [(i, i ^ d) for i in range(size)])]
  transfers between devices with their start and end apart: 21 -> 23, of which waited for: 14 -> 12; matrix products, arithmetic and copies ran while one was open for 1% -> 1% of each run, Pallas kernels for 30% -> 34%
where the time goes in v4:
time: 307 us; the launch traced here: 306 us
  blocking collectives  109 us (36%)
  Pallas kernels  107 us (35%)
  waiting for transfers between devices  51.6 us (17%)
  starting transfers between devices  32.4 us (11%)
  local copies, waits for them, and re-layouts  3.13 us (1%)
    psum x5, blocking collectives, body(): lax.psum(local, 'fsdp')  109 us
    ppermute x22, waiting for transfers between devices, swap(): return lax.ppermute(array, axis, [(i, i ^ d) for i in range(size)])  51.6 us
    pallas_call x9, Pallas kernels, export_chunk(): pl.pallas_call(functools.partial(export_kernel, tp, ds, first), out_shape...  46.2 us
    pallas_call x9, Pallas kernels, move(): pl.pallas_call(functools.partial(move_kernel, moves, len(arrays), direct)...  34.7 us
    ppermute x22, starting transfers between devices, swap(): return lax.ppermute(array, axis, [(i, i ^ d) for i in range(size)])  23.6 us
    pallas_call x7, Pallas kernels, column_squares(): pl.pallas_call(functools.partial(squares_kernel, len(ds)), out_shape=jax....  23 us
    all_to_all x1, starting transfers between devices, body(): lax.all_to_all(pack_near(after(me, *pieces), base, tp), 'tp', 0, 0, tiled...  8.85 us
  transfers between devices with their start and end apart: 23, of which 12 were waited for; matrix products, arithmetic and copies ran while one was open for 1% of the time, Pallas kernels for 34%

profile of v4, /device:TPU:0, one launch (start us, length us, event | category | flops | bytes accessed | tf_op | source)
XLA Modules:
  0.0 305.7 jit_solution(6293193355246028327)
XLA Ops:
  3.4 3.0 collective-permute-start
  9.2 3.3 %shard_map.62 = (bf16[512,1024]{1,0:T(8,128)(2,1)}, bf16[512,1024]{1,0:T(8,128)(2,1)}) custom-call(s32[2]{0:T(128)} %pad_add_fusion.me_ref, bf16[512,26624]{1,0:T(8,128)(2,1)} %refs_0_.45), custom_call_target="tpu_custom_call" | custom-call | bytes 1398101 | tf_op jit(solution)/shard_map/pallas_call | solution.py:78
  14.4 10.4 %shard_map.63 = bf16[1024,6656]{1,0:T(8,128)(2,1)} custom-call(s32[2]{0:T(128)} %pad_add_fusion.me_ref, bf16[512,26624]{1,0:T(8,128)(2,1)} %refs_0_.45), custom_call_target="tpu_custom_call" | custom-call | bytes 9087658 | tf_op jit(solution)/shard_map/pallas_call | solution.py:78
  24.9 8.8 %all-to-all-start = ((bf16[2,512,6656]{2,1,0:T(8,128)(2,1)}), bf16[2,512,6656]{2,1,0:T(8,128)(2,1)}, u32[]{:S(2)}, u32[]{:S(2)}) async-start(bf16[2,512,6656]{2,1,0:T(8,128)(2,1)} %bitcast.32), calls=%async_computation | async-start | bytes 27262976 | tf_op jit(solution)/shard_map/all_to_all | solution.py:406
  33.8 20.8 %collective-permute-done.1.refs_3_ = bf16[512,1024]{1,0:T(8,128)(2,1)} collective-permute-done((bf16[512,1024]{1,0:T(8,128)(2,1)}, bf16[512,1024]{1,0:T(8,128)(2,1)}, u32[]{:S(2)}, u32[]{:S(2)}) %collective-permute-start.1) | collective-permute-done | bytes 1048608 | tf_op jit(solution)/shard_map/ppermute | solution.py:39
  56.9 3.3 %shard_map.61 = (bf16[512,1024]{1,0:T(8,128)(2,1)}, bf16[512,1024]{1,0:T(8,128)(2,1)}) custom-call(s32[2]{0:T(128)} %pad_add_fusion.me_ref, bf16[512,26624]{1,0:T(8,128)(2,1)} %refs_0_.45), custom_call_target="tpu_custom_call" | custom-call | bytes 1398101 | tf_op jit(solution)/shard_map/pallas_call | solution.py:78
  64.4 3.7 %shard_map.64 = f32[1,1024]{1,0:T(1,128)S(1)} custom-call(s32[2]{0:T(128)S(1)} %copy-done.4, bf16[512,26624]{1,0:T(8,128)(2,1)} %refs_0_.45, bf16[1024,6656]{1,0:T(8,128)(2,1)} %bitcast.4.refs_1_, bf16[560,1024]{1,0:T(8,128)(2,1)} %collective-permute-done.refs_2_, bf16[512,1024]{1,0:T(8,128)(2,1)} %collective-permute-done.1.refs_3_, ...), custom_call_target="tpu_custom_call" | custom-call | flops 89478488 | bytes 1398101 | tf_op jit(solution)/shard_map/pallas_call | solution.py:249
  68.1 20.7 %psum.35.refs_9_ = f32[1,1024]{1,0:T(1,128)S(1)} all-reduce(f32[1,1024]{1,0:T(1,128)S(1)} %shard_map.64), channel_id=1, replica_groups=mesh['fsdp'=8,'tp'=4] {'fsdp'}, use_global_device_ids=true, to_apply=%region_0.1 | all-reduce | flops 1024 | bytes 8192 | tf_op jit(solution)/shard_map/psum | solution.py:467
  88.8 6.3 %shard_map.65 = (bf16[2048,6656]{1,0:T(8,128)(2,1)}, f32[16,52]{1,0:T(8,128)S(1)}) custom-call(s32[2]{0:T(128)S(1)} %copy-done.4, bf16[512,26624]{1,0:T(8,128)(2,1)} %refs_0_.45, bf16[1024,6656]{1,0:T(8,128)(2,1)} %bitcast.4.refs_1_, bf16[560,1024]{1,0:T(8,128)(2,1)} %collective-permute-done.refs_2_, bf16[512,1024]{1,0:T(8,128)(2,1)} %collective-permute-done.1.refs_3_, ...), custom_call_target="tpu_custom_call" | custom-call | flops 89478488 | bytes 2796202 | tf_op jit(solution)/shard_map/pallas_call | solution.py:355
  95.1 4.4 %collective-permute-done.5.refs_3_ = bf16[512,1024]{1,0:T(8,128)(2,1)} collective-permute-done((bf16[512,1024]{1,0:T(8,128)(2,1)}, bf16[512,1024]{1,0:T(8,128)(2,1)}, u32[]{:S(2)}, u32[]{:S(2)}) %collective-permute-start.5) | collective-permute-done | bytes 1048608 | tf_op jit(solution)/shard_map/ppermute | solution.py:39
  99.6 3.3 %shard_map.71 = (bf16[512,1024]{1,0:T(8,128)(2,1)}, bf16[512,1024]{1,0:T(8,128)(2,1)}) custom-call(s32[2]{0:T(128)} %pad_add_fusion.me_ref, bf16[512,26624]{1,0:T(8,128)(2,1)} %refs_0_.45), custom_call_target="tpu_custom_call" | custom-call | bytes 1398101 | tf_op jit(solution)/shard_map/pallas_call | solution.py:78
  105.7 3.7 %shard_map.66 = f32[1,1024]{1,0:T(1,128)S(1)} custom-call(s32[2]{0:T(128)S(1)} %copy-done.5, bf16[512,26624]{1,0:T(8,128)(2,1)} %refs_0_.45, bf16[1024,6656]{1,0:T(8,128)(2,1)} %bitcast.4.refs_1_, bf16[512,1024]{1,0:T(8,128)(2,1)} %copy-done.10, bf16[512,1024]{1,0:T(8,128)(2,1)} %collective-permute-done.5.refs_3_, bf16[64,512]{1,0:T(8,128)(2,1)S(1)} %bitcast.11, ...), custom_call_target="tpu_custom_call" | custom-call | flops 89478488 | bytes 1398101 | tf_op jit(solution)/shard_map/pallas_call | solution.py:249
  109.4 21.7 %psum.36.refs_9_ = f32[1,1024]{1,0:T(1,128)S(1)} all-reduce(f32[1,1024]{1,0:T(1,128)S(1)} %shard_map.66), channel_id=1, replica_groups=mesh['fsdp'=8,'tp'=4] {'fsdp'}, use_global_device_ids=true, to_apply=%region_1.2 | all-reduce | flops 1024 | bytes 8192 | tf_op jit(solution)/shard_map/psum | solution.py:467
  131.1 6.5 %shard_map.67 = (bf16[2048,6656]{1,0:T(8,128)(2,1)}, f32[16,52]{1,0:T(8,128)S(1)}) custom-call(s32[2]{0:T(128)S(1)} %copy-done.5, bf16[512,26624]{1,0:T(8,128)(2,1)} %refs_0_.45, bf16[1024,6656]{1,0:T(8,128)(2,1)} %bitcast.4.refs_1_, bf16[512,1024]{1,0:T(8,128)(2,1)} %copy-done.10, ...), custom_call_target="tpu_custom_call", output_to_operand_aliasing={{0}: (12, {})} | custom-call | flops 89478488 | bytes 2796202 | tf_op jit(solution)/shard_map/pallas_call | solution.py:355
  138.5 6.0 %collective-permute-done.3.refs_3_ = bf16[512,1024]{1,0:T(8,128)(2,1)} collective-permute-done((bf16[512,1024]{1,0:T(8,128)(2,1)}, bf16[512,1024]{1,0:T(8,128)(2,1)}, u32[]{:S(2)}, u32[]{:S(2)}) %collective-permute-start.3) | collective-permute-done | bytes 1048608 | tf_op jit(solution)/shard_map/ppermute | solution.py:39
  149.3 3.3 %shard_map.70 = (bf16[528,1024]{1,0:T(8,128)(2,1)}, bf16[512,1024]{1,0:T(8,128)(2,1)}) custom-call(s32[2]{0:T(128)} %pad_add_fusion.me_ref, bf16[512,26624]{1,0:T(8,128)(2,1)} %refs_0_.45, bf16[32,512]{1,0:T(8,128)(2,1)} %copy-done.9), custom_call_target="tpu_custom_call" | custom-call | bytes 1419946 | tf_op jit(solution)/shard_map/pallas_call | solution.py:78
  154.7 3.7 %shard_map.72 = f32[1,1024]{1,0:T(1,128)S(1)} custom-call(s32[2]{0:T(128)S(1)} %copy-done.6, bf16[512,26624]{1,0:T(8,128)(2,1)} %refs_0_.45, bf16[1024,6656]{1,0:T(8,128)(2,1)} %bitcast.4.refs_1_, bf16[512,1024]{1,0:T(8,128)(2,1)} %copy-done.11, bf16[512,1024]{1,0:T(8,128)(2,1)} %collective-permute-done.3.refs_3_, bf16[64,512]{1,0:T(8,128)(2,1)S(1)} %bitcast.14, ...), custom_call_target="tpu_custom_call" | custom-call | flops 89478488 | bytes 1398101 | tf_op jit(solution)/shard_map/pallas_call | solution.py:249
  158.3 21.8 %psum.37.refs_9_ = f32[1,1024]{1,0:T(1,128)S(1)} all-reduce(f32[1,1024]{1,0:T(1,128)S(1)} %shard_map.72), channel_id=1, replica_groups=mesh['fsdp'=8,'tp'=4] {'fsdp'}, use_global_device_ids=true, to_apply=%region_2.3 | all-reduce | flops 1024 | bytes 8192 | tf_op jit(solution)/shard_map/psum | solution.py:467
  180.2 6.4 %shard_map.73 = (bf16[2048,6656]{1,0:T(8,128)(2,1)}, f32[16,52]{1,0:T(8,128)S(1)}) custom-call(s32[2]{0:T(128)S(1)} %copy-done.6, bf16[512,26624]{1,0:T(8,128)(2,1)} %refs_0_.45, bf16[1024,6656]{1,0:T(8,128)(2,1)} %bitcast.4.refs_1_, bf16[512,1024]{1,0:T(8,128)(2,1)} %copy-done.11, ...), custom_call_target="tpu_custom_call", output_to_operand_aliasing={{0}: (12, {})} | custom-call | flops 89478488 | bytes 2796202 | tf_op jit(solution)/shard_map/pallas_call | solution.py:355
  189.4 3.3 %shard_map.78 = (bf16[512,1024]{1,0:T(8,128)(2,1)}, bf16[512,1024]{1,0:T(8,128)(2,1)}) custom-call(s32[2]{0:T(128)} %pad_add_fusion.me_ref, bf16[512,26624]{1,0:T(8,128)(2,1)} %refs_0_.45), custom_call_target="tpu_custom_call" | custom-call | bytes 1398101 | tf_op jit(solution)/shard_map/pallas_call | solution.py:78
  194.8 3.7 %shard_map.74 = f32[1,1024]{1,0:T(1,128)S(1)} custom-call(s32[2]{0:T(128)S(1)} %copy-done.7, bf16[512,26624]{1,0:T(8,128)(2,1)} %refs_0_.45, bf16[1024,6656]{1,0:T(8,128)(2,1)} %bitcast.4.refs_1_, bf16[512,1024]{1,0:T(8,128)(2,1)} %collective-permute-done.12.refs_2_, bf16[512,1024]{1,0:T(8,128)(2,1)} %collective-permute-done.13.refs_3_, ...), custom_call_target="tpu_custom_call" | custom-call | flops 89478488 | bytes 1398101 | tf_op jit(solution)/shard_map/pallas_call | solution.py:249
  198.5 22.1 %psum.38.refs_9_ = f32[1,1024]{1,0:T(1,128)S(1)} all-reduce(f32[1,1024]{1,0:T(1,128)S(1)} %shard_map.74), channel_id=1, replica_groups=mesh['fsdp'=8,'tp'=4] {'fsdp'}, use_global_device_ids=true, to_apply=%region_3.4 | all-reduce | flops 1024 | bytes 8192 | tf_op jit(solution)/shard_map/psum | solution.py:467
  220.5 6.4 %shard_map.75 = (bf16[2048,6656]{1,0:T(8,128)(2,1)}, f32[16,52]{1,0:T(8,128)S(1)}) custom-call(s32[2]{0:T(128)S(1)} %copy-done.7, bf16[512,26624]{1,0:T(8,128)(2,1)} %refs_0_.45, bf16[1024,6656]{1,0:T(8,128)(2,1)} %bitcast.4.refs_1_, bf16[512,1024]{1,0:T(8,128)(2,1)} %collective-permute-done.12.refs_2_, ...), custom_call_target="tpu_custom_call", output_to_operand_aliasing={{0}: (12, {})} | custom-call | flops 89478488 | bytes 2796202 | tf_op jit(solution)/shard_map/pallas_call | solution.py:355
  227.0 8.1 %collective-permute-done.11.refs_3_ = bf16[512,1024]{1,0:T(8,128)(2,1)} collective-permute-done((bf16[512,1024]{1,0:T(8,128)(2,1)}, bf16[512,1024]{1,0:T(8,128)(2,1)}, u32[]{:S(2)}, u32[]{:S(2)}) %collective-permute-start.11) | collective-permute-done | bytes 1048608 | tf_op jit(solution)/shard_map/ppermute | solution.py:39
  235.1 2.9 shard_map.76
  240.7 3.7 %shard_map.77 = f32[1,1024]{1,0:T(1,128)S(1)} custom-call(s32[2]{0:T(128)S(1)} %copy-done.8, bf16[512,26624]{1,0:T(8,128)(2,1)} %refs_0_.45, bf16[1024,6656]{1,0:T(8,128)(2,1)} %bitcast.4.refs_1_, bf16[528,1024]{1,0:T(8,128)(2,1)} %collective-permute-done.10.refs_2_, bf16[512,1024]{1,0:T(8,128)(2,1)} %collective-permute-done.11.refs_3_, ...), custom_call_target="tpu_custom_call" | custom-call | flops 89478488 | bytes 1398101 | tf_op jit(solution)/shard_map/pallas_call | solution.py:249
  244.4 22.5 %psum.39 = f32[1,1536]{1,0:T(1,128)S(1)} all-reduce(f32[1,1536]{1,0:T(1,128)S(1)} %pad_maximum_fusion.4), channel_id=1, replica_groups=mesh['fsdp'=8,'tp'=4] {'fsdp'}, use_global_device_ids=true, to_apply=%region_5.6 | all-reduce | flops 1536 | bytes 12288 | tf_op jit(solution)/shard_map/psum | solution.py:467
  266.9 6.5 %shard_map.79 = (bf16[2048,6656]{1,0:T(8,128)(2,1)}, f32[16,52]{1,0:T(8,128)S(1)}) custom-call(s32[2]{0:T(128)S(1)} %copy-done.8, bf16[512,26624]{1,0:T(8,128)(2,1)} %refs_0_.45, bf16[1024,6656]{1,0:T(8,128)(2,1)} %bitcast.4.refs_1_, bf16[528,1024]{1,0:T(8,128)(2,1)} %collective-permute-done.10.refs_2_, ...), custom_call_target="tpu_custom_call", output_to_operand_aliasing={{0}: (12, {})} | custom-call | flops 89478488 | bytes 2796202 | tf_op jit(solution)/shard_map/pallas_call | solution.py:355
  273.3 3.9 %shard_map.80 = (bf16[2048,6656]{1,0:T(8,128)(2,1)}, f32[16,52]{1,0:T(8,128)S(1)}) custom-call(s32[2]{0:T(128)S(1)} %copy-done.8, bf16[512,26624]{1,0:T(8,128)(2,1)} %refs_0_.45, bf16[1024,6656]{1,0:T(8,128)(2,1)} %bitcast.4.refs_1_, bf16[64,512]{1,0:T(8,128)(2,1)S(1)} %bitcast.20, ...), custom_call_target="tpu_custom_call", output_to_operand_aliasing={{0}: (8, {})} | custom-call | flops 22369620 | bytes 699050 | tf_op jit(solution)/shard_map/pallas_call | solution.py:355
  277.2 3.2 %shard_map.81.refs_3_ = f32[1,1024]{1,0:T(1,128)S(1)} custom-call(s32[2]{0:T(128)S(1)} %copy-done.8, bf16[512,26624]{1,0:T(8,128)(2,1)} %refs_0_.45, bf16[1024,6656]{1,0:T(8,128)(2,1)} %bitcast.4.refs_1_, bf16[512,1024]{1,0:T(8,128)(2,1)} %collective-permute-done.16.refs_2_, bf16[64,512]{1,0:T(8,128)(2,1)S(1)} %bitcast.21, ...), custom_call_target="tpu_custom_call" | custom-call | flops 67108864 | bytes 1048576 | tf_op jit(solution)/shard_map/pallas_call | solution.py:249
  292.6 6.4 %shard_map.83 = (bf16[2048,6656]{1,0:T(8,128)(2,1)}, f32[16,52]{1,0:T(8,128)S(1)}) custom-call(s32[2]{0:T(128)S(1)} %copy-done.8, bf16[512,26624]{1,0:T(8,128)(2,1)} %refs_0_.45, bf16[1024,6656]{1,0:T(8,128)(2,1)} %bitcast.4.refs_1_, bf16[512,1024]{1,0:T(8,128)(2,1)} %collective-permute-done.16.refs_2_, ...), custom_call_target="tpu_custom_call", output_to_operand_aliasing={{0}: (12, {})} | custom-call | flops 89478488 | bytes 2796202 | tf_op jit(solution)/shard_map/pallas_call | solution.py:355
  299.1 2.9 collective-permute-done.15.refs_0_
  (91 shorter events, 47.9 us)
Async XLA Ops:
  3.4 51.3 %collective-permute-start = (bf16[560,1024]{1,0:T(8,128)(2,1)S(1)}, bf16[560,1024]{1,0:T(8,128)(2,1)}, u32[]{:S(2)}, u32[]{:S(2)}) collective-permute-start(bf16[560,1024]{1,0:T(8,128)(2,1)S(1)} %shard_map.59), channel_id=1, source_target_pairs={{0,2},{1,3},{2,0},{3,1},{4,6},{5,7},{6,4},{7,5},{8,10},{9,11},{10,... | collective-permute-start | bytes 3440648 | tf_op jit(solution)/shard_map/ppermute | solution.py:39
  9.2 45.5 %collective-permute-start.1 = (bf16[512,1024]{1,0:T(8,128)(2,1)}, bf16[512,1024]{1,0:T(8,128)(2,1)}, u32[]{:S(2)}, u32[]{:S(2)}) collective-permute-start(bf16[512,1024]{1,0:T(8,128)(2,1)} %shard_map.60), channel_id=1, source_target_pairs={{0,3},{1,2},{2,1},{3,0},{4,7},{5,6},{6,5},{7,4},{8,11},{9,10},{10,... | collective-permute-start | bytes 3145736 | tf_op jit(solution)/shard_map/ppermute | solution.py:39
  12.5 82.6 %collective-permute-start.4 = (bf16[512,1024]{1,0:T(8,128)(2,1)}, bf16[512,1024]{1,0:T(8,128)(2,1)S(1)}, u32[]{:S(2)}, u32[]{:S(2)}) collective-permute-start(bf16[512,1024]{1,0:T(8,128)(2,1)} %get-tuple-element.49), channel_id=1, source_target_pairs={{0,2},{1,3},{2,0},{3,1},{4,6},{5,7},{6,4},{7,5},{8,10},{9,11},{10,... | collective-permute-start | bytes 3145736 | tf_op jit(solution)/shard_map/ppermute | solution.py:39
  13.8 20.0 %copy-start = (bf16[64,6656]{1,0:T(8,128)(2,1)S(1)}, bf16[64,6656]{1,0:T(8,128)(2,1)}, u32[]{:S(2)}) copy-start(bf16[64,6656]{1,0:T(8,128)(2,1)} %refs_2_.9) | copy-start | bytes 2555908
  13.8 85.8 %collective-permute-start.5 = (bf16[512,1024]{1,0:T(8,128)(2,1)}, bf16[512,1024]{1,0:T(8,128)(2,1)}, u32[]{:S(2)}, u32[]{:S(2)}) collective-permute-start(bf16[512,1024]{1,0:T(8,128)(2,1)} %get-tuple-element.50), channel_id=1, source_target_pairs={{0,3},{1,2},{2,1},{3,0},{4,7},{5,6},{6,5},{7,4},{8,11},{9,10},{10,... | collective-permute-start | bytes 3145736 | tf_op jit(solution)/shard_map/ppermute | solution.py:39
  24.8 38.1 %copy-start.1 = (bf16[512,64]{0,1:T(8,128)(2,1)S(1)}, bf16[512,64]{0,1:T(8,128)(2,1)}, u32[]{:S(2)}) copy-start(bf16[512,64]{0,1:T(8,128)(2,1)} %param.5) | copy-start | bytes 196612
  24.9 39.6 %copy-start.4 = (s32[2]{0:T(128)S(1)}, s32[2]{0:T(128)}, u32[]{:S(2)}) copy-start(s32[2]{0:T(128)} %pad_add_fusion.me_ref) | copy-start | bytes 28
  24.9 39.5 %all-to-all-start = ((bf16[2,512,6656]{2,1,0:T(8,128)(2,1)}), bf16[2,512,6656]{2,1,0:T(8,128)(2,1)}, u32[]{:S(2)}, u32[]{:S(2)}) async-start(bf16[2,512,6656]{2,1,0:T(8,128)(2,1)} %bitcast.32), calls=%async_computation | async-start | bytes 27262976 | tf_op jit(solution)/shard_map/all_to_all | solution.py:406
  55.4 7.6 %collective-permute-start.7 = (bf16[32,512]{1,0:T(8,128)(2,1)S(1)}, bf16[32,512]{1,0:T(8,128)(2,1)S(1)}, u32[]{:S(2)}, u32[]{:S(2)}) collective-permute-start(bf16[32,512]{1,0:T(8,128)(2,1)S(1)} %pad_maximum_fusion.3), channel_id=1, source_target_pairs={{0,4},{4,0},{8,12},{12,8},{16,20},{20,16},{24,28},{28,24},{1,5},{5... | collective-permute-start | bytes 98312 | tf_op jit(solution)/shard_map/ppermute | solution.py:39
  60.2 28.6 %copy-start.2 = (f32[26624]{0:T(1024)S(1)}, f32[26624]{0:T(1024)}, u32[]{:S(2)}) copy-start(f32[26624]{0:T(1024)} %param.7) | copy-start | bytes 319492
  60.2 78.3 %collective-permute-start.2 = (bf16[512,1024]{1,0:T(8,128)(2,1)}, bf16[512,1024]{1,0:T(8,128)(2,1)S(1)}, u32[]{:S(2)}, u32[]{:S(2)}) collective-permute-start(bf16[512,1024]{1,0:T(8,128)(2,1)} %get-tuple-element.46), channel_id=1, source_target_pairs={{0,2},{1,3},{2,0},{3,1},{4,6},{5,7},{6,4},{7,5},{8,10},{9,11},{10,... | collective-permute-start | bytes 3145736 | tf_op jit(solution)/shard_map/ppermute | solution.py:39
  60.8 83.7 %collective-permute-start.3 = (bf16[512,1024]{1,0:T(8,128)(2,1)}, bf16[512,1024]{1,0:T(8,128)(2,1)}, u32[]{:S(2)}, u32[]{:S(2)}) collective-permute-start(bf16[512,1024]{1,0:T(8,128)(2,1)} %get-tuple-element.47), channel_id=1, source_target_pairs={{0,3},{1,2},{2,1},{3,0},{4,7},{5,6},{6,5},{7,4},{8,11},{9,10},{10,... | collective-permute-start | bytes 3145736 | tf_op jit(solution)/shard_map/ppermute | solution.py:39
  63.0 1.4 collective-permute-start.6
  88.8 16.9 %copy-start.5 = (s32[2]{0:T(128)S(1)}, s32[2]{0:T(128)}, u32[]{:S(2)}) copy-start(s32[2]{0:T(128)} %pad_add_fusion.me_ref) | copy-start | bytes 28
  95.1 10.6 %copy-start.10 = (bf16[512,1024]{1,0:T(8,128)(2,1)}, bf16[512,1024]{1,0:T(8,128)(2,1)S(1)}, u32[]{:S(2)}) copy-start(bf16[512,1024]{1,0:T(8,128)(2,1)S(1)} %collective-permute-done.4.refs_2_) | copy-start | bytes 3145732
  102.8 83.8 %collective-permute-start.12 = (bf16[512,1024]{1,0:T(8,128)(2,1)}, bf16[512,1024]{1,0:T(8,128)(2,1)}, u32[]{:S(2)}, u32[]{:S(2)}) collective-permute-start(bf16[512,1024]{1,0:T(8,128)(2,1)} %get-tuple-element.60), channel_id=1, source_target_pairs={{0,2},{1,3},{2,0},{3,1},{4,6},{5,7},{6,4},{7,5},{8,10},{9,11},{10,... | collective-permute-start | bytes 3145736 | tf_op jit(solution)/shard_map/ppermute | solution.py:39
  103.1 86.3 %collective-permute-start.13 = (bf16[512,1024]{1,0:T(8,128)(2,1)}, bf16[512,1024]{1,0:T(8,128)(2,1)}, u32[]{:S(2)}, u32[]{:S(2)}) collective-permute-start(bf16[512,1024]{1,0:T(8,128)(2,1)} %get-tuple-element.61), channel_id=1, source_target_pairs={{0,3},{1,2},{2,1},{3,0},{4,7},{5,6},{6,5},{7,4},{8,11},{9,10},{10,... | collective-permute-start | bytes 3145736 | tf_op jit(solution)/shard_map/ppermute | solution.py:39
  105.6 32.0 %collective-permute-start.8 = (bf16[128,512]{1,0:T(8,128)(2,1)}, bf16[128,512]{1,0:T(8,128)(2,1)}, u32[]{:S(2)}, u32[]{:S(2)}) collective-permute-start(bf16[128,512]{1,0:T(8,128)(2,1)} %pad_maximum_fusion.1), channel_id=1, source_target_pairs={{0,1},{1,0},{2,3},{3,2},{4,5},{5,4},{6,7},{7,6},{8,9},{9,8},{10,11... | collective-permute-start | bytes 393224 | tf_op jit(solution)/shard_map/ppermute | solution.py:39
  138.5 8.9 %copy-start.11 = (bf16[512,1024]{1,0:T(8,128)(2,1)}, bf16[512,1024]{1,0:T(8,128)(2,1)S(1)}, u32[]{:S(2)}) copy-start(bf16[512,1024]{1,0:T(8,128)(2,1)S(1)} %collective-permute-done.2.refs_2_) | copy-start | bytes 3145732
  147.4 1.2 collective-permute-start.9
  152.6 74.4 %collective-permute-start.10 = (bf16[528,1024]{1,0:T(8,128)(2,1)}, bf16[528,1024]{1,0:T(8,128)(2,1)}, u32[]{:S(2)}, u32[]{:S(2)}) collective-permute-start(bf16[528,1024]{1,0:T(8,128)(2,1)} %get-tuple-element.57), channel_id=1, source_target_pairs={{0,2},{1,3},{2,0},{3,1},{4,6},{5,7},{6,4},{7,5},{8,10},{9,11},{10,... | collective-permute-start | bytes 3244040 | tf_op jit(solution)/shard_map/ppermute | solution.py:39
  154.6 80.5 %collective-permute-start.11 = (bf16[512,1024]{1,0:T(8,128)(2,1)}, bf16[512,1024]{1,0:T(8,128)(2,1)}, u32[]{:S(2)}, u32[]{:S(2)}) collective-permute-start(bf16[512,1024]{1,0:T(8,128)(2,1)} %get-tuple-element.58), channel_id=1, source_target_pairs={{0,3},{1,2},{2,1},{3,0},{4,7},{5,6},{6,5},{7,4},{8,11},{9,10},{10,... | collective-permute-start | bytes 3145736 | tf_op jit(solution)/shard_map/ppermute | solution.py:39
  192.7 84.5 %collective-permute-start.16 = (bf16[512,1024]{1,0:T(8,128)(2,1)}, bf16[512,1024]{1,0:T(8,128)(2,1)}, u32[]{:S(2)}, u32[]{:S(2)}) collective-permute-start(bf16[512,1024]{1,0:T(8,128)(2,1)} %get-tuple-element.74), channel_id=1, source_target_pairs={{0,2},{1,3},{2,0},{3,1},{4,6},{5,7},{6,4},{7,5},{8,10},{9,11},{10,... | collective-permute-start | bytes 3145736 | tf_op jit(solution)/shard_map/ppermute | solution.py:39
  193.0 87.5 %collective-permute-start.17 = (bf16[512,1024]{1,0:T(8,128)(2,1)}, bf16[512,1024]{1,0:T(8,128)(2,1)S(1)}, u32[]{:S(2)}, u32[]{:S(2)}) collective-permute-start(bf16[512,1024]{1,0:T(8,128)(2,1)} %get-tuple-element.75), channel_id=1, source_target_pairs={{0,3},{1,2},{2,1},{3,0},{4,7},{5,6},{6,5},{7,4},{8,11},{9,10},{10,... | collective-permute-start | bytes 3145736 | tf_op jit(solution)/shard_map/ppermute | solution.py:39
  227.0 13.7 %copy-start.8 = (s32[2]{0:T(128)S(1)}, s32[2]{0:T(128)}, u32[]{:S(2)}) copy-start(s32[2]{0:T(128)} %pad_add_fusion.me_ref) | copy-start | bytes 28
  237.9 65.9 %collective-permute-start.14 = (bf16[512,512]{1,0:T(8,128)(2,1)}, bf16[512,512]{1,0:T(8,128)(2,1)S(1)}, u32[]{:S(2)}, u32[]{:S(2)}) collective-permute-start(bf16[512,512]{1,0:T(8,128)(2,1)} %get-tuple-element.69), channel_id=1, source_target_pairs={{0,3},{1,2},{2,1},{3,0},{4,7},{5,6},{6,5},{7,4},{8,11},{9,10},{10,... | collective-permute-start | bytes 1572872 | tf_op jit(solution)/shard_map/ppermute | solution.py:39
  239.9 62.1 %collective-permute-start.15 = (bf16[512,512]{1,0:T(8,128)(2,1)}, bf16[512,512]{1,0:T(8,128)(2,1)S(1)}, u32[]{:S(2)}, u32[]{:S(2)}) collective-permute-start(bf16[512,512]{1,0:T(8,128)(2,1)} %get-tuple-element.72), channel_id=1, source_target_pairs={{0,2},{1,3},{2,0},{3,1},{4,6},{5,7},{6,4},{7,5},{8,10},{9,11},{10,... | collective-permute-start | bytes 1572872 | tf_op jit(solution)/shard_map/ppermute | solution.py:39
  280.5 12.2 %copy-start.3 = (bf16[512,1024]{1,0:T(8,128)(2,1)}, bf16[512,1024]{1,0:T(8,128)(2,1)S(1)}, u32[]{:S(2)}) copy-start(bf16[512,1024]{1,0:T(8,128)(2,1)S(1)} %collective-permute-done.17.refs_0_.refs_3_) | copy-start | bytes 3145732
  281.8 4.6 %collective-permute-start.20 = (f32[1,1024]{1,0:T(1,128)S(1)}, f32[1,1024]{1,0:T(1,128)S(1)}, u32[]{:S(2)}, u32[]{:S(2)}) collective-permute-start(f32[1,1024]{1,0:T(1,128)S(1)} %shard_map.82), channel_id=1, source_target_pairs={{0,12},{4,8},{8,4},{12,0},{16,28},{20,24},{24,20},{28,16},{1,13},{... | collective-permute-start | bytes 12296 | tf_op jit(solution)/shard_map/ppermute | solution.py:39
  284.0 3.6 %collective-permute-start.19 = (f32[1,1024]{1,0:T(1,128)S(1)}, f32[1,1024]{1,0:T(1,128)S(1)}, u32[]{:S(2)}, u32[]{:S(2)}) collective-permute-start(f32[1,1024]{1,0:T(1,128)S(1)} %shard_map.82), channel_id=1, source_target_pairs={{0,8},{4,12},{8,0},{12,4},{16,24},{20,28},{24,16},{28,20},{1,9},{5... | collective-permute-start | bytes 12296 | tf_op jit(solution)/shard_map/ppermute | solution.py:39
  284.4 3.6 %collective-permute-start.18 = (f32[1,1024]{1,0:T(1,128)S(1)}, f32[1,1024]{1,0:T(1,128)S(1)}, u32[]{:S(2)}, u32[]{:S(2)}) collective-permute-start(f32[1,1024]{1,0:T(1,128)S(1)} %shard_map.82), channel_id=1, source_target_pairs={{0,4},{4,0},{8,12},{12,8},{16,20},{20,16},{24,28},{28,24},{1,5},{5... | collective-permute-start | bytes 12296 | tf_op jit(solution)/shard_map/ppermute | solution.py:39
  288.1 4.6 %collective-permute-start.21 = (f32[1,1024]{1,0:T(1,128)S(1)}, f32[1,1024]{1,0:T(1,128)S(1)}, u32[]{:S(2)}, u32[]{:S(2)}) collective-permute-start(f32[1,1024]{1,0:T(1,128)S(1)} %add_add_fusion), channel_id=1, source_target_pairs={{0,16},{4,20},{8,24},{12,28},{16,0},{20,4},{24,8},{28,12},{1,17},{... | collective-permute-start | bytes 12296 | tf_op jit(solution)/shard_map/ppermute | solution.py:39
  (3 other events, 16.1 us)

commit v5 on v4

--- a/solution.py
+++ b/solution.py
@@ -49,7 +49,7 @@
 
 
 def move_kernel(moves, number, direct, me_ref, *refs):
-    plan = moves(me_ref[0], me_ref[1])
+    plan = moves(me_ref[0])
     holds = () if direct else refs[-len(plan) - 2 : -2]
     sources, targets = refs[:number], refs[number : len(refs) - len(holds) - 2]
     came, went = refs[-2:]
@@ -72,7 +72,7 @@
 
 def move(me, arrays, shapes, moves, direct=False):
     dtype = arrays[0].dtype
-    plan = moves(0, 0)
+    plan = moves(0)
     kind = pltpu.VMEM if direct else jax.ShapeDtypeStruct
     space = pltpu.VMEM if direct else pl.ANY
     return pl.pallas_call(
@@ -126,19 +126,20 @@
 def pack(me, base, tp, distances, first, cols):
     rows, group = base.shape[0], base.shape[1] // tp
 
-    def moves(me, line):
+    def moves(me):
         return [m for i, d in enumerate(distances) for m in column_moves(me ^ d, rows, cols, group, first, i)]
 
     return move(me, [base], [(rows, cols)] * len(distances), moves)
 
 
-def pack_first(me, base, tp, d, left, right, late, cols):
+def pack_first(place, base, tp, d, left, right, late, cols):
     rows, group = base.shape[0], base.shape[1] // tp
     rank, lane = left.shape
     late_cols = late[1] - late[0]
     half, quarter = rank // 2, rank // 4
 
-    def moves(me, line):
+    def moves(place):
+        line, me = place // tp, place % tp
         result = column_moves(me ^ d, rows, cols, group, 0, 0)
         for i in range(2):
             result.append((1, i * half, 0, half, lane, 0, rows, i * lane))
@@ -146,13 +147,13 @@
             result.append((2, row, late[0], quarter, late_cols, 0, rows + half, i * late_cols))
         return result
 
-    return move(me, [base, left, right], [(rows + half + quarter, cols)], moves, direct=True)[0]
+    return move(place, [base, left, right], [(rows + half + quarter, cols)], moves, direct=True)[0]
 
 
 def pack_carrier(me, base, tp, distances, terms, first, cols):
     rows, group = base.shape[0], base.shape[1] // tp
 
-    def moves(me, line):
+    def moves(me):
         result = []
         for i, d in enumerate(distances):
             result += column_moves(me ^ d, rows, cols, group, first, i)
@@ -166,7 +167,7 @@
 def pack_near(me, base, tp):
     rows, group = base.shape[0], base.shape[1] // tp
 
-    def moves(me, line):
+    def moves(me):
         result = []
         for s in range(2):
             for source, r, col, *rest in column_moves((me // 2) * 2 + s, rows, group, group, 0, 0):
@@ -374,7 +375,8 @@
     chunks, early = chunk_blocks(blocks)
     mag = magnitude.reshape(1, -1)
     line = lax.axis_index("fsdp").astype(jnp.int32)
-    me = jnp.stack([lax.axis_index("tp").astype(jnp.int32), line])
+    me = lax.axis_index("tp").astype(jnp.int32).reshape(1)
+    place = me + tp * line
     lane = -(-rows // BLOCK) * BLOCK
     left = jnp.pad(left.T, ((0, 0), (0, lane - rows)))
     late = (chunks[early][0], chunks[-1][1])
@@ -396,7 +398,7 @@
     pieces = []
     for d in far:
         if d % 2 == 0:
-            piece = pack_first(me, base, tp, d, left, right, (late[0] * BLOCK, late[1] * BLOCK), span(0)[1])
+            piece = pack_first(place, base, tp, d, left, right, (late[0] * BLOCK, late[1] * BLOCK), span(0)[1])
         else:
             piece = pack(after(me, *pieces), base, tp, (d,), *span(0))[0]
         pieces.append(piece)
@@ -449,6 +451,11 @@
                 sums = sums[0::2] + swap(sums[1::2], 1, tp)
                 late_sums = sums[:1]
                 send(following, pack_carrier(turn, base, tp, far, terms_of(sums), *span(following)))
+            elif following == len(chunks) - 1:
+                pieces = []
+                for d in far:
+                    pieces += pack(after(turn, *pieces), base, tp, (d,), *span(following))
+                send(following, pieces)
             else:
                 send(following, pack(turn, base, tp, far, *span(following)))
         if k < early:

time: 307 us -> 302 us (0.984)
  Pallas kernels: 107 us -> 92.9 us
  waiting for transfers between devices: 51.6 us -> 62.1 us
    ppermute x22, waiting for transfers between devices: 51.6 us -> 62.1 us  [swap(): return lax.ppermute(array, axis, [(i, i ^ d) for i in range(size)])]
    pallas_call x9, Pallas kernels: 46.2 us -> 41.3 us  [export_chunk(): pl.pallas_call(functools.partial(export_kernel, tp, ds, first), out_shape...]
    pallas_call x9 -> x10, Pallas kernels: 34.7 us -> 30.1 us  [move(): pl.pallas_call(functools.partial(move_kernel, moves, len(arrays), direct)...]
    pallas_call x7, Pallas kernels: 23 us -> 19.1 us  [column_squares(): pl.pallas_call(functools.partial(squares_kernel, len(ds)), out_shape=jax....]
  transfers between devices with their start and end apart: 23 -> 23, of which waited for: 12 -> 13; matrix products, arithmetic and copies ran while one was open for 1% -> 1% of each run, Pallas kernels for 34% -> 30%
where the time goes in v5:
time: 302 us; the launch traced here: 301 us
  blocking collectives  108 us (36%)
  Pallas kernels  92.9 us (31%)
  waiting for transfers between devices  62.1 us (21%)
  starting transfers between devices  32.5 us (11%)
  local copies, waits for them, and re-layouts  3.11 us (1%)
    psum x5, blocking collectives, body(): lax.psum(local, 'fsdp')  108 us
    ppermute x22, waiting for transfers between devices, swap(): return lax.ppermute(array, axis, [(i, i ^ d) for i in range(size)])  62.1 us
    pallas_call x9, Pallas kernels, export_chunk(): pl.pallas_call(functools.partial(export_kernel, tp, ds, first), out_shape...  41.3 us
    pallas_call x10, Pallas kernels, move(): pl.pallas_call(functools.partial(move_kernel, moves, len(arrays), direct)...  30.1 us
    ppermute x22, starting transfers between devices, swap(): return lax.ppermute(array, axis, [(i, i ^ d) for i in range(size)])  23.6 us
    pallas_call x7, Pallas kernels, column_squares(): pl.pallas_call(functools.partial(squares_kernel, len(ds)), out_shape=jax....  19.1 us
    all_to_all x1, starting transfers between devices, body(): lax.all_to_all(pack_near(after(me, *pieces), base, tp), 'tp', 0, 0, tiled...  8.87 us
  transfers between devices with their start and end apart: 23, of which 13 were waited for; matrix products, arithmetic and copies ran while one was open for 1% of the time, Pallas kernels for 30%

profile of v5, /device:TPU:0, one launch (start us, length us, event | category | flops | bytes accessed | tf_op | source)
XLA Modules:
  0.0 301.5 jit_solution(6024926343659336978)
XLA Ops:
  2.2 3.0 collective-permute-start
  7.3 2.6 shard_map.62
  11.9 9.8 %shard_map.63 = bf16[1024,6656]{1,0:T(8,128)(2,1)} custom-call(s32[1]{0:T(128)} %bitcast.me_ref, bf16[512,26624]{1,0:T(8,128)(2,1)} %refs_0_.47), custom_call_target="tpu_custom_call" | custom-call | bytes 9087658 | tf_op jit(solution)/shard_map/pallas_call | solution.py:78
  21.6 8.9 %all-to-all-start = ((bf16[2,512,6656]{2,1,0:T(8,128)(2,1)}), bf16[2,512,6656]{2,1,0:T(8,128)(2,1)}, u32[]{:S(2)}, u32[]{:S(2)}) async-start(bf16[2,512,6656]{2,1,0:T(8,128)(2,1)} %bitcast.32), calls=%async_computation | async-start | bytes 27262976 | tf_op jit(solution)/shard_map/all_to_all | solution.py:408
  30.6 22.9 %collective-permute-done.1.refs_3_ = bf16[512,1024]{1,0:T(8,128)(2,1)} collective-permute-done((bf16[512,1024]{1,0:T(8,128)(2,1)}, bf16[512,1024]{1,0:T(8,128)(2,1)}, u32[]{:S(2)}, u32[]{:S(2)}) %collective-permute-start.1) | collective-permute-done | bytes 1048608 | tf_op jit(solution)/shard_map/ppermute | solution.py:39
  55.7 2.6 shard_map.61
  62.5 3.1 %shard_map.64 = f32[1,1024]{1,0:T(1,128)S(1)} custom-call(s32[1]{0:T(128)} %bitcast.me_ref, bf16[512,26624]{1,0:T(8,128)(2,1)} %refs_0_.47, bf16[1024,6656]{1,0:T(8,128)(2,1)} %bitcast.4.refs_1_, bf16[560,1024]{1,0:T(8,128)(2,1)} %collective-permute-done.refs_2_, bf16[512,1024]{1,0:T(8,128)(2,1)} %collective-permute-done.1.refs_3_, ...), custom_call_target="tpu_custom_call" | custom-call | flops 89478488 | bytes 1398101 | tf_op jit(solution)/shard_map/pallas_call | solution.py:250
  65.7 20.7 %psum.35.refs_9_ = f32[1,1024]{1,0:T(1,128)S(1)} all-reduce(f32[1,1024]{1,0:T(1,128)S(1)} %shard_map.64), channel_id=1, replica_groups=mesh['fsdp'=8,'tp'=4] {'fsdp'}, use_global_device_ids=true, to_apply=%region_0.1 | all-reduce | flops 1024 | bytes 8192 | tf_op jit(solution)/shard_map/psum | solution.py:474
  86.4 5.8 %shard_map.65 = (bf16[2048,6656]{1,0:T(8,128)(2,1)}, f32[16,52]{1,0:T(8,128)S(1)}) custom-call(s32[1]{0:T(128)} %bitcast.me_ref, bf16[512,26624]{1,0:T(8,128)(2,1)} %refs_0_.47, bf16[1024,6656]{1,0:T(8,128)(2,1)} %bitcast.4.refs_1_, bf16[560,1024]{1,0:T(8,128)(2,1)} %collective-permute-done.refs_2_, bf16[512,1024]{1,0:T(8,128)(2,1)} %collective-permute-done.1.refs_3_, ...), custom_call_target="tpu_custom_call" | custom-call | flops 89478488 | bytes 2796202 | tf_op jit(solution)/shard_map/pallas_call | solution.py:356
  92.2 6.2 %collective-permute-done.5.refs_3_ = bf16[512,1024]{1,0:T(8,128)(2,1)} collective-permute-done((bf16[512,1024]{1,0:T(8,128)(2,1)}, bf16[512,1024]{1,0:T(8,128)(2,1)}, u32[]{:S(2)}, u32[]{:S(2)}) %collective-permute-start.5) | collective-permute-done | bytes 1048608 | tf_op jit(solution)/shard_map/ppermute | solution.py:39
  98.4 2.6 shard_map.71
  103.8 3.1 %shard_map.66 = f32[1,1024]{1,0:T(1,128)S(1)} custom-call(s32[1]{0:T(128)} %bitcast.me_ref, bf16[512,26624]{1,0:T(8,128)(2,1)} %refs_0_.47, bf16[1024,6656]{1,0:T(8,128)(2,1)} %bitcast.4.refs_1_, bf16[512,1024]{1,0:T(8,128)(2,1)} %copy-done.5, bf16[512,1024]{1,0:T(8,128)(2,1)} %collective-permute-done.5.refs_3_, bf16[64,512]{1,0:T(8,128)(2,1)S(1)} %bitcast.11, ...), custom_call_target="tpu_custom_call" | custom-call | flops 89478488 | bytes 1398101 | tf_op jit(solution)/shard_map/pallas_call | solution.py:250
  106.9 21.7 %psum.36.refs_9_ = f32[1,1024]{1,0:T(1,128)S(1)} all-reduce(f32[1,1024]{1,0:T(1,128)S(1)} %shard_map.66), channel_id=1, replica_groups=mesh['fsdp'=8,'tp'=4] {'fsdp'}, use_global_device_ids=true, to_apply=%region_1.2 | all-reduce | flops 1024 | bytes 8192 | tf_op jit(solution)/shard_map/psum | solution.py:474
  128.7 5.9 %shard_map.67 = (bf16[2048,6656]{1,0:T(8,128)(2,1)}, f32[16,52]{1,0:T(8,128)S(1)}) custom-call(s32[1]{0:T(128)} %bitcast.me_ref, bf16[512,26624]{1,0:T(8,128)(2,1)} %refs_0_.47, bf16[1024,6656]{1,0:T(8,128)(2,1)} %bitcast.4.refs_1_, bf16[512,1024]{1,0:T(8,128)(2,1)} %copy-done.5, ...), custom_call_target="tpu_custom_call", output_to_operand_aliasing={{0}: (12, {})} | custom-call | flops 89478488 | bytes 2796202 | tf_op jit(solution)/shard_map/pallas_call | solution.py:356
  135.5 7.8 %collective-permute-done.3.refs_3_ = bf16[512,1024]{1,0:T(8,128)(2,1)} collective-permute-done((bf16[512,1024]{1,0:T(8,128)(2,1)}, bf16[512,1024]{1,0:T(8,128)(2,1)}, u32[]{:S(2)}, u32[]{:S(2)}) %collective-permute-start.3) | collective-permute-done | bytes 1048608 | tf_op jit(solution)/shard_map/ppermute | solution.py:39
  147.5 2.6 shard_map.70
  152.2 3.1 %shard_map.72 = f32[1,1024]{1,0:T(1,128)S(1)} custom-call(s32[1]{0:T(128)} %bitcast.me_ref, bf16[512,26624]{1,0:T(8,128)(2,1)} %refs_0_.47, bf16[1024,6656]{1,0:T(8,128)(2,1)} %bitcast.4.refs_1_, bf16[512,1024]{1,0:T(8,128)(2,1)} %copy-done.6, bf16[512,1024]{1,0:T(8,128)(2,1)} %collective-permute-done.3.refs_3_, bf16[64,512]{1,0:T(8,128)(2,1)S(1)} %bitcast.14, ...), custom_call_target="tpu_custom_call" | custom-call | flops 89478488 | bytes 1398101 | tf_op jit(solution)/shard_map/pallas_call | solution.py:250
  155.3 21.8 %psum.37.refs_9_ = f32[1,1024]{1,0:T(1,128)S(1)} all-reduce(f32[1,1024]{1,0:T(1,128)S(1)} %shard_map.72), channel_id=1, replica_groups=mesh['fsdp'=8,'tp'=4] {'fsdp'}, use_global_device_ids=true, to_apply=%region_2.3 | all-reduce | flops 1024 | bytes 8192 | tf_op jit(solution)/shard_map/psum | solution.py:474
  177.2 5.9 %shard_map.73 = (bf16[2048,6656]{1,0:T(8,128)(2,1)}, f32[16,52]{1,0:T(8,128)S(1)}) custom-call(s32[1]{0:T(128)} %bitcast.me_ref, bf16[512,26624]{1,0:T(8,128)(2,1)} %refs_0_.47, bf16[1024,6656]{1,0:T(8,128)(2,1)} %bitcast.4.refs_1_, bf16[512,1024]{1,0:T(8,128)(2,1)} %copy-done.6, ...), custom_call_target="tpu_custom_call", output_to_operand_aliasing={{0}: (12, {})} | custom-call | flops 89478488 | bytes 2796202 | tf_op jit(solution)/shard_map/pallas_call | solution.py:356
  183.1 5.2 %collective-permute-done.13.refs_3_ = bf16[512,1024]{1,0:T(8,128)(2,1)} collective-permute-done((bf16[512,1024]{1,0:T(8,128)(2,1)}, bf16[512,1024]{1,0:T(8,128)(2,1)}, u32[]{:S(2)}, u32[]{:S(2)}) %collective-permute-start.13) | collective-permute-done | bytes 1048608 | tf_op jit(solution)/shard_map/ppermute | solution.py:39
  188.2 2.6 shard_map.79
  192.9 3.1 %shard_map.74 = f32[1,1024]{1,0:T(1,128)S(1)} custom-call(s32[1]{0:T(128)} %bitcast.me_ref, bf16[512,26624]{1,0:T(8,128)(2,1)} %refs_0_.47, bf16[1024,6656]{1,0:T(8,128)(2,1)} %bitcast.4.refs_1_, bf16[512,1024]{1,0:T(8,128)(2,1)} %collective-permute-done.12.refs_2_, bf16[512,1024]{1,0:T(8,128)(2,1)} %collective-permute-done.13.refs_3_, ...), custom_call_target="tpu_custom_call" | custom-call | flops 89478488 | bytes 1398101 | tf_op jit(solution)/shard_map/pallas_call | solution.py:250
  196.0 22.0 %psum.38.refs_9_ = f32[1,1024]{1,0:T(1,128)S(1)} all-reduce(f32[1,1024]{1,0:T(1,128)S(1)} %shard_map.74), channel_id=1, replica_groups=mesh['fsdp'=8,'tp'=4] {'fsdp'}, use_global_device_ids=true, to_apply=%region_3.4 | all-reduce | flops 1024 | bytes 8192 | tf_op jit(solution)/shard_map/psum | solution.py:474
  218.0 5.9 %shard_map.75 = (bf16[2048,6656]{1,0:T(8,128)(2,1)}, f32[16,52]{1,0:T(8,128)S(1)}) custom-call(s32[1]{0:T(128)} %bitcast.me_ref, bf16[512,26624]{1,0:T(8,128)(2,1)} %refs_0_.47, bf16[1024,6656]{1,0:T(8,128)(2,1)} %bitcast.4.refs_1_, bf16[512,1024]{1,0:T(8,128)(2,1)} %collective-permute-done.12.refs_2_, ...), custom_call_target="tpu_custom_call", output_to_operand_aliasing={{0}: (12, {})} | custom-call | flops 89478488 | bytes 2796202 | tf_op jit(solution)/shard_map/pallas_call | solution.py:356
  224.0 9.9 %collective-permute-done.11.refs_3_ = bf16[512,1024]{1,0:T(8,128)(2,1)} collective-permute-done((bf16[512,1024]{1,0:T(8,128)(2,1)}, bf16[512,1024]{1,0:T(8,128)(2,1)}, u32[]{:S(2)}, u32[]{:S(2)}) %collective-permute-start.11) | collective-permute-done | bytes 1048608 | tf_op jit(solution)/shard_map/ppermute | solution.py:39
  240.3 3.1 %shard_map.78 = f32[1,1024]{1,0:T(1,128)S(1)} custom-call(s32[1]{0:T(128)} %bitcast.me_ref, bf16[512,26624]{1,0:T(8,128)(2,1)} %refs_0_.47, bf16[1024,6656]{1,0:T(8,128)(2,1)} %bitcast.4.refs_1_, bf16[528,1024]{1,0:T(8,128)(2,1)} %collective-permute-done.10.refs_2_, bf16[512,1024]{1,0:T(8,128)(2,1)} %collective-permute-done.11.refs_3_, ...), custom_call_target="tpu_custom_call" | custom-call | flops 89478488 | bytes 1398101 | tf_op jit(solution)/shard_map/pallas_call | solution.py:250
  243.5 22.2 %psum.39 = f32[1,1536]{1,0:T(1,128)S(1)} all-reduce(f32[1,1536]{1,0:T(1,128)S(1)} %pad_maximum_fusion.4), channel_id=1, replica_groups=mesh['fsdp'=8,'tp'=4] {'fsdp'}, use_global_device_ids=true, to_apply=%region_5.6 | all-reduce | flops 1536 | bytes 12288 | tf_op jit(solution)/shard_map/psum | solution.py:474
  265.7 5.9 %shard_map.80 = (bf16[2048,6656]{1,0:T(8,128)(2,1)}, f32[16,52]{1,0:T(8,128)S(1)}) custom-call(s32[1]{0:T(128)} %bitcast.me_ref, bf16[512,26624]{1,0:T(8,128)(2,1)} %refs_0_.47, bf16[1024,6656]{1,0:T(8,128)(2,1)} %bitcast.4.refs_1_, bf16[528,1024]{1,0:T(8,128)(2,1)} %collective-permute-done.10.refs_2_, ...), custom_call_target="tpu_custom_call", output_to_operand_aliasing={{0}: (12, {})} | custom-call | flops 89478488 | bytes 2796202 | tf_op jit(solution)/shard_map/pallas_call | solution.py:356
  271.6 3.3 %shard_map.81 = (bf16[2048,6656]{1,0:T(8,128)(2,1)}, f32[16,52]{1,0:T(8,128)S(1)}) custom-call(s32[1]{0:T(128)} %bitcast.me_ref, bf16[512,26624]{1,0:T(8,128)(2,1)} %refs_0_.47, bf16[1024,6656]{1,0:T(8,128)(2,1)} %bitcast.4.refs_1_, bf16[64,512]{1,0:T(8,128)(2,1)S(1)} %bitcast.20, ...), custom_call_target="tpu_custom_call", output_to_operand_aliasing={{0}: (8, {})} | custom-call | flops 22369620 | bytes 699050 | tf_op jit(solution)/shard_map/pallas_call | solution.py:356
  275.0 2.7 shard_map.82.refs_3_
  286.3 2.7 collective-permute-start.21
  290.9 5.9 %shard_map.84 = (bf16[2048,6656]{1,0:T(8,128)(2,1)}, f32[16,52]{1,0:T(8,128)S(1)}) custom-call(s32[1]{0:T(128)} %bitcast.me_ref, bf16[512,26624]{1,0:T(8,128)(2,1)} %refs_0_.47, bf16[1024,6656]{1,0:T(8,128)(2,1)} %bitcast.4.refs_1_, bf16[512,1024]{1,0:T(8,128)(2,1)} %collective-permute-done.16.refs_2_, ...), custom_call_target="tpu_custom_call", output_to_operand_aliasing={{0}: (12, {})} | custom-call | flops 89478488 | bytes 2796202 | tf_op jit(solution)/shard_map/pallas_call | solution.py:356
  (81 shorter events, 45.7 us)
Async XLA Ops:
  2.2 51.3 %collective-permute-start = (bf16[560,1024]{1,0:T(8,128)(2,1)S(1)}, bf16[560,1024]{1,0:T(8,128)(2,1)}, u32[]{:S(2)}, u32[]{:S(2)}) collective-permute-start(bf16[560,1024]{1,0:T(8,128)(2,1)S(1)} %shard_map.59), channel_id=1, source_target_pairs={{0,2},{1,3},{2,0},{3,1},{4,6},{5,7},{6,4},{7,5},{8,10},{9,11},{10,... | collective-permute-start | bytes 3440648 | tf_op jit(solution)/shard_map/ppermute | solution.py:39
  7.3 46.1 %collective-permute-start.1 = (bf16[512,1024]{1,0:T(8,128)(2,1)}, bf16[512,1024]{1,0:T(8,128)(2,1)}, u32[]{:S(2)}, u32[]{:S(2)}) collective-permute-start(bf16[512,1024]{1,0:T(8,128)(2,1)} %shard_map.60), channel_id=1, source_target_pairs={{0,3},{1,2},{2,1},{3,0},{4,7},{5,6},{6,5},{7,4},{8,11},{9,10},{10,... | collective-permute-start | bytes 3145736 | tf_op jit(solution)/shard_map/ppermute | solution.py:39
  10.0 82.2 %collective-permute-start.4 = (bf16[512,1024]{1,0:T(8,128)(2,1)}, bf16[512,1024]{1,0:T(8,128)(2,1)S(1)}, u32[]{:S(2)}, u32[]{:S(2)}) collective-permute-start(bf16[512,1024]{1,0:T(8,128)(2,1)} %get-tuple-element.48), channel_id=1, source_target_pairs={{0,2},{1,3},{2,0},{3,1},{4,6},{5,7},{6,4},{7,5},{8,10},{9,11},{10,... | collective-permute-start | bytes 3145736 | tf_op jit(solution)/shard_map/ppermute | solution.py:39
  11.2 19.3 %copy-start = (bf16[64,6656]{1,0:T(8,128)(2,1)S(1)}, bf16[64,6656]{1,0:T(8,128)(2,1)}, u32[]{:S(2)}) copy-start(bf16[64,6656]{1,0:T(8,128)(2,1)} %refs_2_.9) | copy-start | bytes 2555908
  11.2 87.1 %collective-permute-start.5 = (bf16[512,1024]{1,0:T(8,128)(2,1)}, bf16[512,1024]{1,0:T(8,128)(2,1)}, u32[]{:S(2)}, u32[]{:S(2)}) collective-permute-start(bf16[512,1024]{1,0:T(8,128)(2,1)} %get-tuple-element.49), channel_id=1, source_target_pairs={{0,3},{1,2},{2,1},{3,0},{4,7},{5,6},{6,5},{7,4},{8,11},{9,10},{10,... | collective-permute-start | bytes 3145736 | tf_op jit(solution)/shard_map/ppermute | solution.py:39
  21.6 39.5 %copy-start.1 = (bf16[512,64]{0,1:T(8,128)(2,1)S(1)}, bf16[512,64]{0,1:T(8,128)(2,1)}, u32[]{:S(2)}) copy-start(bf16[512,64]{0,1:T(8,128)(2,1)} %param.5) | copy-start | bytes 196612
  21.6 40.9 %all-to-all-start = ((bf16[2,512,6656]{2,1,0:T(8,128)(2,1)}), bf16[2,512,6656]{2,1,0:T(8,128)(2,1)}, u32[]{:S(2)}, u32[]{:S(2)}) async-start(bf16[2,512,6656]{2,1,0:T(8,128)(2,1)} %bitcast.32), calls=%async_computation | async-start | bytes 27262976 | tf_op jit(solution)/shard_map/all_to_all | solution.py:408
  54.2 6.9 %collective-permute-start.7 = (bf16[32,512]{1,0:T(8,128)(2,1)S(1)}, bf16[32,512]{1,0:T(8,128)(2,1)S(1)}, u32[]{:S(2)}, u32[]{:S(2)}) collective-permute-start(bf16[32,512]{1,0:T(8,128)(2,1)S(1)} %pad_maximum_fusion.3), channel_id=1, source_target_pairs={{0,4},{4,0},{8,12},{12,8},{16,20},{20,16},{24,28},{28,24},{1,5},{5... | collective-permute-start | bytes 98312 | tf_op jit(solution)/shard_map/ppermute | solution.py:39
  58.3 28.0 %copy-start.2 = (f32[26624]{0:T(1024)S(1)}, f32[26624]{0:T(1024)}, u32[]{:S(2)}) copy-start(f32[26624]{0:T(1024)} %param.7) | copy-start | bytes 319492
  58.3 77.1 %collective-permute-start.2 = (bf16[512,1024]{1,0:T(8,128)(2,1)}, bf16[512,1024]{1,0:T(8,128)(2,1)S(1)}, u32[]{:S(2)}, u32[]{:S(2)}) collective-permute-start(bf16[512,1024]{1,0:T(8,128)(2,1)} %get-tuple-element.45), channel_id=1, source_target_pairs={{0,2},{1,3},{2,0},{3,1},{4,6},{5,7},{6,4},{7,5},{8,10},{9,11},{10,... | collective-permute-start | bytes 3145736 | tf_op jit(solution)/shard_map/ppermute | solution.py:39
  58.9 84.3 %collective-permute-start.3 = (bf16[512,1024]{1,0:T(8,128)(2,1)}, bf16[512,1024]{1,0:T(8,128)(2,1)}, u32[]{:S(2)}, u32[]{:S(2)}) collective-permute-start(bf16[512,1024]{1,0:T(8,128)(2,1)} %get-tuple-element.46), channel_id=1, source_target_pairs={{0,3},{1,2},{2,1},{3,0},{4,7},{5,6},{6,5},{7,4},{8,11},{9,10},{10,... | collective-permute-start | bytes 3145736 | tf_op jit(solution)/shard_map/ppermute | solution.py:39
  61.1 1.4 collective-permute-start.6
  92.2 11.7 %copy-start.5 = (bf16[512,1024]{1,0:T(8,128)(2,1)}, bf16[512,1024]{1,0:T(8,128)(2,1)S(1)}, u32[]{:S(2)}) copy-start(bf16[512,1024]{1,0:T(8,128)(2,1)S(1)} %collective-permute-done.4.refs_2_) | copy-start | bytes 3145732
  101.0 82.1 %collective-permute-start.12 = (bf16[512,1024]{1,0:T(8,128)(2,1)}, bf16[512,1024]{1,0:T(8,128)(2,1)}, u32[]{:S(2)}, u32[]{:S(2)}) collective-permute-start(bf16[512,1024]{1,0:T(8,128)(2,1)} %get-tuple-element.59), channel_id=1, source_target_pairs={{0,2},{1,3},{2,0},{3,1},{4,6},{5,7},{6,4},{7,5},{8,10},{9,11},{10,... | collective-permute-start | bytes 3145736 | tf_op jit(solution)/shard_map/ppermute | solution.py:39
  101.2 87.0 %collective-permute-start.13 = (bf16[512,1024]{1,0:T(8,128)(2,1)}, bf16[512,1024]{1,0:T(8,128)(2,1)}, u32[]{:S(2)}, u32[]{:S(2)}) collective-permute-start(bf16[512,1024]{1,0:T(8,128)(2,1)} %get-tuple-element.60), channel_id=1, source_target_pairs={{0,3},{1,2},{2,1},{3,0},{4,7},{5,6},{6,5},{7,4},{8,11},{9,10},{10,... | collective-permute-start | bytes 3145736 | tf_op jit(solution)/shard_map/ppermute | solution.py:39
  103.7 30.9 %collective-permute-start.8 = (bf16[128,512]{1,0:T(8,128)(2,1)}, bf16[128,512]{1,0:T(8,128)(2,1)}, u32[]{:S(2)}, u32[]{:S(2)}) collective-permute-start(bf16[128,512]{1,0:T(8,128)(2,1)} %pad_maximum_fusion.1), channel_id=1, source_target_pairs={{0,1},{1,0},{2,3},{3,2},{4,5},{5,4},{6,7},{7,6},{8,9},{9,8},{10,11... | collective-permute-start | bytes 393224 | tf_op jit(solution)/shard_map/ppermute | solution.py:39
  135.5 10.1 %copy-start.6 = (bf16[512,1024]{1,0:T(8,128)(2,1)}, bf16[512,1024]{1,0:T(8,128)(2,1)S(1)}, u32[]{:S(2)}) copy-start(bf16[512,1024]{1,0:T(8,128)(2,1)S(1)} %collective-permute-done.2.refs_2_) | copy-start | bytes 3145732
  145.6 1.2 collective-permute-start.9
  146.9 0.6 copy-start.4
  150.2 83.7 %collective-permute-start.10 = (bf16[528,1024]{1,0:T(8,128)(2,1)}, bf16[528,1024]{1,0:T(8,128)(2,1)}, u32[]{:S(2)}, u32[]{:S(2)}) collective-permute-start(bf16[528,1024]{1,0:T(8,128)(2,1)} %get-tuple-element.56), channel_id=1, source_target_pairs={{0,2},{1,3},{2,0},{3,1},{4,6},{5,7},{6,4},{7,5},{8,10},{9,11},{10,... | collective-permute-start | bytes 3244040 | tf_op jit(solution)/shard_map/ppermute | solution.py:39
  152.2 81.7 %collective-permute-start.11 = (bf16[512,1024]{1,0:T(8,128)(2,1)}, bf16[512,1024]{1,0:T(8,128)(2,1)}, u32[]{:S(2)}, u32[]{:S(2)}) collective-permute-start(bf16[512,1024]{1,0:T(8,128)(2,1)} %get-tuple-element.57), channel_id=1, source_target_pairs={{0,3},{1,2},{2,1},{3,0},{4,7},{5,6},{6,5},{7,4},{8,11},{9,10},{10,... | collective-permute-start | bytes 3145736 | tf_op jit(solution)/shard_map/ppermute | solution.py:39
  190.8 84.1 %collective-permute-start.16 = (bf16[512,1024]{1,0:T(8,128)(2,1)}, bf16[512,1024]{1,0:T(8,128)(2,1)}, u32[]{:S(2)}, u32[]{:S(2)}) collective-permute-start(bf16[512,1024]{1,0:T(8,128)(2,1)} %get-tuple-element.72), channel_id=1, source_target_pairs={{0,2},{1,3},{2,0},{3,1},{4,6},{5,7},{6,4},{7,5},{8,10},{9,11},{10,... | collective-permute-start | bytes 3145736 | tf_op jit(solution)/shard_map/ppermute | solution.py:39
  191.1 87.7 %collective-permute-start.17 = (bf16[512,1024]{1,0:T(8,128)(2,1)}, bf16[512,1024]{1,0:T(8,128)(2,1)S(1)}, u32[]{:S(2)}, u32[]{:S(2)}) collective-permute-start(bf16[512,1024]{1,0:T(8,128)(2,1)} %get-tuple-element.73), channel_id=1, source_target_pairs={{0,3},{1,2},{2,1},{3,0},{4,7},{5,6},{6,5},{7,4},{8,11},{9,10},{10,... | collective-permute-start | bytes 3145736 | tf_op jit(solution)/shard_map/ppermute | solution.py:39
  235.7 61.1 %collective-permute-start.15 = (bf16[512,512]{1,0:T(8,128)(2,1)}, bf16[512,512]{1,0:T(8,128)(2,1)S(1)}, u32[]{:S(2)}, u32[]{:S(2)}) collective-permute-start(bf16[512,512]{1,0:T(8,128)(2,1)} %shard_map.76), channel_id=1, source_target_pairs={{0,2},{1,3},{2,0},{3,1},{4,6},{5,7},{6,4},{7,5},{8,10},{9,11},{10,... | collective-permute-start | bytes 1572872 | tf_op jit(solution)/shard_map/ppermute | solution.py:39
  237.8 62.3 %collective-permute-start.14 = (bf16[512,512]{1,0:T(8,128)(2,1)}, bf16[512,512]{1,0:T(8,128)(2,1)S(1)}, u32[]{:S(2)}, u32[]{:S(2)}) collective-permute-start(bf16[512,512]{1,0:T(8,128)(2,1)} %shard_map.77), channel_id=1, source_target_pairs={{0,3},{1,2},{2,1},{3,0},{4,7},{5,6},{6,5},{7,4},{8,11},{9,10},{10,... | collective-permute-start | bytes 1572872 | tf_op jit(solution)/shard_map/ppermute | solution.py:39
  278.8 12.1 %copy-start.3 = (bf16[512,1024]{1,0:T(8,128)(2,1)}, bf16[512,1024]{1,0:T(8,128)(2,1)S(1)}, u32[]{:S(2)}) copy-start(bf16[512,1024]{1,0:T(8,128)(2,1)S(1)} %collective-permute-done.17.refs_0_.refs_3_) | copy-start | bytes 3145732
  279.6 4.6 %collective-permute-start.20 = (f32[1,1024]{1,0:T(1,128)S(1)}, f32[1,1024]{1,0:T(1,128)S(1)}, u32[]{:S(2)}, u32[]{:S(2)}) collective-permute-start(f32[1,1024]{1,0:T(1,128)S(1)} %shard_map.83), channel_id=1, source_target_pairs={{0,12},{4,8},{8,4},{12,0},{16,28},{20,24},{24,20},{28,16},{1,13},{... | collective-permute-start | bytes 12296 | tf_op jit(solution)/shard_map/ppermute | solution.py:39
  282.2 3.6 %collective-permute-start.19 = (f32[1,1024]{1,0:T(1,128)S(1)}, f32[1,1024]{1,0:T(1,128)S(1)}, u32[]{:S(2)}, u32[]{:S(2)}) collective-permute-start(f32[1,1024]{1,0:T(1,128)S(1)} %shard_map.83), channel_id=1, source_target_pairs={{0,8},{4,12},{8,0},{12,4},{16,24},{20,28},{24,16},{28,20},{1,9},{5... | collective-permute-start | bytes 12296 | tf_op jit(solution)/shard_map/ppermute | solution.py:39
  282.7 3.6 %collective-permute-start.18 = (f32[1,1024]{1,0:T(1,128)S(1)}, f32[1,1024]{1,0:T(1,128)S(1)}, u32[]{:S(2)}, u32[]{:S(2)}) collective-permute-start(f32[1,1024]{1,0:T(1,128)S(1)} %shard_map.83), channel_id=1, source_target_pairs={{0,4},{4,0},{8,12},{12,8},{16,20},{20,16},{24,28},{28,24},{1,5},{5... | collective-permute-start | bytes 12296 | tf_op jit(solution)/shard_map/ppermute | solution.py:39
  286.3 4.6 %collective-permute-start.21 = (f32[1,1024]{1,0:T(1,128)S(1)}, f32[1,1024]{1,0:T(1,128)S(1)}, u32[]{:S(2)}, u32[]{:S(2)}) collective-permute-start(f32[1,1024]{1,0:T(1,128)S(1)} %add_add_fusion), channel_id=1, source_target_pairs={{0,16},{4,20},{8,24},{12,28},{16,0},{20,4},{24,8},{28,12},{1,17},{... | collective-permute-start | bytes 12296 | tf_op jit(solution)/shard_map/ppermute | solution.py:39

commit v6 on v5

--- a/solution.py
+++ b/solution.py
@@ -16,8 +16,8 @@
 CARRIER = 4
 TERMS = 3
 SUMS_ROWS = 16
-PARAMS = pltpu.CompilerParams(vmem_limit_bytes=52 * 2**20)
-MOVE_PARAMS = pltpu.CompilerParams(vmem_limit_bytes=56 * 2**20)
+PARAMS = pltpu.CompilerParams(vmem_limit_bytes=48 * 2**20)
+MOVE_PARAMS = pltpu.CompilerParams(vmem_limit_bytes=48 * 2**20)
 
 
 def chunk_blocks(total):
@@ -129,7 +129,7 @@
     def moves(me):
         return [m for i, d in enumerate(distances) for m in column_moves(me ^ d, rows, cols, group, first, i)]
 
-    return move(me, [base], [(rows, cols)] * len(distances), moves)
+    return move(me, [base], [(rows, cols)] * len(distances), moves, direct=True)
 
 
 def pack_first(place, base, tp, d, left, right, late, cols):
@@ -161,7 +161,7 @@
                 result.append((1, d // 2 * SUMS_ROWS, 0, SUMS_ROWS, terms.shape[1], i, rows, 0))
         return result
 
-    return move(me, [base, terms], [(rows + (d + 1) % 2 * SUMS_ROWS, cols) for d in distances], moves)
+    return move(me, [base, terms], [(rows + (d + 1) % 2 * SUMS_ROWS, cols) for d in distances], moves, direct=True)
 
 
 def pack_near(me, base, tp):

time: 302 us -> 307 us (1.017)
  Pallas kernels: 92.9 us -> 99.4 us
    pallas_call x10, Pallas kernels: 30.1 us -> 34.8 us  [move(): pl.pallas_call(functools.partial(move_kernel, moves, len(arrays), direct)...]
  transfers between devices with their start and end apart: 23 -> 23, of which waited for: 13 -> 13; matrix products, arithmetic and copies ran while one was open for 1% -> 0% of each run, Pallas kernels for 30% -> 31%
where the time goes in v6:
time: 307 us; the launch traced here: 306 us
  blocking collectives  108 us (35%)
  Pallas kernels  99.4 us (32%)
  waiting for transfers between devices  61.4 us (20%)
  starting transfers between devices  32.6 us (11%)
    psum x5, blocking collectives, body(): lax.psum(local, 'fsdp')  108 us
    ppermute x22, waiting for transfers between devices, swap(): return lax.ppermute(array, axis, [(i, i ^ d) for i in range(size)])  61.4 us
    pallas_call x9, Pallas kernels, export_chunk(): pl.pallas_call(functools.partial(export_kernel, tp, ds, first), out_shape...  42.8 us
    pallas_call x10, Pallas kernels, move(): pl.pallas_call(functools.partial(move_kernel, moves, len(arrays), direct)...  34.8 us
    ppermute x22, starting transfers between devices, swap(): return lax.ppermute(array, axis, [(i, i ^ d) for i in range(size)])  23.8 us
    pallas_call x7, Pallas kernels, column_squares(): pl.pallas_call(functools.partial(squares_kernel, len(ds)), out_shape=jax....  19.4 us
    all_to_all x1, starting transfers between devices, body(): lax.all_to_all(pack_near(after(me, *pieces), base, tp), 'tp', 0, 0, tiled...  8.87 us
  transfers between devices with their start and end apart: 23, of which 13 were waited for; matrix products, arithmetic and copies ran while one was open for 0% of the time, Pallas kernels for 31%

profile of v6, /device:TPU:0, one launch (start us, length us, event | category | flops | bytes accessed | tf_op | source)
XLA Modules:
  0.0 305.7 jit_solution(5426771298405232171)
XLA Ops:
  5.2 3.0 collective-permute-start
  10.6 3.2 %shard_map.62 = (bf16[512,1024]{1,0:T(8,128)(2,1)}, bf16[512,1024]{1,0:T(8,128)(2,1)}) custom-call(s32[1]{0:T(128)} %bitcast.me_ref, bf16[512,26624]{1,0:T(8,128)(2,1)} %refs_0_.47), custom_call_target="tpu_custom_call" | custom-call | bytes 1398101 | tf_op jit(solution)/shard_map/pallas_call | solution.py:78
  15.7 9.8 %shard_map.63 = bf16[1024,6656]{1,0:T(8,128)(2,1)} custom-call(s32[1]{0:T(128)} %bitcast.me_ref, bf16[512,26624]{1,0:T(8,128)(2,1)} %refs_0_.47), custom_call_target="tpu_custom_call" | custom-call | bytes 9087658 | tf_op jit(solution)/shard_map/pallas_call | solution.py:78
  25.5 8.9 %all-to-all-start = ((bf16[2,512,6656]{2,1,0:T(8,128)(2,1)}), bf16[2,512,6656]{2,1,0:T(8,128)(2,1)}, u32[]{:S(2)}, u32[]{:S(2)}) async-start(bf16[2,512,6656]{2,1,0:T(8,128)(2,1)} %bitcast.32), calls=%async_computation | async-start | bytes 27262976 | tf_op jit(solution)/shard_map/all_to_all | solution.py:408
  34.4 22.2 %collective-permute-done.1.refs_3_ = bf16[512,1024]{1,0:T(8,128)(2,1)} collective-permute-done((bf16[512,1024]{1,0:T(8,128)(2,1)}, bf16[512,1024]{1,0:T(8,128)(2,1)}, u32[]{:S(2)}, u32[]{:S(2)}) %collective-permute-start.1) | collective-permute-done | bytes 1048608 | tf_op jit(solution)/shard_map/ppermute | solution.py:39
  58.2 3.2 %shard_map.61 = (bf16[512,1024]{1,0:T(8,128)(2,1)}, bf16[512,1024]{1,0:T(8,128)(2,1)}) custom-call(s32[1]{0:T(128)} %bitcast.me_ref, bf16[512,26624]{1,0:T(8,128)(2,1)} %refs_0_.47), custom_call_target="tpu_custom_call" | custom-call | bytes 1398101 | tf_op jit(solution)/shard_map/pallas_call | solution.py:78
  64.9 3.0 shard_map.64
  67.9 20.7 %psum.35.refs_9_ = f32[1,1024]{1,0:T(1,128)S(1)} all-reduce(f32[1,1024]{1,0:T(1,128)S(1)} %shard_map.64), channel_id=1, replica_groups=mesh['fsdp'=8,'tp'=4] {'fsdp'}, use_global_device_ids=true, to_apply=%region_0.1 | all-reduce | flops 1024 | bytes 8192 | tf_op jit(solution)/shard_map/psum | solution.py:474
  88.6 5.7 %shard_map.65 = (bf16[2048,6656]{1,0:T(8,128)(2,1)}, f32[16,52]{1,0:T(8,128)S(1)}) custom-call(s32[1]{0:T(128)} %bitcast.me_ref, bf16[512,26624]{1,0:T(8,128)(2,1)} %refs_0_.47, bf16[1024,6656]{1,0:T(8,128)(2,1)} %bitcast.4.refs_1_, bf16[560,1024]{1,0:T(8,128)(2,1)S(1)} %collective-permute-done.refs_2_, bf16[512,1024]{1,0:T(8,128)(2,1)} %collective-permute-done.1.refs_3_, ...), custom_call_target="tpu_custom_call" | custom-call | flops 89478488 | bytes 2796202 | tf_op jit(solution)/shard_map/pallas_call | solution.py:356
  94.9 6.6 %collective-permute-done.5.refs_3_ = bf16[512,1024]{1,0:T(8,128)(2,1)} collective-permute-done((bf16[512,1024]{1,0:T(8,128)(2,1)}, bf16[512,1024]{1,0:T(8,128)(2,1)}, u32[]{:S(2)}, u32[]{:S(2)}) %collective-permute-start.5) | collective-permute-done | bytes 1048608 | tf_op jit(solution)/shard_map/ppermute | solution.py:39
  101.6 3.2 %shard_map.71 = (bf16[512,1024]{1,0:T(8,128)(2,1)}, bf16[512,1024]{1,0:T(8,128)(2,1)}) custom-call(s32[1]{0:T(128)} %bitcast.me_ref, bf16[512,26624]{1,0:T(8,128)(2,1)} %refs_0_.47), custom_call_target="tpu_custom_call" | custom-call | bytes 1398101 | tf_op jit(solution)/shard_map/pallas_call | solution.py:78
  107.1 2.9 shard_map.66
  110.1 21.8 %psum.36.refs_9_ = f32[1,1024]{1,0:T(1,128)S(1)} all-reduce(f32[1,1024]{1,0:T(1,128)S(1)} %shard_map.66), channel_id=1, replica_groups=mesh['fsdp'=8,'tp'=4] {'fsdp'}, use_global_device_ids=true, to_apply=%region_1.2 | all-reduce | flops 1024 | bytes 8192 | tf_op jit(solution)/shard_map/psum | solution.py:474
  131.8 5.8 %shard_map.67 = (bf16[2048,6656]{1,0:T(8,128)(2,1)}, f32[16,52]{1,0:T(8,128)S(1)}) custom-call(s32[1]{0:T(128)} %bitcast.me_ref, bf16[512,26624]{1,0:T(8,128)(2,1)} %refs_0_.47, bf16[1024,6656]{1,0:T(8,128)(2,1)} %bitcast.4.refs_1_, bf16[512,1024]{1,0:T(8,128)(2,1)S(1)} %collective-permute-done.4.refs_2_, ...), custom_call_target="tpu_custom_call", output_to_operand_aliasing={{0}: (12, {})} | custom-call | flops 89478488 | bytes 2796202 | tf_op jit(solution)/shard_map/pallas_call | solution.py:356
  137.6 8.9 %collective-permute-done.3.refs_3_ = bf16[512,1024]{1,0:T(8,128)(2,1)} collective-permute-done((bf16[512,1024]{1,0:T(8,128)(2,1)}, bf16[512,1024]{1,0:T(8,128)(2,1)}, u32[]{:S(2)}, u32[]{:S(2)}) %collective-permute-start.3) | collective-permute-done | bytes 1048608 | tf_op jit(solution)/shard_map/ppermute | solution.py:39
  150.1 3.2 %shard_map.70 = (bf16[528,1024]{1,0:T(8,128)(2,1)}, bf16[512,1024]{1,0:T(8,128)(2,1)}) custom-call(s32[1]{0:T(128)} %bitcast.me_ref, bf16[512,26624]{1,0:T(8,128)(2,1)} %refs_0_.47, bf16[32,512]{1,0:T(8,128)(2,1)S(1)} %shard_map.69.refs_1_), custom_call_target="tpu_custom_call" | custom-call | bytes 1419946 | tf_op jit(solution)/shard_map/pallas_call | solution.py:78
  155.4 3.1 %shard_map.72 = f32[1,1024]{1,0:T(1,128)S(1)} custom-call(s32[1]{0:T(128)} %bitcast.me_ref, bf16[512,26624]{1,0:T(8,128)(2,1)} %refs_0_.47, bf16[1024,6656]{1,0:T(8,128)(2,1)} %bitcast.4.refs_1_, bf16[512,1024]{1,0:T(8,128)(2,1)} %collective-permute-done.2.refs_2_, bf16[512,1024]{1,0:T(8,128)(2,1)} %collective-permute-done.3.refs_3_, ...), custom_call_target="tpu_custom_call" | custom-call | flops 89478488 | bytes 1398101 | tf_op jit(solution)/shard_map/pallas_call | solution.py:250
  158.5 21.8 %psum.37.refs_9_ = f32[1,1024]{1,0:T(1,128)S(1)} all-reduce(f32[1,1024]{1,0:T(1,128)S(1)} %shard_map.72), channel_id=1, replica_groups=mesh['fsdp'=8,'tp'=4] {'fsdp'}, use_global_device_ids=true, to_apply=%region_2.3 | all-reduce | flops 1024 | bytes 8192 | tf_op jit(solution)/shard_map/psum | solution.py:474
  180.4 5.9 %shard_map.73 = (bf16[2048,6656]{1,0:T(8,128)(2,1)}, f32[16,52]{1,0:T(8,128)S(1)}) custom-call(s32[1]{0:T(128)} %bitcast.me_ref, bf16[512,26624]{1,0:T(8,128)(2,1)} %refs_0_.47, bf16[1024,6656]{1,0:T(8,128)(2,1)} %bitcast.4.refs_1_, bf16[512,1024]{1,0:T(8,128)(2,1)} %collective-permute-done.2.refs_2_, ...), custom_call_target="tpu_custom_call", output_to_operand_aliasing={{0}: (12, {})} | custom-call | flops 89478488 | bytes 2796202 | tf_op jit(solution)/shard_map/pallas_call | solution.py:356
  186.3 5.2 %collective-permute-done.13.refs_3_ = bf16[512,1024]{1,0:T(8,128)(2,1)} collective-permute-done((bf16[512,1024]{1,0:T(8,128)(2,1)}, bf16[512,1024]{1,0:T(8,128)(2,1)}, u32[]{:S(2)}, u32[]{:S(2)}) %collective-permute-start.13) | collective-permute-done | bytes 1048608 | tf_op jit(solution)/shard_map/ppermute | solution.py:39
  191.4 3.3 %shard_map.79 = (bf16[512,1024]{1,0:T(8,128)(2,1)}, bf16[512,1024]{1,0:T(8,128)(2,1)}) custom-call(s32[1]{0:T(128)} %bitcast.me_ref, bf16[512,26624]{1,0:T(8,128)(2,1)} %refs_0_.47), custom_call_target="tpu_custom_call" | custom-call | bytes 1398101 | tf_op jit(solution)/shard_map/pallas_call | solution.py:78
  196.8 3.1 %shard_map.74 = f32[1,1024]{1,0:T(1,128)S(1)} custom-call(s32[1]{0:T(128)} %bitcast.me_ref, bf16[512,26624]{1,0:T(8,128)(2,1)} %refs_0_.47, bf16[1024,6656]{1,0:T(8,128)(2,1)} %bitcast.4.refs_1_, bf16[512,1024]{1,0:T(8,128)(2,1)} %collective-permute-done.12.refs_2_, bf16[512,1024]{1,0:T(8,128)(2,1)} %collective-permute-done.13.refs_3_, ...), custom_call_target="tpu_custom_call" | custom-call | flops 89478488 | bytes 1398101 | tf_op jit(solution)/shard_map/pallas_call | solution.py:250
  199.9 22.0 %psum.38.refs_9_ = f32[1,1024]{1,0:T(1,128)S(1)} all-reduce(f32[1,1024]{1,0:T(1,128)S(1)} %shard_map.74), channel_id=1, replica_groups=mesh['fsdp'=8,'tp'=4] {'fsdp'}, use_global_device_ids=true, to_apply=%region_3.4 | all-reduce | flops 1024 | bytes 8192 | tf_op jit(solution)/shard_map/psum | solution.py:474
  221.9 5.9 %shard_map.75 = (bf16[2048,6656]{1,0:T(8,128)(2,1)}, f32[16,52]{1,0:T(8,128)S(1)}) custom-call(s32[1]{0:T(128)} %bitcast.me_ref, bf16[512,26624]{1,0:T(8,128)(2,1)} %refs_0_.47, bf16[1024,6656]{1,0:T(8,128)(2,1)} %bitcast.4.refs_1_, bf16[512,1024]{1,0:T(8,128)(2,1)} %collective-permute-done.12.refs_2_, ...), custom_call_target="tpu_custom_call", output_to_operand_aliasing={{0}: (12, {})} | custom-call | flops 89478488 | bytes 2796202 | tf_op jit(solution)/shard_map/pallas_call | solution.py:356
  227.8 9.3 %collective-permute-done.11.refs_3_ = bf16[512,1024]{1,0:T(8,128)(2,1)} collective-permute-done((bf16[512,1024]{1,0:T(8,128)(2,1)}, bf16[512,1024]{1,0:T(8,128)(2,1)}, u32[]{:S(2)}, u32[]{:S(2)}) %collective-permute-start.11) | collective-permute-done | bytes 1048608 | tf_op jit(solution)/shard_map/ppermute | solution.py:39
  243.2 3.0 shard_map.78
  246.2 22.1 %psum.39 = f32[1,1536]{1,0:T(1,128)S(1)} all-reduce(f32[1,1536]{1,0:T(1,128)S(1)} %pad_maximum_fusion.4), channel_id=1, replica_groups=mesh['fsdp'=8,'tp'=4] {'fsdp'}, use_global_device_ids=true, to_apply=%region_5.6 | all-reduce | flops 1536 | bytes 12288 | tf_op jit(solution)/shard_map/psum | solution.py:474
  268.4 5.8 %shard_map.80 = (bf16[2048,6656]{1,0:T(8,128)(2,1)}, f32[16,52]{1,0:T(8,128)S(1)}) custom-call(s32[1]{0:T(128)} %bitcast.me_ref, bf16[512,26624]{1,0:T(8,128)(2,1)} %refs_0_.47, bf16[1024,6656]{1,0:T(8,128)(2,1)} %bitcast.4.refs_1_, bf16[528,1024]{1,0:T(8,128)(2,1)S(1)} %collective-permute-done.10.refs_2_, ...), custom_call_target="tpu_custom_call", output_to_operand_aliasing={{0}: (12, {})} | custom-call | flops 89478488 | bytes 2796202 | tf_op jit(solution)/shard_map/pallas_call | solution.py:356
  274.1 3.3 %shard_map.81 = (bf16[2048,6656]{1,0:T(8,128)(2,1)}, f32[16,52]{1,0:T(8,128)S(1)}) custom-call(s32[1]{0:T(128)} %bitcast.me_ref, bf16[512,26624]{1,0:T(8,128)(2,1)} %refs_0_.47, bf16[1024,6656]{1,0:T(8,128)(2,1)} %bitcast.4.refs_1_, bf16[64,512]{1,0:T(8,128)(2,1)S(1)} %bitcast.20, ...), custom_call_target="tpu_custom_call", output_to_operand_aliasing={{0}: (8, {})} | custom-call | flops 22369620 | bytes 699050 | tf_op jit(solution)/shard_map/pallas_call | solution.py:356
  283.8 2.6 collective-permute-start.20
  290.5 2.7 collective-permute-start.21
  295.0 5.8 %shard_map.84 = (bf16[2048,6656]{1,0:T(8,128)(2,1)}, f32[16,52]{1,0:T(8,128)S(1)}) custom-call(s32[1]{0:T(128)} %bitcast.me_ref, bf16[512,26624]{1,0:T(8,128)(2,1)} %refs_0_.47, bf16[1024,6656]{1,0:T(8,128)(2,1)} %bitcast.4.refs_1_, bf16[512,1024]{1,0:T(8,128)(2,1)S(1)} %collective-permute-done.16.refs_2_, ...), custom_call_target="tpu_custom_call", output_to_operand_aliasing={{0}: (12, {})} | custom-call | flops 89478488 | bytes 2796202 | tf_op jit(solution)/shard_map/pallas_call | solution.py:356
  (81 shorter events, 47.7 us)
Async XLA Ops:
  0.6 1.2 copy-start
  1.8 0.8 copy-start.2
  5.2 51.5 %collective-permute-start = (bf16[560,1024]{1,0:T(8,128)(2,1)}, bf16[560,1024]{1,0:T(8,128)(2,1)S(1)}, u32[]{:S(2)}, u32[]{:S(2)}) collective-permute-start(bf16[560,1024]{1,0:T(8,128)(2,1)} %shard_map.59), channel_id=1, source_target_pairs={{0,2},{1,3},{2,0},{3,1},{4,6},{5,7},{6,4},{7,5},{8,10},{9,11},{10,... | collective-permute-start | bytes 3440648 | tf_op jit(solution)/shard_map/ppermute | solution.py:39
  10.6 46.1 %collective-permute-start.1 = (bf16[512,1024]{1,0:T(8,128)(2,1)}, bf16[512,1024]{1,0:T(8,128)(2,1)}, u32[]{:S(2)}, u32[]{:S(2)}) collective-permute-start(bf16[512,1024]{1,0:T(8,128)(2,1)} %shard_map.60), channel_id=1, source_target_pairs={{0,3},{1,2},{2,1},{3,0},{4,7},{5,6},{6,5},{7,4},{8,11},{9,10},{10,... | collective-permute-start | bytes 3145736 | tf_op jit(solution)/shard_map/ppermute | solution.py:39
  13.9 81.1 %collective-permute-start.4 = (bf16[512,1024]{1,0:T(8,128)(2,1)}, bf16[512,1024]{1,0:T(8,128)(2,1)S(1)}, u32[]{:S(2)}, u32[]{:S(2)}) collective-permute-start(bf16[512,1024]{1,0:T(8,128)(2,1)} %get-tuple-element.48), channel_id=1, source_target_pairs={{0,2},{1,3},{2,0},{3,1},{4,6},{5,7},{6,4},{7,5},{8,10},{9,11},{10,... | collective-permute-start | bytes 3145736 | tf_op jit(solution)/shard_map/ppermute | solution.py:39
  15.1 19.3 %copy-start.1 = (bf16[64,6656]{1,0:T(8,128)(2,1)S(1)}, bf16[64,6656]{1,0:T(8,128)(2,1)}, u32[]{:S(2)}) copy-start(bf16[64,6656]{1,0:T(8,128)(2,1)} %refs_2_.9) | copy-start | bytes 2555908
  15.1 86.5 %collective-permute-start.5 = (bf16[512,1024]{1,0:T(8,128)(2,1)}, bf16[512,1024]{1,0:T(8,128)(2,1)}, u32[]{:S(2)}, u32[]{:S(2)}) collective-permute-start(bf16[512,1024]{1,0:T(8,128)(2,1)} %get-tuple-element.49), channel_id=1, source_target_pairs={{0,3},{1,2},{2,1},{3,0},{4,7},{5,6},{6,5},{7,4},{8,11},{9,10},{10,... | collective-permute-start | bytes 3145736 | tf_op jit(solution)/shard_map/ppermute | solution.py:39
  25.5 37.9 %copy-start.3 = (bf16[512,64]{0,1:T(8,128)(2,1)S(1)}, bf16[512,64]{0,1:T(8,128)(2,1)}, u32[]{:S(2)}) copy-start(bf16[512,64]{0,1:T(8,128)(2,1)} %param.5) | copy-start | bytes 196612
  25.5 39.4 %all-to-all-start = ((bf16[2,512,6656]{2,1,0:T(8,128)(2,1)}), bf16[2,512,6656]{2,1,0:T(8,128)(2,1)}, u32[]{:S(2)}, u32[]{:S(2)}) async-start(bf16[2,512,6656]{2,1,0:T(8,128)(2,1)} %bitcast.32), calls=%async_computation | async-start | bytes 27262976 | tf_op jit(solution)/shard_map/all_to_all | solution.py:408
  56.6 6.8 %collective-permute-start.7 = (bf16[32,512]{1,0:T(8,128)(2,1)S(1)}, bf16[32,512]{1,0:T(8,128)(2,1)S(1)}, u32[]{:S(2)}, u32[]{:S(2)}) collective-permute-start(bf16[32,512]{1,0:T(8,128)(2,1)S(1)} %pad_maximum_fusion.3), channel_id=1, source_target_pairs={{0,4},{4,0},{8,12},{12,8},{16,20},{20,16},{24,28},{28,24},{1,5},{5... | collective-permute-start | bytes 98312 | tf_op jit(solution)/shard_map/ppermute | solution.py:39
  61.4 27.1 %copy-start.4 = (f32[26624]{0:T(1024)S(1)}, f32[26624]{0:T(1024)}, u32[]{:S(2)}) copy-start(f32[26624]{0:T(1024)} %param.7) | copy-start | bytes 319492
  61.5 76.2 %collective-permute-start.2 = (bf16[512,1024]{1,0:T(8,128)(2,1)}, bf16[512,1024]{1,0:T(8,128)(2,1)}, u32[]{:S(2)}, u32[]{:S(2)}) collective-permute-start(bf16[512,1024]{1,0:T(8,128)(2,1)} %get-tuple-element.45), channel_id=1, source_target_pairs={{0,2},{1,3},{2,0},{3,1},{4,6},{5,7},{6,4},{7,5},{8,10},{9,11},{10,... | collective-permute-start | bytes 3145736 | tf_op jit(solution)/shard_map/ppermute | solution.py:39
  62.1 84.4 %collective-permute-start.3 = (bf16[512,1024]{1,0:T(8,128)(2,1)}, bf16[512,1024]{1,0:T(8,128)(2,1)}, u32[]{:S(2)}, u32[]{:S(2)}) collective-permute-start(bf16[512,1024]{1,0:T(8,128)(2,1)} %get-tuple-element.46), channel_id=1, source_target_pairs={{0,3},{1,2},{2,1},{3,0},{4,7},{5,6},{6,5},{7,4},{8,11},{9,10},{10,... | collective-permute-start | bytes 3145736 | tf_op jit(solution)/shard_map/ppermute | solution.py:39
  63.5 1.4 collective-permute-start.6
  94.3 0.6 copy-start.5
  104.8 27.0 %copy-start.6 = (f32[16,52]{1,0:T(8,128)S(1)}, f32[16,52]{1,0:T(8,128)}, u32[]{:S(2)}) copy-start(f32[16,52]{1,0:T(8,128)} %copy-done.5) | copy-start | bytes 9988
  104.8 81.4 %collective-permute-start.12 = (bf16[512,1024]{1,0:T(8,128)(2,1)}, bf16[512,1024]{1,0:T(8,128)(2,1)}, u32[]{:S(2)}, u32[]{:S(2)}) collective-permute-start(bf16[512,1024]{1,0:T(8,128)(2,1)} %get-tuple-element.59), channel_id=1, source_target_pairs={{0,2},{1,3},{2,0},{3,1},{4,6},{5,7},{6,4},{7,5},{8,10},{9,11},{10,... | collective-permute-start | bytes 3145736 | tf_op jit(solution)/shard_map/ppermute | solution.py:39
  105.1 86.4 %collective-permute-start.13 = (bf16[512,1024]{1,0:T(8,128)(2,1)}, bf16[512,1024]{1,0:T(8,128)(2,1)}, u32[]{:S(2)}, u32[]{:S(2)}) collective-permute-start(bf16[512,1024]{1,0:T(8,128)(2,1)} %get-tuple-element.60), channel_id=1, source_target_pairs={{0,3},{1,2},{2,1},{3,0},{4,7},{5,6},{6,5},{7,4},{8,11},{9,10},{10,... | collective-permute-start | bytes 3145736 | tf_op jit(solution)/shard_map/ppermute | solution.py:39
  106.9 30.7 %collective-permute-start.8 = (bf16[128,512]{1,0:T(8,128)(2,1)S(1)}, bf16[128,512]{1,0:T(8,128)(2,1)S(1)}, u32[]{:S(2)}, u32[]{:S(2)}) collective-permute-start(bf16[128,512]{1,0:T(8,128)(2,1)S(1)} %pad_maximum_fusion.1), channel_id=1, source_target_pairs={{0,1},{1,0},{2,3},{3,2},{4,5},{5,4},{6,7},{7,6},{8,9},{9,8},{10,11... | collective-permute-start | bytes 393224 | tf_op jit(solution)/shard_map/ppermute | solution.py:39
  148.8 1.2 collective-permute-start.9
  153.3 83.7 %collective-permute-start.10 = (bf16[528,1024]{1,0:T(8,128)(2,1)}, bf16[528,1024]{1,0:T(8,128)(2,1)S(1)}, u32[]{:S(2)}, u32[]{:S(2)}) collective-permute-start(bf16[528,1024]{1,0:T(8,128)(2,1)} %get-tuple-element.56), channel_id=1, source_target_pairs={{0,2},{1,3},{2,0},{3,1},{4,6},{5,7},{6,4},{7,5},{8,10},{9,11},{10,... | collective-permute-start | bytes 3244040 | tf_op jit(solution)/shard_map/ppermute | solution.py:39
  155.4 81.7 %collective-permute-start.11 = (bf16[512,1024]{1,0:T(8,128)(2,1)}, bf16[512,1024]{1,0:T(8,128)(2,1)}, u32[]{:S(2)}, u32[]{:S(2)}) collective-permute-start(bf16[512,1024]{1,0:T(8,128)(2,1)} %get-tuple-element.57), channel_id=1, source_target_pairs={{0,3},{1,2},{2,1},{3,0},{4,7},{5,6},{6,5},{7,4},{8,11},{9,10},{10,... | collective-permute-start | bytes 3145736 | tf_op jit(solution)/shard_map/ppermute | solution.py:39
  194.7 82.8 %collective-permute-start.16 = (bf16[512,1024]{1,0:T(8,128)(2,1)}, bf16[512,1024]{1,0:T(8,128)(2,1)S(1)}, u32[]{:S(2)}, u32[]{:S(2)}) collective-permute-start(bf16[512,1024]{1,0:T(8,128)(2,1)} %get-tuple-element.72), channel_id=1, source_target_pairs={{0,2},{1,3},{2,0},{3,1},{4,6},{5,7},{6,4},{7,5},{8,10},{9,11},{10,... | collective-permute-start | bytes 3145736 | tf_op jit(solution)/shard_map/ppermute | solution.py:39
  195.0 87.1 %collective-permute-start.17 = (bf16[512,1024]{1,0:T(8,128)(2,1)}, bf16[512,1024]{1,0:T(8,128)(2,1)}, u32[]{:S(2)}, u32[]{:S(2)}) collective-permute-start(bf16[512,1024]{1,0:T(8,128)(2,1)} %get-tuple-element.73), channel_id=1, source_target_pairs={{0,3},{1,2},{2,1},{3,0},{4,7},{5,6},{6,5},{7,4},{8,11},{9,10},{10,... | collective-permute-start | bytes 3145736 | tf_op jit(solution)/shard_map/ppermute | solution.py:39
  239.1 61.7 %collective-permute-start.15 = (bf16[512,512]{1,0:T(8,128)(2,1)}, bf16[512,512]{1,0:T(8,128)(2,1)}, u32[]{:S(2)}, u32[]{:S(2)}) collective-permute-start(bf16[512,512]{1,0:T(8,128)(2,1)} %shard_map.76), channel_id=1, source_target_pairs={{0,2},{1,3},{2,0},{3,1},{4,6},{5,7},{6,4},{7,5},{8,10},{9,11},{10,... | collective-permute-start | bytes 1572872 | tf_op jit(solution)/shard_map/ppermute | solution.py:39
  241.3 62.0 %collective-permute-start.14 = (bf16[512,512]{1,0:T(8,128)(2,1)}, bf16[512,512]{1,0:T(8,128)(2,1)}, u32[]{:S(2)}, u32[]{:S(2)}) collective-permute-start(bf16[512,512]{1,0:T(8,128)(2,1)} %shard_map.77), channel_id=1, source_target_pairs={{0,3},{1,2},{2,1},{3,0},{4,7},{5,6},{6,5},{7,4},{8,11},{9,10},{10,... | collective-permute-start | bytes 1572872 | tf_op jit(solution)/shard_map/ppermute | solution.py:39
  283.8 4.6 %collective-permute-start.20 = (f32[1,1024]{1,0:T(1,128)S(1)}, f32[1,1024]{1,0:T(1,128)S(1)}, u32[]{:S(2)}, u32[]{:S(2)}) collective-permute-start(f32[1,1024]{1,0:T(1,128)S(1)} %shard_map.83), channel_id=1, source_target_pairs={{0,12},{4,8},{8,4},{12,0},{16,28},{20,24},{24,20},{28,16},{1,13},{... | collective-permute-start | bytes 12296 | tf_op jit(solution)/shard_map/ppermute | solution.py:39
  286.4 3.6 %collective-permute-start.19 = (f32[1,1024]{1,0:T(1,128)S(1)}, f32[1,1024]{1,0:T(1,128)S(1)}, u32[]{:S(2)}, u32[]{:S(2)}) collective-permute-start(f32[1,1024]{1,0:T(1,128)S(1)} %shard_map.83), channel_id=1, source_target_pairs={{0,8},{4,12},{8,0},{12,4},{16,24},{20,28},{24,16},{28,20},{1,9},{5... | collective-permute-start | bytes 12296 | tf_op jit(solution)/shard_map/ppermute | solution.py:39
  286.8 3.6 %collective-permute-start.18 = (f32[1,1024]{1,0:T(1,128)S(1)}, f32[1,1024]{1,0:T(1,128)S(1)}, u32[]{:S(2)}, u32[]{:S(2)}) collective-permute-start(f32[1,1024]{1,0:T(1,128)S(1)} %shard_map.83), channel_id=1, source_target_pairs={{0,4},{4,0},{8,12},{12,8},{16,20},{20,16},{24,28},{28,24},{1,5},{5... | collective-permute-start | bytes 12296 | tf_op jit(solution)/shard_map/ppermute | solution.py:39
  290.5 4.6 %collective-permute-start.21 = (f32[1,1024]{1,0:T(1,128)S(1)}, f32[1,1024]{1,0:T(1,128)S(1)}, u32[]{:S(2)}, u32[]{:S(2)}) collective-permute-start(f32[1,1024]{1,0:T(1,128)S(1)} %add_add_fusion), channel_id=1, source_target_pairs={{0,16},{4,20},{8,24},{12,28},{16,0},{20,4},{24,8},{28,12},{1,17},{... | collective-permute-start | bytes 12296 | tf_op jit(solution)/shard_map/ppermute | solution.py:39

commit v7 on v5

--- a/solution.py
+++ b/solution.py
@@ -9,11 +9,11 @@
 
 BLOCK = 128
 EPSILON = 1e-06
-EARLY = (8, 8, 8, 8, 8, 8)
+EARLY = (12, 12, 12, 12)
 LATE = (4,)
 AHEAD = 2
 SCALE = 3
-CARRIER = 4
+CARRIER = 2
 TERMS = 3
 SUMS_ROWS = 16
 PARAMS = pltpu.CompilerParams(vmem_limit_bytes=52 * 2**20)
@@ -135,19 +135,18 @@
 def pack_first(place, base, tp, d, left, right, late, cols):
     rows, group = base.shape[0], base.shape[1] // tp
     rank, lane = left.shape
-    late_cols = late[1] - late[0]
-    half, quarter = rank // 2, rank // 4
+    half = rank // 2
 
     def moves(place):
         line, me = place // tp, place % tp
         result = column_moves(me ^ d, rows, cols, group, 0, 0)
         for i in range(2):
             result.append((1, i * half, 0, half, lane, 0, rows, i * lane))
-            row = pl.multiple_of(line % 2 * half + i * quarter, quarter)
-            result.append((2, row, late[0], quarter, late_cols, 0, rows + half, i * late_cols))
+        row = pl.multiple_of(line % 2 * half, half)
+        result.append((2, row, late[0], half, late[1] - late[0], 0, rows, 2 * lane))
         return result
 
-    return move(place, [base, left, right], [(rows + half + quarter, cols)], moves, direct=True)[0]
+    return move(place, [base, left, right], [(rows + half, cols)], moves, direct=True)[0]
 
 
 def pack_carrier(me, base, tp, distances, terms, first, cols):
@@ -410,19 +409,17 @@
         axis_index_groups=[[i, i + 1] for i in range(0, tp, 2)],
     )
 
-    def unfold(block, width):
-        return jnp.concatenate([block[:, :width], block[:, width : 2 * width]])
-
     def alternate(even):
         odd = swap(jnp.concatenate(even), 1, tp)
         return [array for i, own in enumerate(even) for array in (own, odd[i * rank : (i + 1) * rank])]
 
     arrived = [received[0][d - 2] for d in far[::2]]
     half, late_cols = rank // 2, (late[1] - late[0]) * BLOCK
-    extras = alternate([left] + [unfold(piece[rows : rows + half], lane) for piece in arrived])
+    halves = [[piece[rows : rows + half, i * lane : (i + 1) * lane] for i in range(2)] for piece in arrived]
+    extras = alternate([left] + [jnp.concatenate(pair) for pair in halves])
 
     def late_rights():
-        mine = jnp.concatenate([unfold(piece[rows + half :], late_cols) for piece in arrived], axis=1)
+        mine = jnp.concatenate([piece[rows:, 2 * lane : 2 * lane + late_cols] for piece in arrived], axis=1)
         other = swap(mine, 1, fsdp, "fsdp")
         both = jnp.where(line % 2 == 0, jnp.concatenate([mine, other]), jnp.concatenate([other, mine]))
         even = [right[:, late[0] * BLOCK : late[1] * BLOCK]]

time: 302 us -> 305 us (level)
  waiting for transfers between devices: 62.1 us -> 123 us
  blocking collectives: 108 us -> 62.1 us
  Pallas kernels: 92.9 us -> 88.7 us
  starting transfers between devices: 32.5 us -> 28.3 us
    ppermute x22 -> x18, waiting for transfers between devices: 62.1 us -> 111 us  [swap(): return lax.ppermute(array, axis, [(i, i ^ d) for i in range(size)])]
    psum x5 -> x3, blocking collectives: 108 us -> 62.1 us  [body(): lax.psum(local, 'fsdp')]
    all_to_all x1, waiting for transfers between devices: 0.01 us -> 11.2 us  [body(): lax.all_to_all(pack_near(after(me, *pieces), base, tp), 'tp', 0, 0, tiled...]
    ppermute x22 -> x18, starting transfers between devices: 23.6 us -> 19.5 us  [swap(): return lax.ppermute(array, axis, [(i, i ^ d) for i in range(size)])]
    pallas_call x10 -> x8, Pallas kernels: 30.1 us -> 27.1 us  [move(): pl.pallas_call(functools.partial(move_kernel, moves, len(arrays), direct)...]
    pallas_call x9 -> x7, Pallas kernels: 41.3 us -> 38.5 us  [export_chunk(): pl.pallas_call(functools.partial(export_kernel, tp, ds, first), out_shape...]
    pallas_call x7 -> x5, Pallas kernels: 19.1 us -> 20.8 us  [column_squares(): pl.pallas_call(functools.partial(squares_kernel, len(ds)), out_shape=jax....]
  transfers between devices with their start and end apart: 23 -> 19, of which waited for: 13 -> 11; matrix products, arithmetic and copies ran while one was open for 1% -> 0% of each run, Pallas kernels for 30% -> 28%
where the time goes in v7:
time: 305 us; the launch traced here: 304 us
  waiting for transfers between devices  123 us (40%)
  Pallas kernels  88.7 us (29%)
  blocking collectives  62.1 us (20%)
  starting transfers between devices  28.3 us (9%)
    ppermute x18, waiting for transfers between devices, swap(): return lax.ppermute(array, axis, [(i, i ^ d) for i in range(size)])  111 us
    psum x3, blocking collectives, body(): lax.psum(local, 'fsdp')  62.1 us
    pallas_call x7, Pallas kernels, export_chunk(): pl.pallas_call(functools.partial(export_kernel, tp, ds, first), out_shape...  38.5 us
    pallas_call x8, Pallas kernels, move(): pl.pallas_call(functools.partial(move_kernel, moves, len(arrays), direct)...  27.1 us
    pallas_call x5, Pallas kernels, column_squares(): pl.pallas_call(functools.partial(squares_kernel, len(ds)), out_shape=jax....  20.8 us
    ppermute x18, starting transfers between devices, swap(): return lax.ppermute(array, axis, [(i, i ^ d) for i in range(size)])  19.5 us
    all_to_all x1, waiting for transfers between devices, body(): lax.all_to_all(pack_near(after(me, *pieces), base, tp), 'tp', 0, 0, tiled...  11.2 us
    all_to_all x1, starting transfers between devices, body(): lax.all_to_all(pack_near(after(me, *pieces), base, tp), 'tp', 0, 0, tiled...  8.77 us
  transfers between devices with their start and end apart: 19, of which 11 were waited for; matrix products, arithmetic and copies ran while one was open for 0% of the time, Pallas kernels for 28%

profile of v7, /device:TPU:0, one launch (start us, length us, event | category | flops | bytes accessed | tf_op | source)
XLA Modules:
  0.0 304.2 jit_solution(130919914090221786)
XLA Ops:
  2.3 3.0 collective-permute-start
  5.3 2.3 shard_map.60
  7.7 3.3 %shard_map.64 = (bf16[512,1536]{1,0:T(8,128)(2,1)}, bf16[512,1536]{1,0:T(8,128)(2,1)}) custom-call(s32[1]{0:T(128)} %bitcast.me_ref, bf16[512,26624]{1,0:T(8,128)(2,1)} %refs_0_.35), custom_call_target="tpu_custom_call" | custom-call | bytes 2097152 | tf_op jit(solution)/shard_map/pallas_call | solution.py:78
  12.8 29.8 %collective-permute-done.refs_2_ = bf16[544,1536]{1,0:T(8,128)(2,1)S(1)} collective-permute-done((bf16[544,1536]{1,0:T(8,128)(2,1)S(1)}, bf16[544,1536]{1,0:T(8,128)(2,1)S(1)}, u32[]{:S(2)}, u32[]{:S(2)}) %collective-permute-start) | collective-permute-done | bytes 1671200 | tf_op jit(solution)/shard_map/ppermute | solution.py:39
  42.7 2.2 collective-permute-start.2
  44.8 1.9 collective-permute-done.2
  46.8 29.2 %collective-permute-done.1.refs_3_ = bf16[512,1536]{1,0:T(8,128)(2,1)} collective-permute-done((bf16[512,1536]{1,0:T(8,128)(2,1)}, bf16[512,1536]{1,0:T(8,128)(2,1)}, u32[]{:S(2)}, u32[]{:S(2)}) %collective-permute-start.1) | collective-permute-done | bytes 1572896 | tf_op jit(solution)/shard_map/ppermute | solution.py:39
  76.1 2.3 shard_map.61
  80.3 3.3 %shard_map.63 = (bf16[528,1536]{1,0:T(8,128)(2,1)}, bf16[512,1536]{1,0:T(8,128)(2,1)}) custom-call(s32[1]{0:T(128)} %bitcast.me_ref, bf16[512,26624]{1,0:T(8,128)(2,1)} %refs_0_.35, bf16[32,512]{1,0:T(8,128)(2,1)} %copy-done.3), custom_call_target="tpu_custom_call" | custom-call | bytes 2129920 | tf_op jit(solution)/shard_map/pallas_call | solution.py:78
  83.6 2.0 collective-permute-start.5
  85.9 9.8 %shard_map.65 = bf16[1024,6656]{1,0:T(8,128)(2,1)} custom-call(s32[1]{0:T(128)} %bitcast.me_ref, bf16[512,26624]{1,0:T(8,128)(2,1)} %refs_0_.35), custom_call_target="tpu_custom_call" | custom-call | bytes 9087658 | tf_op jit(solution)/shard_map/pallas_call | solution.py:78
  95.6 8.8 %all-to-all-start = ((bf16[2,512,6656]{2,1,0:T(8,128)(2,1)}), bf16[2,512,6656]{2,1,0:T(8,128)(2,1)}, u32[]{:S(2)}, u32[]{:S(2)}) async-start(bf16[2,512,6656]{2,1,0:T(8,128)(2,1)} %bitcast.26), calls=%async_computation | async-start | bytes 27262976 | tf_op jit(solution)/shard_map/all_to_all | solution.py:407
  104.5 11.2 %all-to-all-done = bf16[2,512,6656]{2,1,0:T(8,128)(2,1)} async-done(((bf16[2,512,6656]{2,1,0:T(8,128)(2,1)}), bf16[2,512,6656]{2,1,0:T(8,128)(2,1)}, u32[]{:S(2)}, u32[]{:S(2)}) %all-to-all-start) | async-done | bytes 13631520 | tf_op jit(solution)/shard_map/all_to_all | solution.py:407
  115.6 4.6 %shard_map.66 = f32[1,1536]{1,0:T(1,128)S(1)} custom-call(s32[1]{0:T(128)} %bitcast.me_ref, bf16[512,26624]{1,0:T(8,128)(2,1)} %refs_0_.35, bf16[1024,6656]{1,0:T(8,128)(2,1)} %bitcast.4.refs_1_, bf16[544,1536]{1,0:T(8,128)(2,1)} %copy-done.4, bf16[512,1536]{1,0:T(8,128)(2,1)} %collective-permute-done.1.refs_3_, bf16[64,512]{1,0:T(8,128)(2,1)S(1)} %bitcast.10, ...), custom_call_target="tpu_custom_call" | custom-call | flops 134217728 | bytes 2097152 | tf_op jit(solution)/shard_map/pallas_call | solution.py:249
  120.3 22.4 %psum.21.refs_9_ = f32[1,1536]{1,0:T(1,128)S(1)} all-reduce(f32[1,1536]{1,0:T(1,128)S(1)} %shard_map.66), channel_id=1, replica_groups=mesh['fsdp'=8,'tp'=4] {'fsdp'}, use_global_device_ids=true, to_apply=%region_0.1 | all-reduce | flops 1536 | bytes 12288 | tf_op jit(solution)/shard_map/psum | solution.py:471
  142.7 8.1 %shard_map.67 = (bf16[2048,6656]{1,0:T(8,128)(2,1)}, f32[16,52]{1,0:T(8,128)S(1)}) custom-call(s32[1]{0:T(128)} %bitcast.me_ref, bf16[512,26624]{1,0:T(8,128)(2,1)} %refs_0_.35, bf16[1024,6656]{1,0:T(8,128)(2,1)} %bitcast.4.refs_1_, bf16[544,1536]{1,0:T(8,128)(2,1)} %copy-done.4, bf16[512,1536]{1,0:T(8,128)(2,1)} %collective-permute-done.1.refs_3_, ...), custom_call_target="tpu_custom_call" | custom-call | flops 134217728 | bytes 4194304 | tf_op jit(solution)/shard_map/pallas_call | solution.py:355
  150.8 3.2 %shard_map.73 = (bf16[512,1536]{1,0:T(8,128)(2,1)}, bf16[512,1536]{1,0:T(8,128)(2,1)}) custom-call(s32[1]{0:T(128)} %bitcast.me_ref, bf16[512,26624]{1,0:T(8,128)(2,1)} %refs_0_.35), custom_call_target="tpu_custom_call" | custom-call | bytes 2097152 | tf_op jit(solution)/shard_map/pallas_call | solution.py:78
  155.6 4.6 %shard_map.68 = f32[1,1536]{1,0:T(1,128)S(1)} custom-call(s32[1]{0:T(128)} %bitcast.me_ref, bf16[512,26624]{1,0:T(8,128)(2,1)} %refs_0_.35, bf16[1024,6656]{1,0:T(8,128)(2,1)} %bitcast.4.refs_1_, bf16[512,1536]{1,0:T(8,128)(2,1)} %collective-permute-done.7.refs_2_, bf16[512,1536]{1,0:T(8,128)(2,1)} %collective-permute-done.8.refs_3_, ...), custom_call_target="tpu_custom_call" | custom-call | flops 134217728 | bytes 2097152 | tf_op jit(solution)/shard_map/pallas_call | solution.py:249
  160.2 17.4 %psum.22.refs_9_ = f32[1,1536]{1,0:T(1,128)S(1)} all-reduce(f32[1,1536]{1,0:T(1,128)S(1)} %shard_map.68), channel_id=1, replica_groups=mesh['fsdp'=8,'tp'=4] {'fsdp'}, use_global_device_ids=true, to_apply=%region_1.2 | all-reduce | flops 1536 | bytes 12288 | tf_op jit(solution)/shard_map/psum | solution.py:471
  177.6 8.1 %shard_map.69 = (bf16[2048,6656]{1,0:T(8,128)(2,1)}, f32[16,52]{1,0:T(8,128)S(1)}) custom-call(s32[1]{0:T(128)} %bitcast.me_ref, bf16[512,26624]{1,0:T(8,128)(2,1)} %refs_0_.35, bf16[1024,6656]{1,0:T(8,128)(2,1)} %bitcast.4.refs_1_, bf16[512,1536]{1,0:T(8,128)(2,1)} %collective-permute-done.7.refs_2_, ...), custom_call_target="tpu_custom_call", output_to_operand_aliasing={{0}: (12, {})} | custom-call | flops 134217728 | bytes 4194304 | tf_op jit(solution)/shard_map/pallas_call | solution.py:355
  185.8 26.1 %collective-permute-done.6.refs_3_ = bf16[512,1536]{1,0:T(8,128)(2,1)} collective-permute-done((bf16[512,1536]{1,0:T(8,128)(2,1)}, bf16[512,1536]{1,0:T(8,128)(2,1)}, u32[]{:S(2)}, u32[]{:S(2)}) %collective-permute-start.6) | collective-permute-done | bytes 1572896 | tf_op jit(solution)/shard_map/ppermute | solution.py:39
  217.6 4.6 %shard_map.72 = f32[1,1536]{1,0:T(1,128)S(1)} custom-call(s32[1]{0:T(128)} %bitcast.me_ref, bf16[512,26624]{1,0:T(8,128)(2,1)} %refs_0_.35, bf16[1024,6656]{1,0:T(8,128)(2,1)} %bitcast.4.refs_1_, bf16[528,1536]{1,0:T(8,128)(2,1)} %collective-permute-done.5.refs_2_, bf16[512,1536]{1,0:T(8,128)(2,1)} %collective-permute-done.6.refs_3_, ...), custom_call_target="tpu_custom_call" | custom-call | flops 134217728 | bytes 2097152 | tf_op jit(solution)/shard_map/pallas_call | solution.py:249
  223.0 22.3 %psum.23 = f32[1,2048]{1,0:T(1,128)S(1)} all-reduce(f32[1,2048]{1,0:T(1,128)S(1)} %pad_maximum_fusion.3), channel_id=1, replica_groups=mesh['fsdp'=8,'tp'=4] {'fsdp'}, use_global_device_ids=true, to_apply=%region_3.4 | all-reduce | flops 2048 | bytes 16384 | tf_op jit(solution)/shard_map/psum | solution.py:471
  245.4 8.1 %shard_map.74 = (bf16[2048,6656]{1,0:T(8,128)(2,1)}, f32[16,52]{1,0:T(8,128)S(1)}) custom-call(s32[1]{0:T(128)} %bitcast.me_ref, bf16[512,26624]{1,0:T(8,128)(2,1)} %refs_0_.35, bf16[1024,6656]{1,0:T(8,128)(2,1)} %bitcast.4.refs_1_, bf16[528,1536]{1,0:T(8,128)(2,1)} %collective-permute-done.5.refs_2_, ...), custom_call_target="tpu_custom_call", output_to_operand_aliasing={{0}: (12, {})} | custom-call | flops 134217728 | bytes 4194304 | tf_op jit(solution)/shard_map/pallas_call | solution.py:355
  253.5 3.3 %shard_map.75 = (bf16[2048,6656]{1,0:T(8,128)(2,1)}, f32[16,52]{1,0:T(8,128)S(1)}) custom-call(s32[1]{0:T(128)} %bitcast.me_ref, bf16[512,26624]{1,0:T(8,128)(2,1)} %refs_0_.35, bf16[1024,6656]{1,0:T(8,128)(2,1)} %bitcast.4.refs_1_, bf16[64,512]{1,0:T(8,128)(2,1)S(1)} %bitcast.16, ...), custom_call_target="tpu_custom_call", output_to_operand_aliasing={{0}: (8, {})} | custom-call | flops 22369620 | bytes 699050 | tf_op jit(solution)/shard_map/pallas_call | solution.py:355
  256.9 4.1 %shard_map.76.refs_3_ = f32[1,1536]{1,0:T(1,128)S(1)} custom-call(s32[1]{0:T(128)} %bitcast.me_ref, bf16[512,26624]{1,0:T(8,128)(2,1)} %refs_0_.35, bf16[1024,6656]{1,0:T(8,128)(2,1)} %bitcast.4.refs_1_, bf16[512,1536]{1,0:T(8,128)(2,1)} %collective-permute-done.12.refs_2_, bf16[64,512]{1,0:T(8,128)(2,1)S(1)} %bitcast.17, ...), custom_call_target="tpu_custom_call" | custom-call | flops 100663296 | bytes 1572864 | tf_op jit(solution)/shard_map/pallas_call | solution.py:249
  261.0 18.3 %collective-permute-done.13.refs_0_.refs_3_ = bf16[512,1536]{1,0:T(8,128)(2,1)} collective-permute-done((bf16[512,1536]{1,0:T(8,128)(2,1)}, bf16[512,1536]{1,0:T(8,128)(2,1)}, u32[]{:S(2)}, u32[]{:S(2)}) %collective-permute-start.13) | collective-permute-done | bytes 1572896 | tf_op jit(solution)/shard_map/ppermute | solution.py:39
  279.3 2.8 shard_map.77
  282.1 2.6 collective-permute-start.16
  288.8 2.7 collective-permute-start.17
  291.5 1.9 collective-permute-done.17
  293.4 8.2 %shard_map.78 = (bf16[2048,6656]{1,0:T(8,128)(2,1)}, f32[16,52]{1,0:T(8,128)S(1)}) custom-call(s32[1]{0:T(128)} %bitcast.me_ref, bf16[512,26624]{1,0:T(8,128)(2,1)} %refs_0_.35, bf16[1024,6656]{1,0:T(8,128)(2,1)} %bitcast.4.refs_1_, bf16[512,1536]{1,0:T(8,128)(2,1)} %collective-permute-done.12.refs_2_, ...), custom_call_target="tpu_custom_call", output_to_operand_aliasing={{0}: (12, {})} | custom-call | flops 134217728 | bytes 4194304 | tf_op jit(solution)/shard_map/pallas_call | solution.py:355
  (59 shorter events, 20.6 us)
Async XLA Ops:
  2.3 40.3 %collective-permute-start = (bf16[544,1536]{1,0:T(8,128)(2,1)S(1)}, bf16[544,1536]{1,0:T(8,128)(2,1)S(1)}, u32[]{:S(2)}, u32[]{:S(2)}) collective-permute-start(bf16[544,1536]{1,0:T(8,128)(2,1)S(1)} %shard_map.59), channel_id=1, source_target_pairs={{0,2},{1,3},{2,0},{3,1},{4,6},{5,7},{6,4},{7,5},{8,10},{9,11},{10,... | collective-permute-start | bytes 5013512 | tf_op jit(solution)/shard_map/ppermute | solution.py:39
  7.6 37.2 %copy-start = (bf16[64,6656]{1,0:T(8,128)(2,1)S(1)}, bf16[64,6656]{1,0:T(8,128)(2,1)}, u32[]{:S(2)}) copy-start(bf16[64,6656]{1,0:T(8,128)(2,1)} %refs_2_.9) | copy-start | bytes 2555908
  7.6 68.4 %copy-start.1 = (bf16[512,64]{0,1:T(8,128)(2,1)S(1)}, bf16[512,64]{0,1:T(8,128)(2,1)}, u32[]{:S(2)}) copy-start(bf16[512,64]{0,1:T(8,128)(2,1)} %param.5) | copy-start | bytes 196612
  7.6 68.4 %collective-permute-start.1 = (bf16[512,1536]{1,0:T(8,128)(2,1)}, bf16[512,1536]{1,0:T(8,128)(2,1)}, u32[]{:S(2)}, u32[]{:S(2)}) collective-permute-start(bf16[512,1536]{1,0:T(8,128)(2,1)} %shard_map.60), channel_id=1, source_target_pairs={{0,3},{1,2},{2,1},{3,0},{4,7},{5,6},{6,5},{7,4},{8,11},{9,10},{10,... | collective-permute-start | bytes 4718600 | tf_op jit(solution)/shard_map/ppermute | solution.py:39
  11.0 139.8 %collective-permute-start.7 = (bf16[512,1536]{1,0:T(8,128)(2,1)}, bf16[512,1536]{1,0:T(8,128)(2,1)}, u32[]{:S(2)}, u32[]{:S(2)}) collective-permute-start(bf16[512,1536]{1,0:T(8,128)(2,1)} %get-tuple-element.36), channel_id=1, source_target_pairs={{0,2},{1,3},{2,0},{3,1},{4,6},{5,7},{6,4},{7,5},{8,10},{9,11},{10,... | collective-permute-start | bytes 4718600 | tf_op jit(solution)/shard_map/ppermute | solution.py:39
  12.2 138.6 %collective-permute-start.8 = (bf16[512,1536]{1,0:T(8,128)(2,1)}, bf16[512,1536]{1,0:T(8,128)(2,1)}, u32[]{:S(2)}, u32[]{:S(2)}) collective-permute-start(bf16[512,1536]{1,0:T(8,128)(2,1)} %get-tuple-element.37), channel_id=1, source_target_pairs={{0,3},{1,2},{2,1},{3,0},{4,7},{5,6},{6,5},{7,4},{8,11},{9,10},{10,... | collective-permute-start | bytes 4718600 | tf_op jit(solution)/shard_map/ppermute | solution.py:39
  42.6 35.7 %copy-start.4 = (bf16[544,1536]{1,0:T(8,128)(2,1)}, bf16[544,1536]{1,0:T(8,128)(2,1)S(1)}, u32[]{:S(2)}) copy-start(bf16[544,1536]{1,0:T(8,128)(2,1)S(1)} %collective-permute-done.refs_2_) | copy-start | bytes 5013508
  42.7 4.0 %collective-permute-start.2 = (bf16[32,512]{1,0:T(8,128)(2,1)S(1)}, bf16[32,512]{1,0:T(8,128)(2,1)S(1)}, u32[]{:S(2)}, u32[]{:S(2)}) collective-permute-start(bf16[32,512]{1,0:T(8,128)(2,1)S(1)} %get-tuple-element.62), channel_id=1, source_target_pairs={{0,4},{4,0},{8,12},{12,8},{16,20},{20,16},{24,28},{28,24},{1,5},{5... | collective-permute-start | bytes 98312 | tf_op jit(solution)/shard_map/ppermute | solution.py:39
  46.7 29.3 %collective-permute-start.3 = (bf16[128,512]{1,0:T(8,128)(2,1)S(1)}, bf16[128,512]{1,0:T(8,128)(2,1)S(1)}, u32[]{:S(2)}, u32[]{:S(2)}) collective-permute-start(bf16[128,512]{1,0:T(8,128)(2,1)S(1)} %pad_maximum_fusion), channel_id=1, source_target_pairs={{0,1},{1,0},{2,3},{3,2},{4,5},{5,4},{6,7},{7,6},{8,9},{9,8},{10,11... | collective-permute-start | bytes 393224 | tf_op jit(solution)/shard_map/ppermute | solution.py:39
  78.4 1.2 collective-permute-start.4
  79.7 0.6 copy-start.3
  83.6 128.3 %collective-permute-start.5 = (bf16[528,1536]{1,0:T(8,128)(2,1)}, bf16[528,1536]{1,0:T(8,128)(2,1)}, u32[]{:S(2)}, u32[]{:S(2)}) collective-permute-start(bf16[528,1536]{1,0:T(8,128)(2,1)} %get-tuple-element.33), channel_id=1, source_target_pairs={{0,2},{1,3},{2,0},{3,1},{4,6},{5,7},{6,4},{7,5},{8,10},{9,11},{10,... | collective-permute-start | bytes 4866056 | tf_op jit(solution)/shard_map/ppermute | solution.py:39
  85.6 126.3 %collective-permute-start.6 = (bf16[512,1536]{1,0:T(8,128)(2,1)}, bf16[512,1536]{1,0:T(8,128)(2,1)}, u32[]{:S(2)}, u32[]{:S(2)}) collective-permute-start(bf16[512,1536]{1,0:T(8,128)(2,1)} %get-tuple-element.34), channel_id=1, source_target_pairs={{0,3},{1,2},{2,1},{3,0},{4,7},{5,6},{6,5},{7,4},{8,11},{9,10},{10,... | collective-permute-start | bytes 4718600 | tf_op jit(solution)/shard_map/ppermute | solution.py:39
  85.6 18.8 %collective-permute-start.9 = (bf16[128,512]{1,0:T(8,128)(2,1)S(1)}, bf16[128,512]{1,0:T(8,128)(2,1)S(1)}, u32[]{:S(2)}, u32[]{:S(2)}) collective-permute-start(bf16[128,512]{1,0:T(8,128)(2,1)S(1)} %pad_maximum_fusion.1), channel_id=1, source_target_pairs={{0,1},{1,0},{2,3},{3,2},{4,5},{5,4},{6,7},{7,6},{8,9},{9,8},{10,11... | collective-permute-start | bytes 393224 | tf_op jit(solution)/shard_map/ppermute | solution.py:39
  95.6 20.0 %all-to-all-start = ((bf16[2,512,6656]{2,1,0:T(8,128)(2,1)}), bf16[2,512,6656]{2,1,0:T(8,128)(2,1)}, u32[]{:S(2)}, u32[]{:S(2)}) async-start(bf16[2,512,6656]{2,1,0:T(8,128)(2,1)} %bitcast.26), calls=%async_computation | async-start | bytes 27262976 | tf_op jit(solution)/shard_map/all_to_all | solution.py:407
  115.6 27.0 %copy-start.2 = (f32[26624]{0:T(1024)S(1)}, f32[26624]{0:T(1024)}, u32[]{:S(2)}) copy-start(f32[26624]{0:T(1024)} %param.7) | copy-start | bytes 319492
  154.0 102.9 %collective-permute-start.12 = (bf16[512,1536]{1,0:T(8,128)(2,1)}, bf16[512,1536]{1,0:T(8,128)(2,1)}, u32[]{:S(2)}, u32[]{:S(2)}) collective-permute-start(bf16[512,1536]{1,0:T(8,128)(2,1)} %get-tuple-element.48), channel_id=1, source_target_pairs={{0,2},{1,3},{2,0},{3,1},{4,6},{5,7},{6,4},{7,5},{8,10},{9,11},{10,... | collective-permute-start | bytes 4718600 | tf_op jit(solution)/shard_map/ppermute | solution.py:39
  155.6 123.8 %collective-permute-start.13 = (bf16[512,1536]{1,0:T(8,128)(2,1)}, bf16[512,1536]{1,0:T(8,128)(2,1)}, u32[]{:S(2)}, u32[]{:S(2)}) collective-permute-start(bf16[512,1536]{1,0:T(8,128)(2,1)} %get-tuple-element.49), channel_id=1, source_target_pairs={{0,3},{1,2},{2,1},{3,0},{4,7},{5,6},{6,5},{7,4},{8,11},{9,10},{10,... | collective-permute-start | bytes 4718600 | tf_op jit(solution)/shard_map/ppermute | solution.py:39
  213.7 87.8 %collective-permute-start.11 = (bf16[512,512]{1,0:T(8,128)(2,1)}, bf16[512,512]{1,0:T(8,128)(2,1)S(1)}, u32[]{:S(2)}, u32[]{:S(2)}) collective-permute-start(bf16[512,512]{1,0:T(8,128)(2,1)} %shard_map.70), channel_id=1, source_target_pairs={{0,2},{1,3},{2,0},{3,1},{4,6},{5,7},{6,4},{7,5},{8,10},{9,11},{10,... | collective-permute-start | bytes 1572872 | tf_op jit(solution)/shard_map/ppermute | solution.py:39
  215.8 87.1 %collective-permute-start.10 = (bf16[512,512]{1,0:T(8,128)(2,1)}, bf16[512,512]{1,0:T(8,128)(2,1)S(1)}, u32[]{:S(2)}, u32[]{:S(2)}) collective-permute-start(bf16[512,512]{1,0:T(8,128)(2,1)} %shard_map.71), channel_id=1, source_target_pairs={{0,3},{1,2},{2,1},{3,0},{4,7},{5,6},{6,5},{7,4},{8,11},{9,10},{10,... | collective-permute-start | bytes 1572872 | tf_op jit(solution)/shard_map/ppermute | solution.py:39
  282.1 4.6 %collective-permute-start.16 = (f32[1,1536]{1,0:T(1,128)S(1)}, f32[1,1536]{1,0:T(1,128)S(1)}, u32[]{:S(2)}, u32[]{:S(2)}) collective-permute-start(f32[1,1536]{1,0:T(1,128)S(1)} %shard_map.77), channel_id=1, source_target_pairs={{0,12},{4,8},{8,4},{12,0},{16,28},{20,24},{24,20},{28,16},{1,13},{... | collective-permute-start | bytes 18440 | tf_op jit(solution)/shard_map/ppermute | solution.py:39
  284.7 3.6 %collective-permute-start.15 = (f32[1,1536]{1,0:T(1,128)S(1)}, f32[1,1536]{1,0:T(1,128)S(1)}, u32[]{:S(2)}, u32[]{:S(2)}) collective-permute-start(f32[1,1536]{1,0:T(1,128)S(1)} %shard_map.77), channel_id=1, source_target_pairs={{0,8},{4,12},{8,0},{12,4},{16,24},{20,28},{24,16},{28,20},{1,9},{5... | collective-permute-start | bytes 18440 | tf_op jit(solution)/shard_map/ppermute | solution.py:39
  285.2 3.6 %collective-permute-start.14 = (f32[1,1536]{1,0:T(1,128)S(1)}, f32[1,1536]{1,0:T(1,128)S(1)}, u32[]{:S(2)}, u32[]{:S(2)}) collective-permute-start(f32[1,1536]{1,0:T(1,128)S(1)} %shard_map.77), channel_id=1, source_target_pairs={{0,4},{4,0},{8,12},{12,8},{16,20},{20,16},{24,28},{28,24},{1,5},{5... | collective-permute-start | bytes 18440 | tf_op jit(solution)/shard_map/ppermute | solution.py:39
  288.8 4.6 %collective-permute-start.17 = (f32[1,1536]{1,0:T(1,128)S(1)}, f32[1,1536]{1,0:T(1,128)S(1)}, u32[]{:S(2)}, u32[]{:S(2)}) collective-permute-start(f32[1,1536]{1,0:T(1,128)S(1)} %add_add_fusion), channel_id=1, source_target_pairs={{0,16},{4,20},{8,24},{12,28},{16,0},{20,4},{24,8},{28,12},{1,17},{... | collective-permute-start | bytes 18440 | tf_op jit(solution)/shard_map/ppermute | solution.py:39

commit v8 on v7

--- a/solution.py
+++ b/solution.py
@@ -9,7 +9,7 @@
 
 BLOCK = 128
 EPSILON = 1e-06
-EARLY = (12, 12, 12, 12)
+EARLY = (12, 12, 12, 6, 6)
 LATE = (4,)
 AHEAD = 2
 SCALE = 3

time: 305 us -> 312 us (1.023)
  blocking collectives: 62.1 us -> 79.2 us
  waiting for transfers between devices: 123 us -> 107 us
  Pallas kernels: 88.7 us -> 94 us
    psum x3 -> x4, blocking collectives: 62.1 us -> 79.2 us  [body(): lax.psum(local, 'fsdp')]
    ppermute x18 -> x20, waiting for transfers between devices: 111 us -> 96 us  [swap(): return lax.ppermute(array, axis, [(i, i ^ d) for i in range(size)])]
    pallas_call x7 -> x8, Pallas kernels: 38.5 us -> 41.1 us  [export_chunk(): pl.pallas_call(functools.partial(export_kernel, tp, ds, first), out_shape...]
    pallas_call x8 -> x9, Pallas kernels: 27.1 us -> 29.3 us  [move(): pl.pallas_call(functools.partial(move_kernel, moves, len(arrays), direct)...]
    ppermute x18 -> x20, starting transfers between devices: 19.5 us -> 19 us  [swap(): return lax.ppermute(array, axis, [(i, i ^ d) for i in range(size)])]
    pallas_call x5 -> x6, Pallas kernels: 20.8 us -> 21.3 us  [column_squares(): pl.pallas_call(functools.partial(squares_kernel, len(ds)), out_shape=jax....]
  transfers between devices with their start and end apart: 19 -> 21, of which waited for: 11 -> 10; matrix products, arithmetic and copies ran while one was open for 0% -> 0% of each run, Pallas kernels for 28% -> 29%
where the time goes in v8:
time: 312 us; the launch traced here: 311 us
  waiting for transfers between devices  107 us (34%)
  Pallas kernels  94 us (30%)
  blocking collectives  79.2 us (25%)
  starting transfers between devices  27.7 us (9%)
    ppermute x20, waiting for transfers between devices, swap(): return lax.ppermute(array, axis, [(i, i ^ d) for i in range(size)])  96 us
    psum x4, blocking collectives, body(): lax.psum(local, 'fsdp')  79.2 us
    pallas_call x8, Pallas kernels, export_chunk(): pl.pallas_call(functools.partial(export_kernel, tp, ds, first), out_shape...  41.1 us
    pallas_call x9, Pallas kernels, move(): pl.pallas_call(functools.partial(move_kernel, moves, len(arrays), direct)...  29.3 us
    pallas_call x6, Pallas kernels, column_squares(): pl.pallas_call(functools.partial(squares_kernel, len(ds)), out_shape=jax....  21.3 us
    ppermute x20, starting transfers between devices, swap(): return lax.ppermute(array, axis, [(i, i ^ d) for i in range(size)])  19 us
    all_to_all x1, waiting for transfers between devices, body(): lax.all_to_all(pack_near(after(me, *pieces), base, tp), 'tp', 0, 0, tiled...  11.2 us
    all_to_all x1, starting transfers between devices, body(): lax.all_to_all(pack_near(after(me, *pieces), base, tp), 'tp', 0, 0, tiled...  8.75 us
  transfers between devices with their start and end apart: 21, of which 10 were waited for; matrix products, arithmetic and copies ran while one was open for 0% of the time, Pallas kernels for 29%

profile of v8, /device:TPU:0, one launch (start us, length us, event | category | flops | bytes accessed | tf_op | source)
XLA Modules:
  0.0 310.6 jit_solution(8350619012527988567)
XLA Ops:
  2.3 3.0 collective-permute-start.2
  5.3 2.3 shard_map.60
  7.7 34.9 %collective-permute-done.2.refs_2_ = bf16[544,1536]{1,0:T(8,128)(2,1)S(1)} collective-permute-done((bf16[544,1536]{1,0:T(8,128)(2,1)S(1)}, bf16[544,1536]{1,0:T(8,128)(2,1)S(1)}, u32[]{:S(2)}, u32[]{:S(2)}) %collective-permute-start.2) | collective-permute-done | bytes 1671200 | tf_op jit(solution)/shard_map/ppermute | solution.py:39
  42.7 2.2 collective-permute-start.7
  46.8 3.2 %shard_map.61 = (bf16[512,1536]{1,0:T(8,128)(2,1)}, bf16[512,1536]{1,0:T(8,128)(2,1)}) custom-call(s32[1]{0:T(128)} %bitcast.me_ref, bf16[512,26624]{1,0:T(8,128)(2,1)} %refs_0_.41), custom_call_target="tpu_custom_call" | custom-call | bytes 2097152 | tf_op jit(solution)/shard_map/pallas_call | solution.py:78
  50.1 2.1 collective-permute-start
  52.3 23.7 %collective-permute-done.3.refs_3_ = bf16[512,1536]{1,0:T(8,128)(2,1)} collective-permute-done((bf16[512,1536]{1,0:T(8,128)(2,1)}, bf16[512,1536]{1,0:T(8,128)(2,1)}, u32[]{:S(2)}, u32[]{:S(2)}) %collective-permute-start.3) | collective-permute-done | bytes 1572896 | tf_op jit(solution)/shard_map/ppermute | solution.py:39
  76.1 2.3 shard_map.66
  80.3 3.2 %shard_map.68 = (bf16[528,1536]{1,0:T(8,128)(2,1)}, bf16[512,1536]{1,0:T(8,128)(2,1)}) custom-call(s32[1]{0:T(128)} %bitcast.me_ref, bf16[512,26624]{1,0:T(8,128)(2,1)} %refs_0_.41, bf16[32,512]{1,0:T(8,128)(2,1)} %copy-done.5), custom_call_target="tpu_custom_call" | custom-call | bytes 2129920 | tf_op jit(solution)/shard_map/pallas_call | solution.py:78
  85.8 9.8 %shard_map.62 = bf16[1024,6656]{1,0:T(8,128)(2,1)} custom-call(s32[1]{0:T(128)} %bitcast.me_ref, bf16[512,26624]{1,0:T(8,128)(2,1)} %refs_0_.41), custom_call_target="tpu_custom_call" | custom-call | bytes 9087658 | tf_op jit(solution)/shard_map/pallas_call | solution.py:78
  95.6 8.7 %all-to-all-start = ((bf16[2,512,6656]{2,1,0:T(8,128)(2,1)}), bf16[2,512,6656]{2,1,0:T(8,128)(2,1)}, u32[]{:S(2)}, u32[]{:S(2)}) async-start(bf16[2,512,6656]{2,1,0:T(8,128)(2,1)} %bitcast.29), calls=%async_computation | async-start | bytes 27262976 | tf_op jit(solution)/shard_map/all_to_all | solution.py:407
  104.4 11.2 %all-to-all-done = bf16[2,512,6656]{2,1,0:T(8,128)(2,1)} async-done(((bf16[2,512,6656]{2,1,0:T(8,128)(2,1)}), bf16[2,512,6656]{2,1,0:T(8,128)(2,1)}, u32[]{:S(2)}, u32[]{:S(2)}) %all-to-all-start) | async-done | bytes 13631520 | tf_op jit(solution)/shard_map/all_to_all | solution.py:407
  115.6 4.6 %shard_map.63 = f32[1,1536]{1,0:T(1,128)S(1)} custom-call(s32[1]{0:T(128)} %bitcast.me_ref, bf16[512,26624]{1,0:T(8,128)(2,1)} %refs_0_.41, bf16[1024,6656]{1,0:T(8,128)(2,1)} %bitcast.4.refs_1_, bf16[544,1536]{1,0:T(8,128)(2,1)} %copy-done.6, bf16[512,1536]{1,0:T(8,128)(2,1)} %collective-permute-done.3.refs_3_, bf16[64,512]{1,0:T(8,128)(2,1)S(1)} %bitcast.10, ...), custom_call_target="tpu_custom_call" | custom-call | flops 134217728 | bytes 2097152 | tf_op jit(solution)/shard_map/pallas_call | solution.py:249
  120.2 22.4 %psum.28.refs_9_ = f32[1,1536]{1,0:T(1,128)S(1)} all-reduce(f32[1,1536]{1,0:T(1,128)S(1)} %shard_map.63), channel_id=1, replica_groups=mesh['fsdp'=8,'tp'=4] {'fsdp'}, use_global_device_ids=true, to_apply=%region_0.1 | all-reduce | flops 1536 | bytes 12288 | tf_op jit(solution)/shard_map/psum | solution.py:471
  142.6 8.1 %shard_map.64 = (bf16[2048,6656]{1,0:T(8,128)(2,1)}, f32[16,52]{1,0:T(8,128)S(1)}) custom-call(s32[1]{0:T(128)} %bitcast.me_ref, bf16[512,26624]{1,0:T(8,128)(2,1)} %refs_0_.41, bf16[1024,6656]{1,0:T(8,128)(2,1)} %bitcast.4.refs_1_, bf16[544,1536]{1,0:T(8,128)(2,1)} %copy-done.6, bf16[512,1536]{1,0:T(8,128)(2,1)} %collective-permute-done.3.refs_3_, ...), custom_call_target="tpu_custom_call" | custom-call | flops 134217728 | bytes 4194304 | tf_op jit(solution)/shard_map/pallas_call | solution.py:355
  150.7 3.0 shard_map.65
  155.3 4.6 %shard_map.69 = f32[1,1536]{1,0:T(1,128)S(1)} custom-call(s32[1]{0:T(128)} %bitcast.me_ref, bf16[512,26624]{1,0:T(8,128)(2,1)} %refs_0_.41, bf16[1024,6656]{1,0:T(8,128)(2,1)} %bitcast.4.refs_1_, bf16[512,1536]{1,0:T(8,128)(2,1)} %copy-done.7, bf16[512,1536]{1,0:T(8,128)(2,1)} %collective-permute-done.1.refs_3_, bf16[64,512]{1,0:T(8,128)(2,1)S(1)} %bitcast.12, ...), custom_call_target="tpu_custom_call" | custom-call | flops 134217728 | bytes 2097152 | tf_op jit(solution)/shard_map/pallas_call | solution.py:249
  159.9 17.4 %psum.29.refs_9_ = f32[1,1536]{1,0:T(1,128)S(1)} all-reduce(f32[1,1536]{1,0:T(1,128)S(1)} %shard_map.69), channel_id=1, replica_groups=mesh['fsdp'=8,'tp'=4] {'fsdp'}, use_global_device_ids=true, to_apply=%region_1.2 | all-reduce | flops 1536 | bytes 12288 | tf_op jit(solution)/shard_map/psum | solution.py:471
  177.3 8.2 %shard_map.70 = (bf16[2048,6656]{1,0:T(8,128)(2,1)}, f32[16,52]{1,0:T(8,128)S(1)}) custom-call(s32[1]{0:T(128)} %bitcast.me_ref, bf16[512,26624]{1,0:T(8,128)(2,1)} %refs_0_.41, bf16[1024,6656]{1,0:T(8,128)(2,1)} %bitcast.4.refs_1_, bf16[512,1536]{1,0:T(8,128)(2,1)} %copy-done.7, ...), custom_call_target="tpu_custom_call", output_to_operand_aliasing={{0}: (12, {})} | custom-call | flops 134217728 | bytes 4194304 | tf_op jit(solution)/shard_map/pallas_call | solution.py:355
  185.5 26.4 %collective-permute-done.11.refs_3_ = bf16[512,1536]{1,0:T(8,128)(2,1)} collective-permute-done((bf16[512,1536]{1,0:T(8,128)(2,1)}, bf16[512,1536]{1,0:T(8,128)(2,1)}, u32[]{:S(2)}, u32[]{:S(2)}) %collective-permute-start.11) | collective-permute-done | bytes 1572896 | tf_op jit(solution)/shard_map/ppermute | solution.py:39
  211.9 2.5 shard_map.75
  217.2 4.7 %shard_map.71 = f32[1,1536]{1,0:T(1,128)S(1)} custom-call(s32[1]{0:T(128)} %bitcast.me_ref, bf16[512,26624]{1,0:T(8,128)(2,1)} %refs_0_.41, bf16[1024,6656]{1,0:T(8,128)(2,1)} %bitcast.4.refs_1_, bf16[528,1536]{1,0:T(8,128)(2,1)} %collective-permute-done.10.refs_2_, bf16[512,1536]{1,0:T(8,128)(2,1)} %collective-permute-done.11.refs_3_, ...), custom_call_target="tpu_custom_call" | custom-call | flops 134217728 | bytes 2097152 | tf_op jit(solution)/shard_map/pallas_call | solution.py:249
  221.9 22.1 %psum.30 = f32[1,2048]{1,0:T(1,128)S(1)} all-reduce(f32[1,2048]{1,0:T(1,128)S(1)} %pad_maximum_fusion.3), channel_id=1, replica_groups=mesh['fsdp'=8,'tp'=4] {'fsdp'}, use_global_device_ids=true, to_apply=%region_3.4 | all-reduce | flops 2048 | bytes 16384 | tf_op jit(solution)/shard_map/psum | solution.py:471
  244.0 8.2 %shard_map.72 = (bf16[2048,6656]{1,0:T(8,128)(2,1)}, f32[16,52]{1,0:T(8,128)S(1)}) custom-call(s32[1]{0:T(128)} %bitcast.me_ref, bf16[512,26624]{1,0:T(8,128)(2,1)} %refs_0_.41, bf16[1024,6656]{1,0:T(8,128)(2,1)} %bitcast.4.refs_1_, bf16[528,1536]{1,0:T(8,128)(2,1)} %collective-permute-done.10.refs_2_, ...), custom_call_target="tpu_custom_call", output_to_operand_aliasing={{0}: (12, {})} | custom-call | flops 134217728 | bytes 4194304 | tf_op jit(solution)/shard_map/pallas_call | solution.py:355
  257.5 3.5 %shard_map.76 = f32[1,768]{1,0:T(1,128)S(1)} custom-call(s32[1]{0:T(128)} %bitcast.me_ref, bf16[512,26624]{1,0:T(8,128)(2,1)} %refs_0_.41, bf16[1024,6656]{1,0:T(8,128)(2,1)} %bitcast.4.refs_1_, bf16[512,768]{1,0:T(8,128)(2,1)} %collective-permute-done.5.refs_2_, bf16[512,768]{1,0:T(8,128)(2,1)} %collective-permute-done.6.refs_3_, ...), custom_call_target="tpu_custom_call" | custom-call | flops 67108864 | bytes 1048576 | tf_op jit(solution)/shard_map/pallas_call | solution.py:249
  261.0 17.3 %psum.31.refs_9_ = f32[1,768]{1,0:T(1,128)S(1)} all-reduce(f32[1,768]{1,0:T(1,128)S(1)} %shard_map.76), channel_id=1, replica_groups=mesh['fsdp'=8,'tp'=4] {'fsdp'}, use_global_device_ids=true, to_apply=%region_4.5 | all-reduce | flops 768 | bytes 6144 | tf_op jit(solution)/shard_map/psum | solution.py:471
  278.3 5.5 %shard_map.77 = (bf16[2048,6656]{1,0:T(8,128)(2,1)}, f32[16,52]{1,0:T(8,128)S(1)}) custom-call(s32[1]{0:T(128)} %bitcast.me_ref, bf16[512,26624]{1,0:T(8,128)(2,1)} %refs_0_.41, bf16[1024,6656]{1,0:T(8,128)(2,1)} %bitcast.4.refs_1_, bf16[512,768]{1,0:T(8,128)(2,1)} %collective-permute-done.5.refs_2_, ...), custom_call_target="tpu_custom_call", output_to_operand_aliasing={{0}: (12, {})} | custom-call | flops 67108864 | bytes 2097152 | tf_op jit(solution)/shard_map/pallas_call | solution.py:355
  283.8 3.3 %shard_map.78 = (bf16[2048,6656]{1,0:T(8,128)(2,1)}, f32[16,52]{1,0:T(8,128)S(1)}) custom-call(s32[1]{0:T(128)} %bitcast.me_ref, bf16[512,26624]{1,0:T(8,128)(2,1)} %refs_0_.41, bf16[1024,6656]{1,0:T(8,128)(2,1)} %bitcast.4.refs_1_, bf16[64,512]{1,0:T(8,128)(2,1)S(1)} %bitcast.18, ...), custom_call_target="tpu_custom_call", output_to_operand_aliasing={{0}: (8, {})} | custom-call | flops 22369620 | bytes 699050 | tf_op jit(solution)/shard_map/pallas_call | solution.py:355
  287.2 3.0 shard_map.79.refs_3_
  291.3 3.3 %collective-permute-start.17 = (f32[1,768]{1,0:T(1,128)S(1)}, f32[1,768]{1,0:T(1,128)S(1)}, u32[]{:S(2)}, u32[]{:S(2)}) collective-permute-start(f32[1,768]{1,0:T(1,128)S(1)} %shard_map.80), channel_id=1, source_target_pairs={{0,8},{4,12},{8,0},{12,4},{16,24},{20,28},{24,16},{28,20},{1,9},{5... | collective-permute-start | bytes 9224 | tf_op jit(solution)/shard_map/ppermute | solution.py:39
  298.3 4.5 %collective-permute-done.19 = f32[1,768]{1,0:T(1,128)S(1)} collective-permute-done((f32[1,768]{1,0:T(1,128)S(1)}, f32[1,768]{1,0:T(1,128)S(1)}, u32[]{:S(2)}, u32[]{:S(2)}) %collective-permute-start.19) | collective-permute-done | bytes 3104 | tf_op jit(solution)/shard_map/ppermute | solution.py:39
  302.8 5.2 %shard_map.81 = (bf16[2048,6656]{1,0:T(8,128)(2,1)}, f32[16,52]{1,0:T(8,128)S(1)}) custom-call(s32[1]{0:T(128)} %bitcast.me_ref, bf16[512,26624]{1,0:T(8,128)(2,1)} %refs_0_.41, bf16[1024,6656]{1,0:T(8,128)(2,1)} %bitcast.4.refs_1_, bf16[512,768]{1,0:T(8,128)(2,1)S(1)} %collective-permute-done.14.refs_2_, ...), custom_call_target="tpu_custom_call", output_to_operand_aliasing={{0}: (12, {})} | custom-call | flops 67108864 | bytes 2097152 | tf_op jit(solution)/shard_map/pallas_call | solution.py:355
  (73 shorter events, 25.3 us)
Async XLA Ops:
  2.3 42.5 %copy-start = (bf16[64,6656]{1,0:T(8,128)(2,1)S(1)}, bf16[64,6656]{1,0:T(8,128)(2,1)}, u32[]{:S(2)}) copy-start(bf16[64,6656]{1,0:T(8,128)(2,1)} %refs_2_.9) | copy-start | bytes 2555908
  2.3 40.3 %collective-permute-start.2 = (bf16[544,1536]{1,0:T(8,128)(2,1)S(1)}, bf16[544,1536]{1,0:T(8,128)(2,1)S(1)}, u32[]{:S(2)}, u32[]{:S(2)}) collective-permute-start(bf16[544,1536]{1,0:T(8,128)(2,1)S(1)} %shard_map.59), channel_id=1, source_target_pairs={{0,2},{1,3},{2,0},{3,1},{4,6},{5,7},{6,4},{7,5},{8,10},{9,11},{10,... | collective-permute-start | bytes 5013512 | tf_op jit(solution)/shard_map/ppermute | solution.py:39
  7.6 68.4 %collective-permute-start.3 = (bf16[512,1536]{1,0:T(8,128)(2,1)}, bf16[512,1536]{1,0:T(8,128)(2,1)}, u32[]{:S(2)}, u32[]{:S(2)}) collective-permute-start(bf16[512,1536]{1,0:T(8,128)(2,1)} %shard_map.60), channel_id=1, source_target_pairs={{0,3},{1,2},{2,1},{3,0},{4,7},{5,6},{6,5},{7,4},{8,11},{9,10},{10,... | collective-permute-start | bytes 4718600 | tf_op jit(solution)/shard_map/ppermute | solution.py:39
  42.7 7.4 %copy-start.6 = (bf16[544,1536]{1,0:T(8,128)(2,1)}, bf16[544,1536]{1,0:T(8,128)(2,1)S(1)}, u32[]{:S(2)}) copy-start(bf16[544,1536]{1,0:T(8,128)(2,1)S(1)} %collective-permute-done.2.refs_2_) | copy-start | bytes 5013508
  42.7 4.0 %collective-permute-start.7 = (bf16[32,512]{1,0:T(8,128)(2,1)S(1)}, bf16[32,512]{1,0:T(8,128)(2,1)S(1)}, u32[]{:S(2)}, u32[]{:S(2)}) collective-permute-start(bf16[32,512]{1,0:T(8,128)(2,1)S(1)} %get-tuple-element.72), channel_id=1, source_target_pairs={{0,4},{4,0},{8,12},{12,8},{16,20},{20,16},{24,28},{28,24},{1,5},{5... | collective-permute-start | bytes 98312 | tf_op jit(solution)/shard_map/ppermute | solution.py:39
  46.8 29.3 %copy-start.3 = (bf16[512,64]{0,1:T(8,128)(2,1)S(1)}, bf16[512,64]{0,1:T(8,128)(2,1)}, u32[]{:S(2)}) copy-start(bf16[512,64]{0,1:T(8,128)(2,1)} %param.5) | copy-start | bytes 196612
  46.8 29.3 %collective-permute-start.8 = (bf16[128,512]{1,0:T(8,128)(2,1)S(1)}, bf16[128,512]{1,0:T(8,128)(2,1)S(1)}, u32[]{:S(2)}, u32[]{:S(2)}) collective-permute-start(bf16[128,512]{1,0:T(8,128)(2,1)S(1)} %pad_maximum_fusion.1), channel_id=1, source_target_pairs={{0,1},{1,0},{2,3},{3,2},{4,5},{5,4},{6,7},{7,6},{8,9},{9,8},{10,11... | collective-permute-start | bytes 393224 | tf_op jit(solution)/shard_map/ppermute | solution.py:39
  50.1 100.6 %collective-permute-start = (bf16[512,1536]{1,0:T(8,128)(2,1)}, bf16[512,1536]{1,0:T(8,128)(2,1)S(1)}, u32[]{:S(2)}, u32[]{:S(2)}) collective-permute-start(bf16[512,1536]{1,0:T(8,128)(2,1)} %get-tuple-element.39), channel_id=1, source_target_pairs={{0,2},{1,3},{2,0},{3,1},{4,6},{5,7},{6,4},{7,5},{8,10},{9,11},{10,... | collective-permute-start | bytes 4718600 | tf_op jit(solution)/shard_map/ppermute | solution.py:39
  52.1 98.6 %collective-permute-start.1 = (bf16[512,1536]{1,0:T(8,128)(2,1)}, bf16[512,1536]{1,0:T(8,128)(2,1)}, u32[]{:S(2)}, u32[]{:S(2)}) collective-permute-start(bf16[512,1536]{1,0:T(8,128)(2,1)} %get-tuple-element.40), channel_id=1, source_target_pairs={{0,3},{1,2},{2,1},{3,0},{4,7},{5,6},{6,5},{7,4},{8,11},{9,10},{10,... | collective-permute-start | bytes 4718600 | tf_op jit(solution)/shard_map/ppermute | solution.py:39
  78.4 1.2 collective-permute-start.9
  79.7 0.6 copy-start.5
  83.5 128.4 %collective-permute-start.10 = (bf16[528,1536]{1,0:T(8,128)(2,1)}, bf16[528,1536]{1,0:T(8,128)(2,1)}, u32[]{:S(2)}, u32[]{:S(2)}) collective-permute-start(bf16[528,1536]{1,0:T(8,128)(2,1)} %get-tuple-element.47), channel_id=1, source_target_pairs={{0,2},{1,3},{2,0},{3,1},{4,6},{5,7},{6,4},{7,5},{8,10},{9,11},{10,... | collective-permute-start | bytes 4866056 | tf_op jit(solution)/shard_map/ppermute | solution.py:39
  85.5 126.4 %collective-permute-start.11 = (bf16[512,1536]{1,0:T(8,128)(2,1)}, bf16[512,1536]{1,0:T(8,128)(2,1)}, u32[]{:S(2)}, u32[]{:S(2)}) collective-permute-start(bf16[512,1536]{1,0:T(8,128)(2,1)} %get-tuple-element.48), channel_id=1, source_target_pairs={{0,3},{1,2},{2,1},{3,0},{4,7},{5,6},{6,5},{7,4},{8,11},{9,10},{10,... | collective-permute-start | bytes 4718600 | tf_op jit(solution)/shard_map/ppermute | solution.py:39
  85.6 18.8 %collective-permute-start.4 = (bf16[128,512]{1,0:T(8,128)(2,1)S(1)}, bf16[128,512]{1,0:T(8,128)(2,1)S(1)}, u32[]{:S(2)}, u32[]{:S(2)}) collective-permute-start(bf16[128,512]{1,0:T(8,128)(2,1)S(1)} %pad_maximum_fusion), channel_id=1, source_target_pairs={{0,1},{1,0},{2,3},{3,2},{4,5},{5,4},{6,7},{7,6},{8,9},{9,8},{10,11... | collective-permute-start | bytes 393224 | tf_op jit(solution)/shard_map/ppermute | solution.py:39
  95.6 20.0 %all-to-all-start = ((bf16[2,512,6656]{2,1,0:T(8,128)(2,1)}), bf16[2,512,6656]{2,1,0:T(8,128)(2,1)}, u32[]{:S(2)}, u32[]{:S(2)}) async-start(bf16[2,512,6656]{2,1,0:T(8,128)(2,1)} %bitcast.29), calls=%async_computation | async-start | bytes 27262976 | tf_op jit(solution)/shard_map/all_to_all | solution.py:407
  115.6 27.0 %copy-start.4 = (f32[26624]{0:T(1024)S(1)}, f32[26624]{0:T(1024)}, u32[]{:S(2)}) copy-start(f32[26624]{0:T(1024)} %param.7) | copy-start | bytes 319492
  150.7 3.0 copy-start.7
  153.7 98.4 %collective-permute-start.5 = (bf16[512,768]{1,0:T(8,128)(2,1)}, bf16[512,768]{1,0:T(8,128)(2,1)}, u32[]{:S(2)}, u32[]{:S(2)}) collective-permute-start(bf16[512,768]{1,0:T(8,128)(2,1)} %get-tuple-element.44), channel_id=1, source_target_pairs={{0,2},{1,3},{2,0},{3,1},{4,6},{5,7},{6,4},{7,5},{8,10},{9,11},{10,... | collective-permute-start | bytes 2359304 | tf_op jit(solution)/shard_map/ppermute | solution.py:39
  155.3 96.9 %collective-permute-start.6 = (bf16[512,768]{1,0:T(8,128)(2,1)}, bf16[512,768]{1,0:T(8,128)(2,1)}, u32[]{:S(2)}, u32[]{:S(2)}) collective-permute-start(bf16[512,768]{1,0:T(8,128)(2,1)} %get-tuple-element.45), channel_id=1, source_target_pairs={{0,3},{1,2},{2,1},{3,0},{4,7},{5,6},{6,5},{7,4},{8,11},{9,10},{10,... | collective-permute-start | bytes 2359304 | tf_op jit(solution)/shard_map/ppermute | solution.py:39
  214.4 72.7 %collective-permute-start.14 = (bf16[512,768]{1,0:T(8,128)(2,1)}, bf16[512,768]{1,0:T(8,128)(2,1)S(1)}, u32[]{:S(2)}, u32[]{:S(2)}) collective-permute-start(bf16[512,768]{1,0:T(8,128)(2,1)} %get-tuple-element.59), channel_id=1, source_target_pairs={{0,2},{1,3},{2,0},{3,1},{4,6},{5,7},{6,4},{7,5},{8,10},{9,11},{10,... | collective-permute-start | bytes 2359304 | tf_op jit(solution)/shard_map/ppermute | solution.py:39
  214.7 75.5 %collective-permute-start.15 = (bf16[512,768]{1,0:T(8,128)(2,1)}, bf16[512,768]{1,0:T(8,128)(2,1)S(1)}, u32[]{:S(2)}, u32[]{:S(2)}) collective-permute-start(bf16[512,768]{1,0:T(8,128)(2,1)} %get-tuple-element.60), channel_id=1, source_target_pairs={{0,3},{1,2},{2,1},{3,0},{4,7},{5,6},{6,5},{7,4},{8,11},{9,10},{10,... | collective-permute-start | bytes 2359304 | tf_op jit(solution)/shard_map/ppermute | solution.py:39
  254.0 54.0 %collective-permute-start.13 = (bf16[512,512]{1,0:T(8,128)(2,1)}, bf16[512,512]{1,0:T(8,128)(2,1)S(1)}, u32[]{:S(2)}, u32[]{:S(2)}) collective-permute-start(bf16[512,512]{1,0:T(8,128)(2,1)} %shard_map.73), channel_id=1, source_target_pairs={{0,2},{1,3},{2,0},{3,1},{4,6},{5,7},{6,4},{7,5},{8,10},{9,11},{10,... | collective-permute-start | bytes 1572872 | tf_op jit(solution)/shard_map/ppermute | solution.py:39
  257.4 51.9 %collective-permute-start.12 = (bf16[512,512]{1,0:T(8,128)(2,1)}, bf16[512,512]{1,0:T(8,128)(2,1)S(1)}, u32[]{:S(2)}, u32[]{:S(2)}) collective-permute-start(bf16[512,512]{1,0:T(8,128)(2,1)} %shard_map.74), channel_id=1, source_target_pairs={{0,3},{1,2},{2,1},{3,0},{4,7},{5,6},{6,5},{7,4},{8,11},{9,10},{10,... | collective-permute-start | bytes 1572872 | tf_op jit(solution)/shard_map/ppermute | solution.py:39
  278.3 5.5 %copy-start.1 = (bf16[64,6656]{1,0:T(8,128)(2,1)S(1)}, bf16[64,6656]{1,0:T(8,128)(2,1)}, u32[]{:S(2)}) copy-start(bf16[64,6656]{1,0:T(8,128)(2,1)} %refs_2_.9) | copy-start | bytes 2555908
  291.1 4.6 %collective-permute-start.18 = (f32[1,768]{1,0:T(1,128)S(1)}, f32[1,768]{1,0:T(1,128)S(1)}, u32[]{:S(2)}, u32[]{:S(2)}) collective-permute-start(f32[1,768]{1,0:T(1,128)S(1)} %shard_map.80), channel_id=1, source_target_pairs={{0,12},{4,8},{8,4},{12,0},{16,28},{20,24},{24,20},{28,16},{1,13},{... | collective-permute-start | bytes 9224 | tf_op jit(solution)/shard_map/ppermute | solution.py:39
  291.3 4.9 %collective-permute-start.17 = (f32[1,768]{1,0:T(1,128)S(1)}, f32[1,768]{1,0:T(1,128)S(1)}, u32[]{:S(2)}, u32[]{:S(2)}) collective-permute-start(f32[1,768]{1,0:T(1,128)S(1)} %shard_map.80), channel_id=1, source_target_pairs={{0,8},{4,12},{8,0},{12,4},{16,24},{20,28},{24,16},{28,20},{1,9},{5... | collective-permute-start | bytes 9224 | tf_op jit(solution)/shard_map/ppermute | solution.py:39
  294.6 3.6 %collective-permute-start.16 = (f32[1,768]{1,0:T(1,128)S(1)}, f32[1,768]{1,0:T(1,128)S(1)}, u32[]{:S(2)}, u32[]{:S(2)}) collective-permute-start(f32[1,768]{1,0:T(1,128)S(1)} %shard_map.80), channel_id=1, source_target_pairs={{0,4},{4,0},{8,12},{12,8},{16,20},{20,16},{24,28},{28,24},{1,5},{5... | collective-permute-start | bytes 9224 | tf_op jit(solution)/shard_map/ppermute | solution.py:39
  298.2 4.6 %collective-permute-start.19 = (f32[1,768]{1,0:T(1,128)S(1)}, f32[1,768]{1,0:T(1,128)S(1)}, u32[]{:S(2)}, u32[]{:S(2)}) collective-permute-start(f32[1,768]{1,0:T(1,128)S(1)} %add_add_fusion), channel_id=1, source_target_pairs={{0,16},{4,20},{8,24},{12,28},{16,0},{20,4},{24,8},{28,12},{1,17},{... | collective-permute-start | bytes 9224 | tf_op jit(solution)/shard_map/ppermute | solution.py:39
  302.8 5.2 %copy-start.2 = (bf16[64,6656]{1,0:T(8,128)(2,1)S(1)}, bf16[64,6656]{1,0:T(8,128)(2,1)}, u32[]{:S(2)}) copy-start(bf16[64,6656]{1,0:T(8,128)(2,1)} %refs_2_.9) | copy-start | bytes 2555908

commit v9 on v5

--- a/solution.py
+++ b/solution.py
@@ -92,7 +92,7 @@
 
 
 def parts_of(rows):
-    height = rows // 8 if rows % BLOCK == 0 else rows
+    height = rows // 2 if rows % BLOCK == 0 else rows
     return [(r, height) for r in range(0, rows, height)]
 
 

time: 302 us -> 302 us (level)
  transfers between devices with their start and end apart: 23 -> 23, of which waited for: 13 -> 13; matrix products, arithmetic and copies ran while one was open for 1% -> 1% of each run, Pallas kernels for 30% -> 29%
where the time goes in v9:
time: 302 us; the launch traced here: 301 us
  blocking collectives  108 us (36%)
  Pallas kernels  91.3 us (30%)
  waiting for transfers between devices  63.4 us (21%)
  starting transfers between devices  32.5 us (11%)
  local copies, waits for them, and re-layouts  3.11 us (1%)
    psum x5, blocking collectives, body(): lax.psum(local, 'fsdp')  108 us
    ppermute x22, waiting for transfers between devices, swap(): return lax.ppermute(array, axis, [(i, i ^ d) for i in range(size)])  63.4 us
    pallas_call x9, Pallas kernels, export_chunk(): pl.pallas_call(functools.partial(export_kernel, tp, ds, first), out_shape...  41.3 us
    pallas_call x10, Pallas kernels, move(): pl.pallas_call(functools.partial(move_kernel, moves, len(arrays), direct)...  28.7 us
    ppermute x22, starting transfers between devices, swap(): return lax.ppermute(array, axis, [(i, i ^ d) for i in range(size)])  23.7 us
    pallas_call x7, Pallas kernels, column_squares(): pl.pallas_call(functools.partial(squares_kernel, len(ds)), out_shape=jax....  19 us
    all_to_all x1, starting transfers between devices, body(): lax.all_to_all(pack_near(after(me, *pieces), base, tp), 'tp', 0, 0, tiled...  8.87 us
  transfers between devices with their start and end apart: 23, of which 13 were waited for; matrix products, arithmetic and copies ran while one was open for 1% of the time, Pallas kernels for 29%

profile of v9, /device:TPU:0, one launch (start us, length us, event | category | flops | bytes accessed | tf_op | source)
XLA Modules:
  0.0 301.3 jit_solution(4445013889207038374)
XLA Ops:
  2.0 3.0 collective-permute-start
  11.5 9.4 %shard_map.63 = bf16[1024,6656]{1,0:T(8,128)(2,1)} custom-call(s32[1]{0:T(128)} %bitcast.me_ref, bf16[512,26624]{1,0:T(8,128)(2,1)} %refs_0_.47), custom_call_target="tpu_custom_call" | custom-call | bytes 9087658 | tf_op jit(solution)/shard_map/pallas_call | solution.py:78
  20.9 8.9 %all-to-all-start = ((bf16[2,512,6656]{2,1,0:T(8,128)(2,1)}), bf16[2,512,6656]{2,1,0:T(8,128)(2,1)}, u32[]{:S(2)}, u32[]{:S(2)}) async-start(bf16[2,512,6656]{2,1,0:T(8,128)(2,1)} %bitcast.32), calls=%async_computation | async-start | bytes 27262976 | tf_op jit(solution)/shard_map/all_to_all | solution.py:408
  29.8 23.4 %collective-permute-done.1.refs_3_ = bf16[512,1024]{1,0:T(8,128)(2,1)} collective-permute-done((bf16[512,1024]{1,0:T(8,128)(2,1)}, bf16[512,1024]{1,0:T(8,128)(2,1)}, u32[]{:S(2)}, u32[]{:S(2)}) %collective-permute-start.1) | collective-permute-done | bytes 1048608 | tf_op jit(solution)/shard_map/ppermute | solution.py:39
  55.5 2.5 shard_map.61
  62.2 3.1 %shard_map.64 = f32[1,1024]{1,0:T(1,128)S(1)} custom-call(s32[1]{0:T(128)} %bitcast.me_ref, bf16[512,26624]{1,0:T(8,128)(2,1)} %refs_0_.47, bf16[1024,6656]{1,0:T(8,128)(2,1)} %bitcast.4.refs_1_, bf16[560,1024]{1,0:T(8,128)(2,1)} %collective-permute-done.refs_2_, bf16[512,1024]{1,0:T(8,128)(2,1)} %collective-permute-done.1.refs_3_, ...), custom_call_target="tpu_custom_call" | custom-call | flops 89478488 | bytes 1398101 | tf_op jit(solution)/shard_map/pallas_call | solution.py:250
  65.3 20.7 %psum.35.refs_9_ = f32[1,1024]{1,0:T(1,128)S(1)} all-reduce(f32[1,1024]{1,0:T(1,128)S(1)} %shard_map.64), channel_id=1, replica_groups=mesh['fsdp'=8,'tp'=4] {'fsdp'}, use_global_device_ids=true, to_apply=%region_0.1 | all-reduce | flops 1024 | bytes 8192 | tf_op jit(solution)/shard_map/psum | solution.py:474
  86.0 5.8 %shard_map.65 = (bf16[2048,6656]{1,0:T(8,128)(2,1)}, f32[16,52]{1,0:T(8,128)S(1)}) custom-call(s32[1]{0:T(128)} %bitcast.me_ref, bf16[512,26624]{1,0:T(8,128)(2,1)} %refs_0_.47, bf16[1024,6656]{1,0:T(8,128)(2,1)} %bitcast.4.refs_1_, bf16[560,1024]{1,0:T(8,128)(2,1)} %collective-permute-done.refs_2_, bf16[512,1024]{1,0:T(8,128)(2,1)} %collective-permute-done.1.refs_3_, ...), custom_call_target="tpu_custom_call" | custom-call | flops 89478488 | bytes 2796202 | tf_op jit(solution)/shard_map/pallas_call | solution.py:356
  91.8 6.3 %collective-permute-done.5.refs_3_ = bf16[512,1024]{1,0:T(8,128)(2,1)} collective-permute-done((bf16[512,1024]{1,0:T(8,128)(2,1)}, bf16[512,1024]{1,0:T(8,128)(2,1)}, u32[]{:S(2)}, u32[]{:S(2)}) %collective-permute-start.5) | collective-permute-done | bytes 1048608 | tf_op jit(solution)/shard_map/ppermute | solution.py:39
  98.2 2.4 shard_map.71
  103.5 3.1 %shard_map.66 = f32[1,1024]{1,0:T(1,128)S(1)} custom-call(s32[1]{0:T(128)} %bitcast.me_ref, bf16[512,26624]{1,0:T(8,128)(2,1)} %refs_0_.47, bf16[1024,6656]{1,0:T(8,128)(2,1)} %bitcast.4.refs_1_, bf16[512,1024]{1,0:T(8,128)(2,1)} %copy-done.5, bf16[512,1024]{1,0:T(8,128)(2,1)} %collective-permute-done.5.refs_3_, bf16[64,512]{1,0:T(8,128)(2,1)S(1)} %bitcast.11, ...), custom_call_target="tpu_custom_call" | custom-call | flops 89478488 | bytes 1398101 | tf_op jit(solution)/shard_map/pallas_call | solution.py:250
  106.6 21.7 %psum.36.refs_9_ = f32[1,1024]{1,0:T(1,128)S(1)} all-reduce(f32[1,1024]{1,0:T(1,128)S(1)} %shard_map.66), channel_id=1, replica_groups=mesh['fsdp'=8,'tp'=4] {'fsdp'}, use_global_device_ids=true, to_apply=%region_1.2 | all-reduce | flops 1024 | bytes 8192 | tf_op jit(solution)/shard_map/psum | solution.py:474
  128.3 5.9 %shard_map.67 = (bf16[2048,6656]{1,0:T(8,128)(2,1)}, f32[16,52]{1,0:T(8,128)S(1)}) custom-call(s32[1]{0:T(128)} %bitcast.me_ref, bf16[512,26624]{1,0:T(8,128)(2,1)} %refs_0_.47, bf16[1024,6656]{1,0:T(8,128)(2,1)} %bitcast.4.refs_1_, bf16[512,1024]{1,0:T(8,128)(2,1)} %copy-done.5, ...), custom_call_target="tpu_custom_call", output_to_operand_aliasing={{0}: (12, {})} | custom-call | flops 89478488 | bytes 2796202 | tf_op jit(solution)/shard_map/pallas_call | solution.py:356
  135.1 8.0 %collective-permute-done.3.refs_3_ = bf16[512,1024]{1,0:T(8,128)(2,1)} collective-permute-done((bf16[512,1024]{1,0:T(8,128)(2,1)}, bf16[512,1024]{1,0:T(8,128)(2,1)}, u32[]{:S(2)}, u32[]{:S(2)}) %collective-permute-start.3) | collective-permute-done | bytes 1048608 | tf_op jit(solution)/shard_map/ppermute | solution.py:39
  147.3 2.5 shard_map.70
  151.9 3.1 %shard_map.72 = f32[1,1024]{1,0:T(1,128)S(1)} custom-call(s32[1]{0:T(128)} %bitcast.me_ref, bf16[512,26624]{1,0:T(8,128)(2,1)} %refs_0_.47, bf16[1024,6656]{1,0:T(8,128)(2,1)} %bitcast.4.refs_1_, bf16[512,1024]{1,0:T(8,128)(2,1)} %copy-done.6, bf16[512,1024]{1,0:T(8,128)(2,1)} %collective-permute-done.3.refs_3_, bf16[64,512]{1,0:T(8,128)(2,1)S(1)} %bitcast.14, ...), custom_call_target="tpu_custom_call" | custom-call | flops 89478488 | bytes 1398101 | tf_op jit(solution)/shard_map/pallas_call | solution.py:250
  155.0 21.8 %psum.37.refs_9_ = f32[1,1024]{1,0:T(1,128)S(1)} all-reduce(f32[1,1024]{1,0:T(1,128)S(1)} %shard_map.72), channel_id=1, replica_groups=mesh['fsdp'=8,'tp'=4] {'fsdp'}, use_global_device_ids=true, to_apply=%region_2.3 | all-reduce | flops 1024 | bytes 8192 | tf_op jit(solution)/shard_map/psum | solution.py:474
  176.9 5.9 %shard_map.73 = (bf16[2048,6656]{1,0:T(8,128)(2,1)}, f32[16,52]{1,0:T(8,128)S(1)}) custom-call(s32[1]{0:T(128)} %bitcast.me_ref, bf16[512,26624]{1,0:T(8,128)(2,1)} %refs_0_.47, bf16[1024,6656]{1,0:T(8,128)(2,1)} %bitcast.4.refs_1_, bf16[512,1024]{1,0:T(8,128)(2,1)} %copy-done.6, ...), custom_call_target="tpu_custom_call", output_to_operand_aliasing={{0}: (12, {})} | custom-call | flops 89478488 | bytes 2796202 | tf_op jit(solution)/shard_map/pallas_call | solution.py:356
  182.8 5.3 %collective-permute-done.13.refs_3_ = bf16[512,1024]{1,0:T(8,128)(2,1)} collective-permute-done((bf16[512,1024]{1,0:T(8,128)(2,1)}, bf16[512,1024]{1,0:T(8,128)(2,1)}, u32[]{:S(2)}, u32[]{:S(2)}) %collective-permute-start.13) | collective-permute-done | bytes 1048608 | tf_op jit(solution)/shard_map/ppermute | solution.py:39
  188.0 2.4 shard_map.79
  192.5 3.1 %shard_map.74 = f32[1,1024]{1,0:T(1,128)S(1)} custom-call(s32[1]{0:T(128)} %bitcast.me_ref, bf16[512,26624]{1,0:T(8,128)(2,1)} %refs_0_.47, bf16[1024,6656]{1,0:T(8,128)(2,1)} %bitcast.4.refs_1_, bf16[512,1024]{1,0:T(8,128)(2,1)} %collective-permute-done.12.refs_2_, bf16[512,1024]{1,0:T(8,128)(2,1)} %collective-permute-done.13.refs_3_, ...), custom_call_target="tpu_custom_call" | custom-call | flops 89478488 | bytes 1398101 | tf_op jit(solution)/shard_map/pallas_call | solution.py:250
  195.7 22.0 %psum.38.refs_9_ = f32[1,1024]{1,0:T(1,128)S(1)} all-reduce(f32[1,1024]{1,0:T(1,128)S(1)} %shard_map.74), channel_id=1, replica_groups=mesh['fsdp'=8,'tp'=4] {'fsdp'}, use_global_device_ids=true, to_apply=%region_3.4 | all-reduce | flops 1024 | bytes 8192 | tf_op jit(solution)/shard_map/psum | solution.py:474
  217.7 5.9 %shard_map.75 = (bf16[2048,6656]{1,0:T(8,128)(2,1)}, f32[16,52]{1,0:T(8,128)S(1)}) custom-call(s32[1]{0:T(128)} %bitcast.me_ref, bf16[512,26624]{1,0:T(8,128)(2,1)} %refs_0_.47, bf16[1024,6656]{1,0:T(8,128)(2,1)} %bitcast.4.refs_1_, bf16[512,1024]{1,0:T(8,128)(2,1)} %collective-permute-done.12.refs_2_, ...), custom_call_target="tpu_custom_call", output_to_operand_aliasing={{0}: (12, {})} | custom-call | flops 89478488 | bytes 2796202 | tf_op jit(solution)/shard_map/pallas_call | solution.py:356
  223.6 10.1 %collective-permute-done.11.refs_3_ = bf16[512,1024]{1,0:T(8,128)(2,1)} collective-permute-done((bf16[512,1024]{1,0:T(8,128)(2,1)}, bf16[512,1024]{1,0:T(8,128)(2,1)}, u32[]{:S(2)}, u32[]{:S(2)}) %collective-permute-start.11) | collective-permute-done | bytes 1048608 | tf_op jit(solution)/shard_map/ppermute | solution.py:39
  240.1 3.1 %shard_map.78 = f32[1,1024]{1,0:T(1,128)S(1)} custom-call(s32[1]{0:T(128)} %bitcast.me_ref, bf16[512,26624]{1,0:T(8,128)(2,1)} %refs_0_.47, bf16[1024,6656]{1,0:T(8,128)(2,1)} %bitcast.4.refs_1_, bf16[528,1024]{1,0:T(8,128)(2,1)} %collective-permute-done.10.refs_2_, bf16[512,1024]{1,0:T(8,128)(2,1)} %collective-permute-done.11.refs_3_, ...), custom_call_target="tpu_custom_call" | custom-call | flops 89478488 | bytes 1398101 | tf_op jit(solution)/shard_map/pallas_call | solution.py:250
  243.2 22.2 %psum.39 = f32[1,1536]{1,0:T(1,128)S(1)} all-reduce(f32[1,1536]{1,0:T(1,128)S(1)} %pad_maximum_fusion.4), channel_id=1, replica_groups=mesh['fsdp'=8,'tp'=4] {'fsdp'}, use_global_device_ids=true, to_apply=%region_5.6 | all-reduce | flops 1536 | bytes 12288 | tf_op jit(solution)/shard_map/psum | solution.py:474
  265.4 5.9 %shard_map.80 = (bf16[2048,6656]{1,0:T(8,128)(2,1)}, f32[16,52]{1,0:T(8,128)S(1)}) custom-call(s32[1]{0:T(128)} %bitcast.me_ref, bf16[512,26624]{1,0:T(8,128)(2,1)} %refs_0_.47, bf16[1024,6656]{1,0:T(8,128)(2,1)} %bitcast.4.refs_1_, bf16[528,1024]{1,0:T(8,128)(2,1)} %collective-permute-done.10.refs_2_, ...), custom_call_target="tpu_custom_call", output_to_operand_aliasing={{0}: (12, {})} | custom-call | flops 89478488 | bytes 2796202 | tf_op jit(solution)/shard_map/pallas_call | solution.py:356
  271.4 3.3 %shard_map.81 = (bf16[2048,6656]{1,0:T(8,128)(2,1)}, f32[16,52]{1,0:T(8,128)S(1)}) custom-call(s32[1]{0:T(128)} %bitcast.me_ref, bf16[512,26624]{1,0:T(8,128)(2,1)} %refs_0_.47, bf16[1024,6656]{1,0:T(8,128)(2,1)} %bitcast.4.refs_1_, bf16[64,512]{1,0:T(8,128)(2,1)S(1)} %bitcast.20, ...), custom_call_target="tpu_custom_call", output_to_operand_aliasing={{0}: (8, {})} | custom-call | flops 22369620 | bytes 699050 | tf_op jit(solution)/shard_map/pallas_call | solution.py:356
  274.7 2.7 shard_map.82.refs_3_
  279.4 2.6 collective-permute-start.20
  286.1 2.7 collective-permute-start.21
  290.7 5.9 %shard_map.84 = (bf16[2048,6656]{1,0:T(8,128)(2,1)}, f32[16,52]{1,0:T(8,128)S(1)}) custom-call(s32[1]{0:T(128)} %bitcast.me_ref, bf16[512,26624]{1,0:T(8,128)(2,1)} %refs_0_.47, bf16[1024,6656]{1,0:T(8,128)(2,1)} %bitcast.4.refs_1_, bf16[512,1024]{1,0:T(8,128)(2,1)} %collective-permute-done.16.refs_2_, ...), custom_call_target="tpu_custom_call", output_to_operand_aliasing={{0}: (12, {})} | custom-call | flops 89478488 | bytes 2796202 | tf_op jit(solution)/shard_map/pallas_call | solution.py:356
  (81 shorter events, 45.4 us)
Async XLA Ops:
  2.0 51.3 %collective-permute-start = (bf16[560,1024]{1,0:T(8,128)(2,1)S(1)}, bf16[560,1024]{1,0:T(8,128)(2,1)}, u32[]{:S(2)}, u32[]{:S(2)}) collective-permute-start(bf16[560,1024]{1,0:T(8,128)(2,1)S(1)} %shard_map.59), channel_id=1, source_target_pairs={{0,2},{1,3},{2,0},{3,1},{4,6},{5,7},{6,4},{7,5},{8,10},{9,11},{10,... | collective-permute-start | bytes 3440648 | tf_op jit(solution)/shard_map/ppermute | solution.py:39
  7.1 46.2 %collective-permute-start.1 = (bf16[512,1024]{1,0:T(8,128)(2,1)}, bf16[512,1024]{1,0:T(8,128)(2,1)}, u32[]{:S(2)}, u32[]{:S(2)}) collective-permute-start(bf16[512,1024]{1,0:T(8,128)(2,1)} %shard_map.60), channel_id=1, source_target_pairs={{0,3},{1,2},{2,1},{3,0},{4,7},{5,6},{6,5},{7,4},{8,11},{9,10},{10,... | collective-permute-start | bytes 3145736 | tf_op jit(solution)/shard_map/ppermute | solution.py:39
  9.6 82.2 %collective-permute-start.4 = (bf16[512,1024]{1,0:T(8,128)(2,1)}, bf16[512,1024]{1,0:T(8,128)(2,1)S(1)}, u32[]{:S(2)}, u32[]{:S(2)}) collective-permute-start(bf16[512,1024]{1,0:T(8,128)(2,1)} %get-tuple-element.48), channel_id=1, source_target_pairs={{0,2},{1,3},{2,0},{3,1},{4,6},{5,7},{6,4},{7,5},{8,10},{9,11},{10,... | collective-permute-start | bytes 3145736 | tf_op jit(solution)/shard_map/ppermute | solution.py:39
  10.8 18.9 %copy-start = (bf16[64,6656]{1,0:T(8,128)(2,1)S(1)}, bf16[64,6656]{1,0:T(8,128)(2,1)}, u32[]{:S(2)}) copy-start(bf16[64,6656]{1,0:T(8,128)(2,1)} %refs_2_.9) | copy-start | bytes 2555908
  10.8 87.4 %collective-permute-start.5 = (bf16[512,1024]{1,0:T(8,128)(2,1)}, bf16[512,1024]{1,0:T(8,128)(2,1)}, u32[]{:S(2)}, u32[]{:S(2)}) collective-permute-start(bf16[512,1024]{1,0:T(8,128)(2,1)} %get-tuple-element.49), channel_id=1, source_target_pairs={{0,3},{1,2},{2,1},{3,0},{4,7},{5,6},{6,5},{7,4},{8,11},{9,10},{10,... | collective-permute-start | bytes 3145736 | tf_op jit(solution)/shard_map/ppermute | solution.py:39
  20.8 39.9 %copy-start.1 = (bf16[512,64]{0,1:T(8,128)(2,1)S(1)}, bf16[512,64]{0,1:T(8,128)(2,1)}, u32[]{:S(2)}) copy-start(bf16[512,64]{0,1:T(8,128)(2,1)} %param.5) | copy-start | bytes 196612
  20.9 41.3 %all-to-all-start = ((bf16[2,512,6656]{2,1,0:T(8,128)(2,1)}), bf16[2,512,6656]{2,1,0:T(8,128)(2,1)}, u32[]{:S(2)}, u32[]{:S(2)}) async-start(bf16[2,512,6656]{2,1,0:T(8,128)(2,1)} %bitcast.32), calls=%async_computation | async-start | bytes 27262976 | tf_op jit(solution)/shard_map/all_to_all | solution.py:408
  54.0 6.8 %collective-permute-start.7 = (bf16[32,512]{1,0:T(8,128)(2,1)S(1)}, bf16[32,512]{1,0:T(8,128)(2,1)S(1)}, u32[]{:S(2)}, u32[]{:S(2)}) collective-permute-start(bf16[32,512]{1,0:T(8,128)(2,1)S(1)} %pad_maximum_fusion.3), channel_id=1, source_target_pairs={{0,4},{4,0},{8,12},{12,8},{16,20},{20,16},{24,28},{28,24},{1,5},{5... | collective-permute-start | bytes 98312 | tf_op jit(solution)/shard_map/ppermute | solution.py:39
  58.0 28.0 %copy-start.2 = (f32[26624]{0:T(1024)S(1)}, f32[26624]{0:T(1024)}, u32[]{:S(2)}) copy-start(f32[26624]{0:T(1024)} %param.7) | copy-start | bytes 319492
  58.0 77.1 %collective-permute-start.2 = (bf16[512,1024]{1,0:T(8,128)(2,1)}, bf16[512,1024]{1,0:T(8,128)(2,1)S(1)}, u32[]{:S(2)}, u32[]{:S(2)}) collective-permute-start(bf16[512,1024]{1,0:T(8,128)(2,1)} %get-tuple-element.45), channel_id=1, source_target_pairs={{0,2},{1,3},{2,0},{3,1},{4,6},{5,7},{6,4},{7,5},{8,10},{9,11},{10,... | collective-permute-start | bytes 3145736 | tf_op jit(solution)/shard_map/ppermute | solution.py:39
  58.6 84.5 %collective-permute-start.3 = (bf16[512,1024]{1,0:T(8,128)(2,1)}, bf16[512,1024]{1,0:T(8,128)(2,1)}, u32[]{:S(2)}, u32[]{:S(2)}) collective-permute-start(bf16[512,1024]{1,0:T(8,128)(2,1)} %get-tuple-element.46), channel_id=1, source_target_pairs={{0,3},{1,2},{2,1},{3,0},{4,7},{5,6},{6,5},{7,4},{8,11},{9,10},{10,... | collective-permute-start | bytes 3145736 | tf_op jit(solution)/shard_map/ppermute | solution.py:39
  60.7 1.4 collective-permute-start.6
  91.8 11.7 %copy-start.5 = (bf16[512,1024]{1,0:T(8,128)(2,1)}, bf16[512,1024]{1,0:T(8,128)(2,1)S(1)}, u32[]{:S(2)}) copy-start(bf16[512,1024]{1,0:T(8,128)(2,1)S(1)} %collective-permute-done.4.refs_2_) | copy-start | bytes 3145732
  100.6 82.2 %collective-permute-start.12 = (bf16[512,1024]{1,0:T(8,128)(2,1)}, bf16[512,1024]{1,0:T(8,128)(2,1)}, u32[]{:S(2)}, u32[]{:S(2)}) collective-permute-start(bf16[512,1024]{1,0:T(8,128)(2,1)} %get-tuple-element.59), channel_id=1, source_target_pairs={{0,2},{1,3},{2,0},{3,1},{4,6},{5,7},{6,4},{7,5},{8,10},{9,11},{10,... | collective-permute-start | bytes 3145736 | tf_op jit(solution)/shard_map/ppermute | solution.py:39
  100.9 87.2 %collective-permute-start.13 = (bf16[512,1024]{1,0:T(8,128)(2,1)}, bf16[512,1024]{1,0:T(8,128)(2,1)}, u32[]{:S(2)}, u32[]{:S(2)}) collective-permute-start(bf16[512,1024]{1,0:T(8,128)(2,1)} %get-tuple-element.60), channel_id=1, source_target_pairs={{0,3},{1,2},{2,1},{3,0},{4,7},{5,6},{6,5},{7,4},{8,11},{9,10},{10,... | collective-permute-start | bytes 3145736 | tf_op jit(solution)/shard_map/ppermute | solution.py:39
  103.3 30.9 %collective-permute-start.8 = (bf16[128,512]{1,0:T(8,128)(2,1)}, bf16[128,512]{1,0:T(8,128)(2,1)}, u32[]{:S(2)}, u32[]{:S(2)}) collective-permute-start(bf16[128,512]{1,0:T(8,128)(2,1)} %pad_maximum_fusion.1), channel_id=1, source_target_pairs={{0,1},{1,0},{2,3},{3,2},{4,5},{5,4},{6,7},{7,6},{8,9},{9,8},{10,11... | collective-permute-start | bytes 393224 | tf_op jit(solution)/shard_map/ppermute | solution.py:39
  135.1 10.3 %copy-start.6 = (bf16[512,1024]{1,0:T(8,128)(2,1)}, bf16[512,1024]{1,0:T(8,128)(2,1)S(1)}, u32[]{:S(2)}) copy-start(bf16[512,1024]{1,0:T(8,128)(2,1)S(1)} %collective-permute-done.2.refs_2_) | copy-start | bytes 3145732
  145.4 1.2 collective-permute-start.9
  146.7 0.6 copy-start.4
  149.8 83.8 %collective-permute-start.10 = (bf16[528,1024]{1,0:T(8,128)(2,1)}, bf16[528,1024]{1,0:T(8,128)(2,1)}, u32[]{:S(2)}, u32[]{:S(2)}) collective-permute-start(bf16[528,1024]{1,0:T(8,128)(2,1)} %get-tuple-element.56), channel_id=1, source_target_pairs={{0,2},{1,3},{2,0},{3,1},{4,6},{5,7},{6,4},{7,5},{8,10},{9,11},{10,... | collective-permute-start | bytes 3244040 | tf_op jit(solution)/shard_map/ppermute | solution.py:39
  151.9 81.8 %collective-permute-start.11 = (bf16[512,1024]{1,0:T(8,128)(2,1)}, bf16[512,1024]{1,0:T(8,128)(2,1)}, u32[]{:S(2)}, u32[]{:S(2)}) collective-permute-start(bf16[512,1024]{1,0:T(8,128)(2,1)} %get-tuple-element.57), channel_id=1, source_target_pairs={{0,3},{1,2},{2,1},{3,0},{4,7},{5,6},{6,5},{7,4},{8,11},{9,10},{10,... | collective-permute-start | bytes 3145736 | tf_op jit(solution)/shard_map/ppermute | solution.py:39
  190.5 84.2 %collective-permute-start.16 = (bf16[512,1024]{1,0:T(8,128)(2,1)}, bf16[512,1024]{1,0:T(8,128)(2,1)}, u32[]{:S(2)}, u32[]{:S(2)}) collective-permute-start(bf16[512,1024]{1,0:T(8,128)(2,1)} %get-tuple-element.72), channel_id=1, source_target_pairs={{0,2},{1,3},{2,0},{3,1},{4,6},{5,7},{6,4},{7,5},{8,10},{9,11},{10,... | collective-permute-start | bytes 3145736 | tf_op jit(solution)/shard_map/ppermute | solution.py:39
  190.7 87.9 %collective-permute-start.17 = (bf16[512,1024]{1,0:T(8,128)(2,1)}, bf16[512,1024]{1,0:T(8,128)(2,1)S(1)}, u32[]{:S(2)}, u32[]{:S(2)}) collective-permute-start(bf16[512,1024]{1,0:T(8,128)(2,1)} %get-tuple-element.73), channel_id=1, source_target_pairs={{0,3},{1,2},{2,1},{3,0},{4,7},{5,6},{6,5},{7,4},{8,11},{9,10},{10,... | collective-permute-start | bytes 3145736 | tf_op jit(solution)/shard_map/ppermute | solution.py:39
  235.5 61.1 %collective-permute-start.15 = (bf16[512,512]{1,0:T(8,128)(2,1)}, bf16[512,512]{1,0:T(8,128)(2,1)S(1)}, u32[]{:S(2)}, u32[]{:S(2)}) collective-permute-start(bf16[512,512]{1,0:T(8,128)(2,1)} %shard_map.76), channel_id=1, source_target_pairs={{0,2},{1,3},{2,0},{3,1},{4,6},{5,7},{6,4},{7,5},{8,10},{9,11},{10,... | collective-permute-start | bytes 1572872 | tf_op jit(solution)/shard_map/ppermute | solution.py:39
  237.5 62.4 %collective-permute-start.14 = (bf16[512,512]{1,0:T(8,128)(2,1)}, bf16[512,512]{1,0:T(8,128)(2,1)S(1)}, u32[]{:S(2)}, u32[]{:S(2)}) collective-permute-start(bf16[512,512]{1,0:T(8,128)(2,1)} %shard_map.77), channel_id=1, source_target_pairs={{0,3},{1,2},{2,1},{3,0},{4,7},{5,6},{6,5},{7,4},{8,11},{9,10},{10,... | collective-permute-start | bytes 1572872 | tf_op jit(solution)/shard_map/ppermute | solution.py:39
  278.6 12.1 %copy-start.3 = (bf16[512,1024]{1,0:T(8,128)(2,1)}, bf16[512,1024]{1,0:T(8,128)(2,1)S(1)}, u32[]{:S(2)}) copy-start(bf16[512,1024]{1,0:T(8,128)(2,1)S(1)} %collective-permute-done.17.refs_0_.refs_3_) | copy-start | bytes 3145732
  279.4 4.6 %collective-permute-start.20 = (f32[1,1024]{1,0:T(1,128)S(1)}, f32[1,1024]{1,0:T(1,128)S(1)}, u32[]{:S(2)}, u32[]{:S(2)}) collective-permute-start(f32[1,1024]{1,0:T(1,128)S(1)} %shard_map.83), channel_id=1, source_target_pairs={{0,12},{4,8},{8,4},{12,0},{16,28},{20,24},{24,20},{28,16},{1,13},{... | collective-permute-start | bytes 12296 | tf_op jit(solution)/shard_map/ppermute | solution.py:39
  282.0 3.6 %collective-permute-start.19 = (f32[1,1024]{1,0:T(1,128)S(1)}, f32[1,1024]{1,0:T(1,128)S(1)}, u32[]{:S(2)}, u32[]{:S(2)}) collective-permute-start(f32[1,1024]{1,0:T(1,128)S(1)} %shard_map.83), channel_id=1, source_target_pairs={{0,8},{4,12},{8,0},{12,4},{16,24},{20,28},{24,16},{28,20},{1,9},{5... | collective-permute-start | bytes 12296 | tf_op jit(solution)/shard_map/ppermute | solution.py:39
  282.5 3.6 %collective-permute-start.18 = (f32[1,1024]{1,0:T(1,128)S(1)}, f32[1,1024]{1,0:T(1,128)S(1)}, u32[]{:S(2)}, u32[]{:S(2)}) collective-permute-start(f32[1,1024]{1,0:T(1,128)S(1)} %shard_map.83), channel_id=1, source_target_pairs={{0,4},{4,0},{8,12},{12,8},{16,20},{20,16},{24,28},{28,24},{1,5},{5... | collective-permute-start | bytes 12296 | tf_op jit(solution)/shard_map/ppermute | solution.py:39
  286.1 4.6 %collective-permute-start.21 = (f32[1,1024]{1,0:T(1,128)S(1)}, f32[1,1024]{1,0:T(1,128)S(1)}, u32[]{:S(2)}, u32[]{:S(2)}) collective-permute-start(f32[1,1024]{1,0:T(1,128)S(1)} %add_add_fusion), channel_id=1, source_target_pairs={{0,16},{4,20},{8,24},{12,28},{16,0},{20,4},{24,8},{28,12},{1,17},{... | collective-permute-start | bytes 12296 | tf_op jit(solution)/shard_map/ppermute | solution.py:39
